TPU v7x, 32 devices: a whole 2x2x4 slice. The times are simulated.
32 devices in a mesh: seq: 16 (over z, y, x), mp: 2 (over core).
Axes of the slice: x: 2, y: 2, z: 4, core: 2. Of those that a mesh axis runs over, the one named last changes fastest.
Arguments:
- byte_states: bfloat16 [4096, 1024], P('seq'), may hold values from -6 to 6
- outer_gain: float32 [1024], replicated, may hold values from 0.1 to 1.9
- mamba_input: bfloat16 [1024, 1024], P(None, 'mp'), may hold values from -0.1875 to 0.1875
- mamba_step: bfloat16 [1024, 1024], P(None, 'mp'), may hold values from -0.1875 to 0.1875
- decay_rate: float32 [1024], P('mp'), as said below
- mixer_weight: bfloat16 [1024, 1024], P('mp'), may hold values from -0.1875 to 0.1875
- boundaries: int32 [16, 128], P('seq'), may hold values from 0 to 256, as said below
- span_counts: int32 [16], replicated, may hold values from 1 to 128, as said below
- up_weight: bfloat16 [1024, 4096], P('seq', 'mp'), may hold values from -0.1875 to 0.1875
- up_bias: float32 [4096], P('mp'), may hold values from -5 to 5
- inner_gain: float32 [4096], replicated, as said below
- query_weight: bfloat16 [4096, 4096], P('seq', 'mp'), as said below
- key_weight: bfloat16 [4096, 1024], P('seq', 'mp'), as said below
- value_weight: bfloat16 [4096, 1024], P('seq', 'mp'), may hold values from -0.09375 to 0.09375
- return_weight: bfloat16 [4096, 1024], P('mp'), may hold values from -0.09375 to 0.09375
Outputs:
- joined: bfloat16 [4096, 1024], P('seq', 'mp')
Inputs may be any that keep to these rules, and one draw needn't show every extreme that they name: `boundaries`: row s lists the spans of shard s: its first span_counts[s] entries rise strictly from 0 and are byte positions within the shard; each span runs to the next entry, the last to the shard's end; the other entries equal 256. `span_counts`: the counts sum to 1024; some shard has exactly 128 spans. `decay_rate`: Positive. `inner_gain`: Positive. `query_weight`: Finite. `key_weight`: Finite.
All inputs are finite; a program needn't handle non-finite values.
Results may differ from a plain program's by a relative error of at most 0.01.
Values may be sent and summed in bfloat16 or wider, within the bound.
No kernel may reach another device: no remote copies, remote signals or barrier semaphores. Data moves between devices by JAX's collectives and lax.ppermute only.
A program may use at most 128 MiB of HBM per device.

v0:
```python
import functools
import math

import jax
import jax.numpy as jnp
from jax import lax
from jax.experimental import pallas as pl
from jax.experimental.pallas import tpu as pltpu
from jax.sharding import PartitionSpec as P

HEADS = 32
KV_HEADS = 8
HEAD = 128
CH_OWN = 64


eps = 1e-05
masked = -1e30
TILE = 16


def swapped(value):
    return lax.ppermute(value, "mp", [(0, 1), (1, 0)])


def vmem():
    return pl.BlockSpec(memory_space=pltpu.VMEM)


def smem():
    return pl.BlockSpec(memory_space=pltpu.SMEM)


def in_place():
    return pl.BlockSpec(memory_space=pl.ANY)


def in_hbm():
    return pl.BlockSpec(memory_space=pltpu.HBM)


def seat():
    return lax.axis_index("seq"), lax.axis_index("mp")


def params(mebibytes=24):
    return pltpu.CompilerParams(vmem_limit_bytes=mebibytes * 2**20)


def brief():
    return pl.CostEstimate(flops=1, bytes_accessed=1, transcendentals=0)


def lanes(which, size):
    return pl.ds(pl.multiple_of(which * size, size), size)


def rows_at(which, size):
    return pl.ds(pl.multiple_of(which * size, size), size)


def start_all(pairs, sems):
    copies = []
    for index, (from_ref, to_ref) in enumerate(pairs):
        copy = pltpu.make_async_copy(from_ref, to_ref, sems.at[index])
        copy.start()
        copies.append(copy)
    return copies


def copy_all(pairs, sems):
    for copy in start_all(pairs, sems):
        copy.wait()


def one_minus_exp(u):
    series = jnp.ones_like(u)
    for order in range(9, 1, -1):
        series = 1.0 - u * (1.0 / order) * series
    return jnp.where(u < 0.5, u * series, 1.0 - jnp.exp(-u))


def softplus(v):
    tail = jnp.exp(-jnp.abs(v))
    series = jnp.ones_like(tail)
    for order in range(6, 1, -1):
        series = 1.0 - tail * ((order - 1.0) / order) * series
    return jnp.maximum(v, 0.0) + jnp.where(tail < 0.03, tail * series, jnp.log(1.0 + tail))


def start_cuts(plane, query_ref, key_ref, value_ref, pair_outs, sems):
    layers = len(pair_outs)
    me, _ = seat()
    layer = me // plane
    group = plane * HEAD
    pairs = []
    for step, out_ref in enumerate(pair_outs):
        target = layer ^ step
        pairs.append((query_ref.at[:, lanes(target, group)], out_ref.at[:, pl.ds(0, group)]))
        pairs.append((key_ref.at[:, lanes(target, HEAD)], out_ref.at[:, pl.ds(group, HEAD)]))
        pairs.append(
            (value_ref.at[:, lanes(target, HEAD)], out_ref.at[:, pl.ds(group + HEAD, HEAD)])
        )
    return start_all(pairs, sems)


def scan_kernel(plane, layers, *refs):
    bytes_hbm, gain_ref, input_hbm, step_hbm, rate_ref = refs[:5]
    others, refs = refs[5:8], refs[8:]
    local_ref, through_ref, ends_ref = refs[:3]
    pair_outs, refs = refs[3 : 3 + layers], refs[3 + layers :]
    bytes_ref, input_ref, step_ref, *held, sems, cut_sems = refs
    fetches = start_all(
        [(bytes_hbm, bytes_ref), (step_hbm, step_ref), (input_hbm, input_ref), *zip(others, held)],
        sems,
    )
    fetches[0].wait()
    values = bytes_ref[...].astype(jnp.float32)
    scale = lax.rsqrt(jnp.mean(values * values, axis=1, keepdims=True) + eps)
    normed = (values * scale * gain_ref[...]).astype(jnp.bfloat16)
    fetches[1].wait()
    steps = softplus(jnp.dot(normed, step_ref[...], preferred_element_type=jnp.float32))
    rate_steps = steps * rate_ref[...]
    fetches[2].wait()
    inputs = jnp.dot(normed, input_ref[...], preferred_element_type=jnp.float32)
    for fetch in fetches[3:]:
        fetch.wait()
    cuts = start_cuts(plane, *held, pair_outs, cut_sems)
    decays = jnp.exp(-rate_steps)
    drives = jnp.sqrt(one_minus_exp(2.0 * rate_steps)) * inputs
    rows, width = decays.shape
    tile = 8
    decays = decays.reshape(rows // tile, tile, width)
    drives = drives.reshape(rows // tile, tile, width)
    place = lax.broadcasted_iota(jnp.int32, decays.shape, 1)
    for reach in (1, 2, 4):
        before_decays = pltpu.roll(decays, reach, 1)
        before_drives = pltpu.roll(drives, reach, 1)
        inside = place >= reach
        drives = jnp.where(inside, decays * before_drives + drives, drives)
        decays = jnp.where(inside, decays * before_decays, decays)
    state = jnp.zeros((1, width), jnp.float32)
    kept = jnp.ones((1, width), jnp.float32)
    for index in range(rows // tile):
        states = decays[index] * state + drives[index]
        passing = decays[index] * kept
        local_ref[pl.ds(index * tile, tile), :] = states
        through_ref[pl.ds(index * tile, tile), :] = passing
        state = states[tile - 1 :, :]
        kept = passing[tile - 1 :, :]
    for index in range(ends_ref.shape[0]):
        ends_ref[index, 0:1, :] = kept
        ends_ref[index, 1:2, :] = state
    for cut in cuts:
        cut.wait()


def states_kernel(local_ref, through_ref, mixer_ref, ends_ref, states_ref, other_ref):
    me, lane = seat()
    carry = jnp.zeros((1, local_ref.shape[1]), jnp.float32)
    for shard in range(ends_ref.shape[0]):
        later = ends_ref[shard, 0:1, :] * carry + ends_ref[shard, 1:2, :]
        carry = jnp.where(shard < me, later, carry)
    states = (local_ref[...] + through_ref[...] * carry).astype(jnp.bfloat16)
    states_ref[...] = states
    half = other_ref.shape[1]
    other_ref[...] = jnp.dot(
        states, mixer_ref[:, lanes(1 - lane, half)], preferred_element_type=jnp.float32
    )


def pool_kernel(
    plane, states_ref, mixer_ref, other_ref, bytes_ref, pick_ref, encoded_ref, out_ref
):
    half = other_ref.shape[1]
    columns = lanes(seat()[1], half)
    mixed = jnp.dot(states_ref[...], mixer_ref[:, columns], preferred_element_type=jnp.float32)
    skip = bytes_ref[:, columns].astype(jnp.float32)
    encoded = (skip + (mixed + other_ref[...])).astype(jnp.bfloat16)
    encoded_ref[...] = encoded
    picked = jnp.dot(pick_ref[...], encoded, preferred_element_type=jnp.float32)
    picked = picked.astype(jnp.bfloat16)
    size = out_ref.shape[1]
    for target in range(out_ref.shape[0]):
        start = target % plane * size
        out_ref[target] = picked[start : start + size, :]


def cut_kernel(plane, gate_ref, *refs):
    layers = len(refs) - plane - 3
    pieces, (*outs, held, sems, cut_sems) = refs[:layers], refs[layers:]
    copy_all([(piece, held.at[step]) for step, piece in enumerate(pieces)], sems)
    cross = lax.rem(seat()[0], plane)
    pairs = []
    for mask, out_ref in enumerate(outs):
        size = 2 * out_ref.shape[2] // layers
        for number in range(layers // 2):
            columns = lanes(number * plane + (cross ^ mask), size)
            pairs.append((held.at[:, :, columns], out_ref.at[:, :, pl.ds(number * size, size)]))
    copy_all(pairs, cut_sems)


def own_kernel(pick_ref, arrived_ref, out_ref):
    shards, slots, half = arrived_ref.shape
    rows = arrived_ref[...].reshape(shards * slots, half)
    own = jnp.dot(pick_ref[...], rows, preferred_element_type=jnp.float32).astype(jnp.bfloat16)
    for index in range(out_ref.shape[0]):
        out_ref[index] = own


def inner_kernel(plane, layers, bias_ref, gain_ref, near_ref, far_ref, *refs):
    up_own, refs = refs[:plane], refs[plane:]
    up_far, refs = refs[:plane], refs[plane:]
    pieces, refs = refs[:layers], refs[layers:]
    query_ref, *pair_refs, pooled, up, weights, squares, pairs_held, sems, out_sems = refs
    me, lane = seat()
    layer, cross = me // plane, lax.rem(me, plane)
    half = near_ref.shape[1]
    up_rows, up_half = up_own[0].shape[1:]
    pairs = [
        (near_ref, pooled.at[:, lanes(lane, half)]),
        (far_ref, pooled.at[:, lanes(1 - lane, half)]),
    ]
    for step in range(layers):
        for mask in range(plane):
            where = rows_at((layer ^ step) * plane + (cross ^ mask), up_rows)
            pairs.append((up_own[mask].at[step], up.at[where, lanes(lane, up_half)]))
            pairs.append((up_far[mask].at[step], up.at[where, lanes(1 - lane, up_half)]))
    for step, piece in enumerate(pieces):
        pairs.append((piece, weights.at[rows_at(layer ^ step, piece.shape[0]), :]))
    copies = start_all(pairs, sems)
    for copy in copies[:-layers]:
        copy.wait()
    rows = pooled.shape[0]
    block = rows // plane
    ones = jnp.ones((8, up.shape[1]), jnp.bfloat16)
    for index in range(plane):
        where = pl.ds(index * block, block)
        widened = jnp.dot(pooled[where, :], up[...], preferred_element_type=jnp.float32)
        widened = (widened + bias_ref[...]).astype(jnp.bfloat16).astype(jnp.float32)
        inner = (widened * gain_ref[...]).astype(jnp.bfloat16)
        square = widened * widened
        coarse = square.astype(jnp.bfloat16)
        fine = (square - coarse.astype(jnp.float32)).astype(jnp.bfloat16)
        squares[:, where] = sum(
            lax.dot_general(
                ones, part, (((1,), (1,)), ((), ())), preferred_element_type=jnp.float32
            )
            for part in (coarse, fine)
        )
        if index == 0:
            for copy in copies[-layers:]:
                copy.wait()
        sums = jnp.dot(inner, weights[...], preferred_element_type=jnp.float32)
        sums = sums.astype(jnp.bfloat16)
        for head in range(plane):
            query_ref[head, where, :] = sums[:, head * HEAD : (head + 1) * HEAD]
        for number in range(2):
            start = (plane + number) * HEAD
            pairs_held[index, pl.ds(number * block, block), :] = sums[:, start : start + HEAD]
    total = jnp.concatenate(
        [squares[0:1, start : start + HEAD] for start in range(0, rows, HEAD)], axis=0
    )
    coarse = total.astype(jnp.bfloat16).astype(jnp.float32)
    both = jnp.concatenate([coarse, total - coarse], axis=0).astype(jnp.bfloat16)
    for index in range(plane):
        pairs_held[index, pl.ds(2 * block, both.shape[0]), :] = both
    copy_all(
        [(pairs_held.at[cross ^ mask], out_ref) for mask, out_ref in enumerate(pair_refs)], out_sems
    )


def added(refs, start, size):
    parts = [ref[pl.ds(start, size), :].astype(jnp.float32) for ref in refs]
    return sum(parts[1:], parts[0])


def row_scale(features, refs, lines):
    both = added(refs, refs[0].shape[0] - 2 * lines, 2 * lines)
    total = both[:lines, :] + both[lines:, :]
    return jnp.transpose(lax.rsqrt(total * (1.0 / features) + eps))


def pairs_kernel(features, lines, *refs):
    got_refs, pair_ref = refs[:-1], refs[-1]
    scale = row_scale(features, got_refs, lines)
    cross = lax.rem(seat()[0], len(got_refs))
    per_block = lines // len(got_refs)
    for line in range(per_block):
        mine = scale[:, line : line + 1]
        for index in range(1, len(got_refs)):
            column = index * per_block + line
            mine = jnp.where(cross == index, scale[:, column : column + 1], mine)
        for number in range(2):
            start = (number * per_block + line) * HEAD
            pair_ref[pl.ds(start, HEAD), :] = (added(got_refs, start, HEAD) * mine).astype(
                jnp.bfloat16
            )


def queries_kernel(features, got_ref, *refs):
    pair_refs, (query_ref, queries) = refs[:-2], refs[-2:]
    plane, rows, _ = got_ref.shape
    lines = rows // HEAD
    shards = rows // CH_OWN
    layers = shards // plane
    scale = row_scale(features, pair_refs, lines)
    for line in range(lines):
        parts = [got_ref.at[index] for index in range(plane)]
        scaled = added(parts, line * HEAD, HEAD) * scale[:, line : line + 1]
        for start in range(0, HEAD, CH_OWN):
            index = (line * HEAD + start) // CH_OWN
            shard = (index % layers) * plane + index // layers
            queries[pl.ds(shard, CH_OWN, stride=shards), :] = scaled[start : start + CH_OWN, :]
    query_ref[...] = queries[...].astype(jnp.bfloat16)


def attend_kernel(plane, place_ref, query_ref, *refs):
    pair_refs, (out_ref, natural, keys, values, attended) = refs[:plane], refs[plane:]
    rows = query_ref.shape[0]
    window = out_ref.shape[1]
    part = rows // plane
    shards = rows // CH_OWN
    layers = shards // plane
    cross = lax.rem(seat()[0], plane)
    for number, held in enumerate((keys, values)):
        for mask, pair_ref in enumerate(pair_refs):
            for layer in range(layers):
                piece = pair_ref[pl.ds(number * part + layer * CH_OWN, CH_OWN), :]
                where = pl.ds(layer * plane + (cross ^ mask), CH_OWN, stride=shards)
                natural[where, :] = piece.astype(jnp.float32)
        held[...] = natural[...].astype(jnp.bfloat16)
    block = min(256, rows)
    score_scale = 1.0 / math.sqrt(HEAD)
    for start in range(0, rows, block):
        stop = start + block
        scores = lax.dot_general(
            query_ref[start:stop, :],
            keys[0:stop, :],
            (((1,), (1,)), ((), ())),
            preferred_element_type=jnp.float32,
        )
        spots = lax.broadcasted_iota(jnp.int32, scores.shape, 1)
        mine = lax.broadcasted_iota(jnp.int32, scores.shape, 0) + start
        scores = jnp.where(spots <= mine, scores * score_scale, masked)
        peak = jnp.max(scores, axis=1, keepdims=True)
        lifted = jnp.exp(scores - peak)
        denominator = jnp.sum(lifted, axis=1, keepdims=True)
        weighted = jnp.dot(
            lifted.astype(jnp.bfloat16), values[0:stop, :], preferred_element_type=jnp.float32
        )
        attended[start:stop, :] = (weighted / denominator).astype(jnp.bfloat16)
    attended[rows:, :] = jnp.zeros((attended.shape[0] - rows, HEAD), jnp.bfloat16)
    for shard in range(out_ref.shape[0]):
        first = place_ref[shard]
        out_ref[shard] = attended[pl.ds(pl.multiple_of(first * TILE, TILE), window), :]


def return_kernel(weight_ref, pieces_ref, own_ref, other_ref, attended):
    half = own_ref.shape[1]
    lane = seat()[1]
    for head in range(pieces_ref.shape[0]):
        attended[:, head * HEAD : (head + 1) * HEAD] = pieces_ref[head]
    other_ref[...] = jnp.dot(
        attended[...], weight_ref[:, lanes(1 - lane, half)], preferred_element_type=jnp.float32
    )
    own_ref[...] = jnp.dot(
        attended[...], weight_ref[:, lanes(lane, half)], preferred_element_type=jnp.float32
    )


def join_kernel(own_ref, other_ref, encoded_ref, spread_ref, out_ref):
    returned = (own_ref[...] + other_ref[...]).astype(jnp.bfloat16)
    results = jnp.dot(spread_ref[...], returned, preferred_element_type=jnp.float32)
    out_ref[...] = (encoded_ref[...].astype(jnp.float32) + results).astype(jnp.bfloat16)


def one_head_each(
    byte_states,
    outer_gain,
    mamba_input,
    mamba_step,
    decay_rate,
    mixer_weight,
    boundaries,
    span_counts,
    up_weight,
    up_bias,
    inner_gain,
    query_weight,
    key_weight,
    value_weight,
    return_weight,
):
    shards = lax.axis_size("seq")
    me = lax.axis_index("seq")
    lane = lax.axis_index("mp")
    plane = HEADS // KV_HEADS
    layers = shards // plane
    rows_here, width = byte_states.shape
    half = mamba_input.shape[1]
    capacity = boundaries.shape[1]
    window = capacity + TILE
    total_rows = CH_OWN * shards
    inner_width = inner_gain.shape[0]
    inner_half = up_bias.shape[0]
    weight_rows = query_weight.shape[0]
    f32, bf16 = jnp.float32, jnp.bfloat16
    layer, cross = me // plane, me % plane
    plane_groups = [[first * plane + step for step in range(plane)] for first in range(layers)]

    def over(value, mask):
        return lax.ppermute(value, "seq", [(i, i ^ mask) for i in range(shards)])

    def after(value, done):
        return lax.optimization_barrier((value, done))[0]

    own_bias = up_bias.reshape(layers // 2, plane, weight_rows)
    own_bias = lax.dynamic_index_in_dim(own_bias, cross, 1, keepdims=False).reshape(1, -1)
    own_gain = inner_gain.reshape(layers, plane, weight_rows)
    own_gain = lax.dynamic_index_in_dim(own_gain, cross, 1, keepdims=False).reshape(1, -1)

    seq_ids = jnp.arange(shards, dtype=jnp.int32)
    offsets = jnp.cumsum(span_counts) - span_counts
    own_offset = jnp.sum(jnp.where(seq_ids == me, offsets, 0))
    own_count = jnp.sum(jnp.where(seq_ids == me, span_counts, 0))
    place = offsets // TILE
    own_marks = boundaries[0]
    positions = jnp.arange(rows_here, dtype=jnp.int32)
    spans_here = jnp.arange(capacity, dtype=jnp.int32)
    live = spans_here < own_count
    slots = capacity // shards
    slot_ids = jnp.arange(slots, dtype=jnp.int32)
    owners = seq_ids.reshape(layers, plane).T
    local_span = slot_ids * shards + ((owners - own_offset) % shards)[:, :, None]
    is_span = spans_here[None, :] == local_span.reshape(-1)[:, None]
    byte_at = jnp.sum(jnp.where(is_span, jnp.minimum(own_marks, rows_here - 1)[None, :], 0), axis=1)
    pool_pick = (positions[None, :] == byte_at[:, None]).astype(bf16)
    near_owner = jnp.arange(layers, dtype=jnp.int32) * plane + cross
    near_spans = near_owner[:, None] + jnp.arange(CH_OWN, dtype=jnp.int32)[None, :] * shards
    origin = jnp.sum((offsets <= near_spans[:, :, None]).astype(jnp.int32), axis=2) - 1
    origin_offset = jnp.sum(jnp.where(seq_ids == origin[:, :, None], offsets, 0), axis=2)
    arrived_row = (
        origin * (layers * slots)
        + jnp.arange(layers, dtype=jnp.int32)[:, None] * slots
        + (near_spans - origin_offset) // shards
    ).reshape(-1)
    near_pick = (
        jnp.arange(shards * layers * slots, dtype=jnp.int32)[None, :] == arrived_row[:, None]
    ).astype(bf16)
    passed = jnp.sum(
        ((own_marks[None, :] <= positions[:, None]) & live[None, :]).astype(jnp.int32), axis=1
    )
    result_row = passed - 1 + own_offset % TILE
    spread = (jnp.arange(window, dtype=jnp.int32)[None, :] == result_row[:, None]).astype(bf16)

    up_half = inner_half // plane
    up_layers = [up_weight] + [over(up_weight, plane * step) for step in range(1, layers)]

    local, through, ends, *pair_cuts = pl.pallas_call(
        functools.partial(scan_kernel, plane, layers),
        out_shape=(
            jax.ShapeDtypeStruct((rows_here, half), f32),
            jax.ShapeDtypeStruct((rows_here, half), f32),
            jax.ShapeDtypeStruct((shards, 2, half), f32),
        )
        + (jax.ShapeDtypeStruct((weight_rows, (plane + 2) * HEAD), bf16),) * layers,
        in_specs=[in_hbm(), vmem(), in_hbm(), in_hbm(), vmem()] + [in_hbm()] * 3,
        out_specs=(vmem(),) * 3 + (in_place(),) * layers,
        scratch_shapes=[
            pltpu.VMEM(array.shape, bf16)
            for array in (
                byte_states,
                mamba_input,
                mamba_step,
                query_weight,
                key_weight,
                value_weight,
            )
        ]
        + [pltpu.SemaphoreType.DMA((6,)), pltpu.SemaphoreType.DMA((3 * layers,))],
        cost_estimate=brief(),
        compiler_params=params(56),
    )(
        byte_states,
        outer_gain[None, :],
        mamba_input,
        mamba_step,
        decay_rate[None, :],
        query_weight,
        key_weight,
        value_weight,
    )
    ends = lax.all_to_all(ends, "seq", 0, 0, tiled=True)
    ends, up_layers = lax.optimization_barrier((ends, up_layers))
    pieces = [pair_cuts[0]] + [over(pair_cuts[step], plane * step) for step in range(1, layers)]
    states, other_part = pl.pallas_call(
        states_kernel,
        out_shape=(
            jax.ShapeDtypeStruct((rows_here, half), bf16),
            jax.ShapeDtypeStruct((rows_here, half), f32),
        ),
        in_specs=[vmem()] * 4,
        out_specs=(vmem(),) * 2,
        cost_estimate=brief(),
        compiler_params=params(56),
    )(local, through, mixer_weight, ends)
    far_bias = swapped(own_bias)
    bias = jnp.where(
        lane == 0,
        jnp.concatenate([own_bias, far_bias], axis=1),
        jnp.concatenate([far_bias, own_bias], axis=1),
    )
    far_part, bias, pieces[1] = lax.optimization_barrier((swapped(other_part), bias, pieces[1]))
    encoded, leaving = pl.pallas_call(
        functools.partial(pool_kernel, plane),
        out_shape=(
            jax.ShapeDtypeStruct((rows_here, half), bf16),
            jax.ShapeDtypeStruct((shards, layers * slots, half), bf16),
        ),
        in_specs=[vmem()] * 5,
        out_specs=(vmem(),) * 2,
        cost_estimate=brief(),
        compiler_params=params(56),
    )(states, mixer_weight, far_part, byte_states, pool_pick)
    arrived = lax.all_to_all(leaving, "seq", 0, 0, tiled=True)
    up_cuts = pl.pallas_call(
        functools.partial(cut_kernel, plane),
        out_shape=(jax.ShapeDtypeStruct((layers, up_weight.shape[0], up_half), bf16),) * plane,
        in_specs=[in_place()] * (1 + layers),
        out_specs=(in_place(),) * plane,
        scratch_shapes=[
            pltpu.VMEM((layers, *up_weight.shape), bf16),
            pltpu.SemaphoreType.DMA((layers,)),
            pltpu.SemaphoreType.DMA((plane * layers // 2,)),
        ],
        cost_estimate=brief(),
        compiler_params=params(56),
    )(leaving, *up_layers)
    up_own = [up_cuts[0]] + [over(up_cuts[mask], mask) for mask in range(1, plane)]
    arrived, pieces, up_own = lax.optimization_barrier((arrived, pieces, up_own))
    near_rows = pl.pallas_call(
        own_kernel,
        out_shape=jax.ShapeDtypeStruct((plane, layers * CH_OWN, half), bf16),
        in_specs=[vmem()] * 2,
        out_specs=vmem(),
        cost_estimate=brief(),
        compiler_params=params(56),
    )(near_pick, arrived)
    near_rows, up_far = lax.optimization_barrier(
        (near_rows, [swapped(piece) for piece in up_own])
    )
    near = lax.all_to_all(
        near_rows, "seq", 0, 0, axis_index_groups=plane_groups, tiled=True
    ).reshape(total_rows, half)

    features = own_gain.shape[1]
    block = total_rows // plane
    lines = total_rows // HEAD
    pair_rows = 2 * block + 2 * lines
    query_sums, *pair_sums = pl.pallas_call(
        functools.partial(inner_kernel, plane, layers),
        out_shape=(jax.ShapeDtypeStruct((plane, total_rows, HEAD), bf16),)
        + (jax.ShapeDtypeStruct((pair_rows, HEAD), bf16),) * plane,
        in_specs=[vmem()] * 2 + [in_place()] * (2 + 2 * plane + layers),
        out_specs=(vmem(),) + (in_place(),) * plane,
        scratch_shapes=[
            pltpu.VMEM((total_rows, width), bf16),
            pltpu.VMEM((width, features), bf16),
            pltpu.VMEM((features, (plane + 2) * HEAD), bf16),
            pltpu.VMEM((8, total_rows), f32),
            pltpu.VMEM((plane, pair_rows, HEAD), bf16),
            pltpu.SemaphoreType.DMA((2 + 2 * shards + layers,)),
            pltpu.SemaphoreType.DMA((plane,)),
        ],
        cost_estimate=brief(),
        compiler_params=params(56),
    )(bias, own_gain, near, swapped(near), *up_own, *up_far, *pieces)
    got_pairs = [pair_sums[0]] + [over(pair_sums[mask], mask) for mask in range(1, plane)]
    got_queries = lax.all_to_all(
        query_sums, "seq", 0, 0, axis_index_groups=plane_groups, tiled=True
    )
    pairs = pl.pallas_call(
        functools.partial(pairs_kernel, inner_width, lines),
        out_shape=jax.ShapeDtypeStruct((2 * block, HEAD), bf16),
        in_specs=[vmem()] * plane,
        out_specs=vmem(),
        cost_estimate=brief(),
        compiler_params=params(8),
    )(*got_pairs)
    whole_pairs = [pairs] + [over(pairs, mask) for mask in range(1, plane)]
    queries = pl.pallas_call(
        functools.partial(queries_kernel, inner_width),
        out_shape=jax.ShapeDtypeStruct((total_rows, HEAD), bf16),
        in_specs=[vmem()] * (1 + plane),
        out_specs=vmem(),
        scratch_shapes=[pltpu.VMEM((total_rows, HEAD), f32)],
        cost_estimate=brief(),
        compiler_params=params(10),
    )(got_queries, *got_pairs)
    leaving = pl.pallas_call(
        functools.partial(attend_kernel, plane),
        out_shape=jax.ShapeDtypeStruct((shards, window, HEAD), bf16),
        in_specs=[smem()] + [vmem()] * (1 + plane),
        out_specs=vmem(),
        scratch_shapes=[
            pltpu.VMEM((total_rows, HEAD), f32),
            pltpu.VMEM((total_rows, HEAD), bf16),
            pltpu.VMEM((total_rows, HEAD), bf16),
            pltpu.VMEM((total_rows + window, HEAD), bf16),
        ],
        cost_estimate=brief(),
        compiler_params=params(12),
    )(place, queries, *whole_pairs)
    pieces = lax.all_to_all(leaving, "seq", 0, 0, tiled=True)
    own_back, other_back = pl.pallas_call(
        return_kernel,
        out_shape=(jax.ShapeDtypeStruct((window, half), f32),) * 2,
        in_specs=[vmem()] * 2,
        out_specs=(vmem(),) * 2,
        scratch_shapes=[pltpu.VMEM((window, shards * HEAD), bf16)],
        cost_estimate=brief(),
        compiler_params=params(12),
    )(return_weight, pieces)
    return pl.pallas_call(
        join_kernel,
        out_shape=jax.ShapeDtypeStruct((rows_here, half), bf16),
        in_specs=[vmem()] * 4,
        out_specs=vmem(),
        cost_estimate=brief(),
        compiler_params=params(8),
    )(own_back, swapped(other_back), encoded, spread)


def prefix(value, axis, join, neutral):
    count, mine = (lax.axis_size(axis), lax.axis_index(axis))
    pieces = jax.tree.map(lambda part: lax.all_gather(part, axis), value)
    so_far = jax.tree.map(
        lambda part, zero: jnp.full_like(part, 0) + jnp.asarray(zero, part.dtype), value, neutral
    )

    def lap(position, so_far):
        longer = join(so_far, jax.tree.map(lambda part: part[position], pieces))
        return jax.tree.map(lambda new, old: jnp.where(position < mine, new, old), longer, so_far)

    return lax.fori_loop(0, count - 1, lap, so_far)


def rms_scale(values, gain):
    values = values.astype(jnp.float32)
    return values * lax.rsqrt(jnp.mean(values * values, axis=-1, keepdims=True) + eps) * gain


def combine_pairs(earlier, later):
    return (earlier[0] * later[0], later[0] * earlier[1] + later[1])


def pick_table(table, wanted, seq_ids):
    return jnp.sum(jnp.where(seq_ids[None, :] == wanted[:, None], table[None, :], 0), axis=1)


def block_size(piece_rows, shard_rows):
    limit = max(1, 1024 // shard_rows)
    pieces = max(1, piece_rows // shard_rows)
    best_size = 1
    for candidate in range(1, limit + 1):
        if pieces % candidate == 0:
            best_size = candidate
    return min(piece_rows, best_size * shard_rows)


def spread_heads(
    byte_states,
    outer_gain,
    mamba_input,
    mamba_step,
    decay_rate,
    mixer_weight,
    boundaries,
    span_counts,
    up_weight,
    up_bias,
    inner_gain,
    query_weight,
    key_weight,
    value_weight,
    return_weight,
):
    shards = lax.axis_size("seq")
    own_shard = lax.axis_index("seq")
    own_lane = lax.axis_index("mp")
    rows_here = byte_states.shape[0]
    capacity = boundaries.shape[1]
    column_count = mamba_input.shape[1]
    kv_local = key_weight.shape[1] // HEAD
    group_size = HEADS // KV_HEADS
    slot_count = capacity // shards
    offsets = jnp.cumsum(span_counts) - span_counts
    seq_ids = jnp.arange(shards, dtype=jnp.int32)
    own_offset = jnp.sum(jnp.where(seq_ids == own_shard, offsets, 0))
    own_count = jnp.sum(jnp.where(seq_ids == own_shard, span_counts, 0))
    normed = rms_scale(byte_states, outer_gain).astype(jnp.bfloat16)
    inputs = jnp.dot(normed, mamba_input, preferred_element_type=jnp.float32)
    step_sizes = jax.nn.softplus(jnp.dot(normed, mamba_step, preferred_element_type=jnp.float32))
    rate_steps = step_sizes * decay_rate
    decays = jnp.exp(-rate_steps)
    drives = jnp.sqrt(-jnp.expm1(-2.0 * rate_steps)) * inputs
    through, local_states = lax.associative_scan(combine_pairs, (decays, drives), axis=0)
    starting = (jnp.ones((column_count,), jnp.float32), jnp.zeros((column_count,), jnp.float32))
    arriving = prefix((through[-1], local_states[-1]), "seq", combine_pairs, starting)
    states = (local_states + through * arriving[1][None, :]).astype(jnp.bfloat16)
    partial_value = jnp.dot(states, mixer_weight, preferred_element_type=jnp.float32)
    mixed_sum = lax.psum(partial_value, "mp")
    encoded = (byte_states.astype(jnp.float32) + mixed_sum).astype(jnp.bfloat16)
    skip_part = lax.dynamic_slice_in_dim(encoded, own_lane * column_count, column_count, 1)
    own_marks = boundaries[0]
    pooled = encoded[jnp.minimum(own_marks, rows_here - 1)]
    row_width = pooled.shape[1]
    outgoing = jnp.roll(pooled.reshape(slot_count, shards, row_width), own_offset % shards, axis=1)
    incoming = lax.all_to_all(outgoing, "seq", split_axis=1, concat_axis=1, tiled=True)
    position = jnp.arange(CH_OWN, dtype=jnp.int32)
    span_index = own_shard + position * shards
    source = jnp.sum((offsets[None, :] <= span_index[:, None]).astype(jnp.int32), axis=1) - 1
    source_offset = pick_table(offsets, source, seq_ids)
    slot_index = (span_index - source_offset) // shards
    gathered_rows = incoming.reshape(slot_count * shards, row_width)[slot_index * shards + source]
    columns = gathered_rows
    widened_sum = jnp.dot(
        columns,
        lax.all_gather(up_weight, "seq", axis=0, tiled=True),
        preferred_element_type=jnp.float32,
    )
    widened_share = (widened_sum + up_bias[None, :]).astype(jnp.bfloat16)
    widened = lax.all_gather(widened_share, "mp", axis=1, tiled=True)
    inner_normed = rms_scale(widened, inner_gain).astype(jnp.bfloat16)
    columns = inner_normed
    query_part = jnp.dot(
        columns,
        lax.all_gather(query_weight, "seq", axis=0, tiled=True),
        preferred_element_type=jnp.float32,
    )
    key_part = jnp.dot(
        columns,
        lax.all_gather(key_weight, "seq", axis=0, tiled=True),
        preferred_element_type=jnp.float32,
    )
    value_part = jnp.dot(
        columns,
        lax.all_gather(value_weight, "seq", axis=0, tiled=True),
        preferred_element_type=jnp.float32,
    )
    queries = query_part.astype(jnp.bfloat16)
    key_rows = key_part.astype(jnp.bfloat16)
    value_rows = value_part.astype(jnp.bfloat16)
    query_count = queries.shape[0]
    grouped = (
        queries.reshape(query_count, kv_local, group_size, HEAD)
        .transpose(1, 0, 2, 3)
        .reshape(kv_local, query_count * group_size, HEAD)
    )
    row_index = jnp.repeat(span_index, group_size)
    shard_rows = key_rows.shape[0]
    score_scale = 1.0 / math.sqrt(HEAD)

    def key_index(whole_index):
        return whole_index // shard_rows + whole_index % shard_rows * shards

    def attend_block(running, key_block, value_block, index_block):
        row_peak, denominator, weighted = running
        scores = (
            jnp.einsum("hqd,khd->hqk", grouped, key_block, preferred_element_type=jnp.float32)
            * score_scale
        )
        scores = jnp.where(index_block[None, None, :] <= row_index[None, :, None], scores, masked)
        new_peak = jnp.maximum(row_peak, jnp.max(scores, axis=2))
        shrink = jnp.exp(row_peak - new_peak)
        lifted = jnp.exp(scores - new_peak[:, :, None])
        denominator = denominator * shrink + jnp.sum(lifted, axis=2)
        weighted = weighted * shrink[:, :, None] + jnp.einsum(
            "hqk,khd->hqd",
            lifted.astype(jnp.bfloat16),
            value_block,
            preferred_element_type=jnp.float32,
        )
        return (new_peak, denominator, weighted)

    query_total = query_count * group_size
    initial = (
        jnp.full((kv_local, query_total), masked, jnp.float32),
        jnp.zeros((kv_local, query_total), jnp.float32),
        jnp.zeros((kv_local, query_total, HEAD), jnp.float32),
    )
    key_piece = lax.all_gather(key_rows, "seq", axis=0, tiled=True)
    value_piece = lax.all_gather(value_rows, "seq", axis=0, tiled=True)
    piece_rows = key_piece.shape[0]
    block_rows = block_size(piece_rows, shard_rows)
    turn_count = piece_rows // block_rows
    key_blocks = key_piece.reshape(turn_count, block_rows, kv_local, HEAD)
    value_blocks = value_piece.reshape(turn_count, block_rows, kv_local, HEAD)

    def one_turn(turn_index, inner_running):
        whole_index = turn_index * block_rows + jnp.arange(block_rows, dtype=jnp.int32)
        return attend_block(
            inner_running, key_blocks[turn_index], value_blocks[turn_index], key_index(whole_index)
        )

    row_peak, denominator, weighted = lax.fori_loop(0, turn_count, one_turn, initial)
    attended = (weighted / denominator[:, :, None]).astype(jnp.bfloat16)
    attended = (
        attended.reshape(kv_local, query_count, group_size, HEAD)
        .transpose(1, 0, 2, 3)
        .reshape(query_count, kv_local * group_size * HEAD)
    )
    projected = jnp.dot(attended, return_weight, preferred_element_type=jnp.float32)
    returned = lax.psum_scatter(
        projected.astype(jnp.bfloat16), "mp", scatter_dimension=1, tiled=True
    )
    slot_ids = jnp.arange(slot_count, dtype=jnp.int32)
    lead_slot = (own_shard - offsets) % shards
    local_span = slot_ids[:, None] * shards + lead_slot[None, :]
    back_index = (offsets[None, :] + local_span - own_shard) // shards
    alive = local_span < span_counts[None, :]
    back_rows = jnp.where(
        alive[:, :, None],
        returned[jnp.clip(back_index, 0, CH_OWN - 1)],
        jnp.zeros((), jnp.bfloat16),
    )
    arrived = lax.all_to_all(back_rows, "seq", split_axis=1, concat_axis=1, tiled=True)
    span_results = jnp.roll(arrived, -(own_offset % shards), axis=1).reshape(capacity, column_count)
    positions = jnp.arange(rows_here, dtype=jnp.int32)
    live_slots = jnp.arange(capacity, dtype=jnp.int32) < own_count
    passed = jnp.sum(
        ((own_marks[None, :] <= positions[:, None]) & live_slots[None, :]).astype(jnp.int32), axis=1
    )
    return (skip_part.astype(jnp.float32) + span_results[passed - 1].astype(jnp.float32)).astype(
        jnp.bfloat16
    )


def solution(mesh):
    in_specs = (
        P("seq", None),
        P(),
        P(None, "mp"),
        P(None, "mp"),
        P("mp"),
        P("mp", None),
        P("seq", None),
        P(),
        P("seq", "mp"),
        P("mp"),
        P(),
        P("seq", "mp"),
        P("seq", "mp"),
        P("seq", "mp"),
        P("mp", None),
    )
    out_specs = P("seq", "mp")
    def on_device(*arrays):
        heads_here = arrays[11].shape[1] // HEAD
        fits = heads_here == mesh.shape["seq"] and mesh.shape["mp"] == 2
        return (one_head_each if fits else spread_heads)(*arrays)

    return jax.shard_map(
        on_device, mesh=mesh, in_specs=in_specs, out_specs=out_specs, check_vma=False
    )
```

profile of v0, /device:TPU:0, one launch (start us, length us, event | category | flops | bytes accessed | tf_op | source)
XLA Modules:
  0.0 176.1 jit_solution(4440071322622394351)
XLA Ops:
  0.0 3.0 %collective-permute-start = (bf16[64,2048]{1,0:T(8,128)(2,1)}, bf16[64,2048]{1,0:T(8,128)(2,1)S(1)}, u32[]{:S(2)}, u32[]{:S(2)}) collective-permute-start(bf16[64,2048]{1,0:T(8,128)(2,1)} %refs_0_.2), channel_id=1, source_target_pairs={{0,8},{2,10},{4,12},{6,14},{8,0},{10,2},{12,4},{14,6},{16,24},{18,... | collective-permute-start | bytes 786440 | tf_op jit(solution)/shard_map/ppermute | solution.py:413
  3.0 2.6 %collective-permute-start.1 = (bf16[64,2048]{1,0:T(8,128)(2,1)}, bf16[64,2048]{1,0:T(8,128)(2,1)S(1)}, u32[]{:S(2)}, u32[]{:S(2)}) collective-permute-start(bf16[64,2048]{1,0:T(8,128)(2,1)} %refs_0_.2), channel_id=1, source_target_pairs={{0,16},{2,18},{4,20},{6,22},{8,24},{10,26},{12,28},{14,30},{16,0},... | collective-permute-start | bytes 786440 | tf_op jit(solution)/shard_map/ppermute | solution.py:413
  5.6 0.7 reshape.257
  6.4 5.7 %shard_map.145 = (f32[256,512]{1,0:T(8,128)}, f32[256,512]{1,0:T(8,128)}, f32[16,2,512]{2,1,0:T(2,128)}, bf16[256,768]{1,0:T(8,128)(2,1)}, bf16[256,768]{1,0:T(8...) custom-call(bf16[256,1024]{1,0:T(8,128)(2,1)} %bytes_ref.1, f32[1,1024]{1,0:T(1,128)} %bitcast.14, ...), custom_call_target="tpu_custom_call" | custom-call | flops 1 | bytes 1 | tf_op jit(solution)/shard_map/pallas_call | solution.py:460
  12.1 7.1 %all-to-all-start = ((f32[16,2,512]{2,1,0:T(2,128)}), f32[16,2,512]{2,1,0:T(2,128)S(1)}, u32[]{:S(2)}, u32[]{:S(2)}) async-start(f32[16,2,512]{2,1,0:T(2,128)} %get-tuple-element.51), calls=%async_computation | async-start | bytes 131072 | tf_op jit(solution)/shard_map/all_to_all | solution.py:494
  19.2 1.9 %collective-permute-start.5 = (bf16[256,768]{1,0:T(8,128)(2,1)}, bf16[256,768]{1,0:T(8,128)(2,1)S(1)}, u32[]{:S(2)}, u32[]{:S(2)}) collective-permute-start(bf16[256,768]{1,0:T(8,128)(2,1)} %get-tuple-element.54), channel_id=1, source_target_pairs={{0,8},{2,10},{4,12},{6,14},{8,0},{10,2},{12,4},{14,6},{16,24},{18,... | collective-permute-start | bytes 1179656 | tf_op jit(solution)/shard_map/ppermute | solution.py:413
  21.3 0.1 reduce
  21.4 0.7 fusion.6
  22.1 0.6 add_select_fusion
  22.9 0.2 select_reduce_fusion
  23.1 2.4 %collective-permute-start.6 = (bf16[256,768]{1,0:T(8,128)(2,1)}, bf16[256,768]{1,0:T(8,128)(2,1)S(1)}, u32[]{:S(2)}, u32[]{:S(2)}) collective-permute-start(bf16[256,768]{1,0:T(8,128)(2,1)} %get-tuple-element.61), channel_id=1, source_target_pairs={{0,16},{2,18},{4,20},{6,22},{8,24},{10,26},{12,28},{14,30},{16,0},... | collective-permute-start | bytes 1179656 | tf_op jit(solution)/shard_map/ppermute | solution.py:413
  25.5 2.3 %collective-permute-start.7 = (bf16[256,768]{1,0:T(8,128)(2,1)}, bf16[256,768]{1,0:T(8,128)(2,1)S(1)}, u32[]{:S(2)}, u32[]{:S(2)}) collective-permute-start(bf16[256,768]{1,0:T(8,128)(2,1)} %get-tuple-element.62), channel_id=1, source_target_pairs={{0,24},{2,26},{4,28},{6,30},{8,16},{10,18},{12,20},{14,22},{16,8},... | collective-permute-start | bytes 1179656 | tf_op jit(solution)/shard_map/ppermute | solution.py:413
  27.8 5.5 %all-to-all-done.ends_ref = f32[16,2,512]{2,1,0:T(2,128)S(1)} async-done(((f32[16,2,512]{2,1,0:T(2,128)}), f32[16,2,512]{2,1,0:T(2,128)S(1)}, u32[]{:S(2)}, u32[]{:S(2)}) %all-to-all-start) | async-done | bytes 65568 | tf_op jit(solution)/shard_map/all_to_all | solution.py:494
  33.3 0.6 copy-done.18
  33.9 2.7 %shard_map.146 = (bf16[256,512]{1,0:T(8,128)(2,1)}, f32[256,512]{1,0:T(8,128)}) custom-call(f32[256,512]{1,0:T(8,128)} %get-tuple-element.49.local_ref, f32[256,512]{1,0:T(8,128)} %get-tuple-element.50.through_ref, bf16[512,1024]{1,0:T(8,128)(2,1)} %mixer_ref.3, f32[16,2,512]{2,1,0:T(2,128)} %copy-done.18), custom_call_target="tpu_custom_call" | custom-call | flops 1 | bytes 1 | tf_op jit(solution)/shard_map/pallas_call | solution.py:497
  36.6 0.7 fusion.2.pick_ref
  37.3 0.6 broadcast_select_fusion.bias_ref
  37.9 0.8 collective-permute-done.3.other_ref
  38.7 0.8 copy-done.7
  39.5 2.8 %shard_map.147 = (bf16[256,512]{1,0:T(8,128)(2,1)}, bf16[16,32,512]{2,1,0:T(8,128)(2,1)}) custom-call(bf16[256,512]{1,0:T(8,128)(2,1)} %get-tuple-element.56.states_ref, bf16[512,1024]{1,0:T(8,128)(2,1)} %mixer_ref.3, f32[256,512]{1,0:T(8,128)} %copy-done.7, bf16[256,1024]{1,0:T(8,128)(2,1)} %bytes_ref.1, bf16[128,256]{1,0:T(8,128)(2,1)} %fusion.2.pick_ref), custom_call_target="tpu_custom_call" | custom-call | flops 1 | bytes 1 | tf_op jit(solution)/shard_map/pallas_call | solution.py:515
  42.4 5.0 %all-to-all-start.1 = ((bf16[16,32,512]{2,1,0:T(8,128)(2,1)}), bf16[16,32,512]{2,1,0:T(8,128)(2,1)S(1)}, u32[]{:S(2)}, u32[]{:S(2)}) async-start(bf16[16,32,512]{2,1,0:T(8,128)(2,1)} %get-tuple-element.58.gate_ref), calls=%async_computation.1 | async-start | bytes 1048576 | tf_op jit(solution)/shard_map/all_to_all | solution.py:526
  47.7 2.3 %shard_map.148 = (bf16[4,64,512]{2,1,0:T(8,128)(2,1)}, bf16[4,64,512]{2,1,0:T(8,128)(2,1)}, bf16[4,64,512]{2,1,0:T(8,128)(2,1)}, bf16[4,64,512]{2,1,0:T(8,128)(2,1)}) custom-call(bf16[16,32,512]{2,1,0:T(8,128)(2,1)} %get-tuple-element.58.gate_ref, bf16[64,2048]{1,0:T(8,128)(2,1)} %refs_0_.2, bf16[64,2048]{1,0:T(8,128)(2,1)} %copy-done.19, ...), custom_call_target="tpu_custom_call" | custom-call | flops 1 | bytes 1 | tf_op jit(solution)/shard_map/pallas_call | solution.py:527
  50.0 2.9 %collective-permute-start.10 = (bf16[4,64,512]{2,1,0:T(8,128)(2,1)}, bf16[4,64,512]{2,1,0:T(8,128)(2,1)S(1)}, u32[]{:S(2)}, u32[]{:S(2)}) collective-permute-start(bf16[4,64,512]{2,1,0:T(8,128)(2,1)} %get-tuple-element.70), channel_id=1, source_target_pairs={{0,6},{2,4},{4,2},{6,0},{8,14},{10,12},{12,10},{14,8},{16,22},{18,... | collective-permute-start | bytes 786440 | tf_op jit(solution)/shard_map/ppermute | solution.py:413
  52.8 0.6 collective-permute-start.8
  53.4 0.1 collective-permute-start.9
  53.8 8.7 %collective-permute-done.6.refs_10_ = bf16[256,768]{1,0:T(8,128)(2,1)S(1)} collective-permute-done((bf16[256,768]{1,0:T(8,128)(2,1)}, bf16[256,768]{1,0:T(8,128)(2,1)S(1)}, u32[]{:S(2)}, u32[]{:S(2)}) %collective-permute-start.6) | collective-permute-done | bytes 393248 | tf_op jit(solution)/shard_map/ppermute | solution.py:413
  62.6 0.7 collective-permute-done.10.refs_3_
  63.3 5.0 %collective-permute-done.8.refs_1_ = bf16[4,64,512]{2,1,0:T(8,128)(2,1)S(1)} collective-permute-done((bf16[4,64,512]{2,1,0:T(8,128)(2,1)}, bf16[4,64,512]{2,1,0:T(8,128)(2,1)S(1)}, u32[]{:S(2)}, u32[]{:S(2)}) %collective-permute-start.8) | collective-permute-done | bytes 262176 | tf_op jit(solution)/shard_map/ppermute | solution.py:413
  68.3 7.7 %all-to-all-done.1.arrived_ref = bf16[16,32,512]{2,1,0:T(8,128)(2,1)S(1)} async-done(((bf16[16,32,512]{2,1,0:T(8,128)(2,1)}), bf16[16,32,512]{2,1,0:T(8,128)(2,1)S(1)}, u32[]{:S(2)}, u32[]{:S(2)}) %all-to-all-start.1) | async-done | bytes 524320 | tf_op jit(solution)/shard_map/all_to_all | solution.py:526
  76.1 0.5 collective-permute-start.12
  76.6 0.4 collective-permute-start.14
  77.1 0.8 fusion.pick_ref
  77.9 2.4 %shard_map.149 = bf16[4,256,512]{2,1,0:T(8,128)(2,1)} custom-call(bf16[256,512]{1,0:T(8,128)(2,1)} %fusion.pick_ref, bf16[16,32,512]{2,1,0:T(8,128)(2,1)} %copy-done.5), custom_call_target="tpu_custom_call" | custom-call | flops 1 | bytes 1 | tf_op jit(solution)/shard_map/pallas_call | solution.py:542
  80.4 18.2 %all_to_all.25 = bf16[4,256,512]{2,1,0:T(8,128)(2,1)S(1)} all-to-all(bf16[4,256,512]{2,1,0:T(8,128)(2,1)} %shard_map.149), channel_id=1, replica_groups={{0,2,4,6},{8,10,12,14},{16,18,20,22},{24,26,28,30},{1,3,5,7},{9,11,13,1..., dimensions={0} | all-to-all | bytes 2097152 | tf_op jit(solution)/shard_map/all_to_all | solution.py:553
  98.7 0.8 reshape.258
  99.4 0.6 constant_dynamic-slice_fusion
  100.0 1.3 collective-permute-done.15.far_ref
  101.3 1.0 copy-done.6
  102.3 10.8 %shard_map.150 = (bf16[4,1024,128]{2,1,0:T(8,128)(2,1)}, bf16[528,128]{1,0:T(8,128)(2,1)}, bf16[528,128]{1,0:T(8,128)(2,1)}, bf16[528,128]{1,0:T(8,128)(2,1)}, bf16[528,128]{1,0:T(8,128)(2,1)}) custom-call(f32[1,1024]{1,0:T(1,128)} %broadcast_select_fusion.bias_ref, f32[1,1024]{1,0:T(1,128)} %bitcast.11, bf16[1024,512]{1,0:T(8,128)(2,1)} %bitcast.10, ...), custom_call_target="tpu_custom_call" | custom-call | flops 1 | bytes 1 | tf_op jit(solution)/shard_map/pallas_call | solution.py:561
  113.1 3.7 %all-to-all-start.3 = ((bf16[4,1024,128]{2,1,0:T(8,128)(2,1)}), bf16[4,1024,128]{2,1,0:T(8,128)(2,1)S(1)}, u32[]{:S(2)}, u32[]{:S(2)}) async-start(bf16[4,1024,128]{2,1,0:T(8,128)(2,1)} %get-tuple-element.85), calls=%async_computation.3 | async-start | bytes 2097152 | tf_op jit(solution)/shard_map/all_to_all | solution.py:580
  116.8 1.8 %collective-permute-start.16 = (bf16[528,128]{1,0:T(8,128)(2,1)}, bf16[528,128]{1,0:T(8,128)(2,1)S(1)}, u32[]{:S(2)}, u32[]{:S(2)}) collective-permute-start(bf16[528,128]{1,0:T(8,128)(2,1)} %get-tuple-element.87), channel_id=1, source_target_pairs={{0,2},{2,0},{4,6},{6,4},{8,10},{10,8},{12,14},{14,12},{16,18},{18,... | collective-permute-start | bytes 405512 | tf_op jit(solution)/shard_map/ppermute | solution.py:413
  118.6 1.5 collective-permute-start.17
  120.1 0.3 collective-permute-start.18
  120.4 14.1 %collective-permute-done.16.refs_1_ = bf16[528,128]{1,0:T(8,128)(2,1)S(1)} collective-permute-done((bf16[528,128]{1,0:T(8,128)(2,1)}, bf16[528,128]{1,0:T(8,128)(2,1)S(1)}, u32[]{:S(2)}, u32[]{:S(2)}) %collective-permute-start.16) | collective-permute-done | bytes 135200 | tf_op jit(solution)/shard_map/ppermute | solution.py:413
  134.5 3.0 %collective-permute-done.18.refs_3_ = bf16[528,128]{1,0:T(8,128)(2,1)S(1)} collective-permute-done((bf16[528,128]{1,0:T(8,128)(2,1)}, bf16[528,128]{1,0:T(8,128)(2,1)S(1)}, u32[]{:S(2)}, u32[]{:S(2)}) %collective-permute-start.18) | collective-permute-done | bytes 135200 | tf_op jit(solution)/shard_map/ppermute | solution.py:413
  137.5 0.9 copy-done.1
  138.4 0.4 shard_map.152.refs_0_
  138.8 0.6 collective-permute-start.19
  139.5 0.5 collective-permute-start.20
  140.0 2.4 %collective-permute-start.21 = (bf16[512,128]{1,0:T(8,128)(2,1)S(1)}, bf16[512,128]{1,0:T(8,128)(2,1)S(1)}, u32[]{:S(2)}, u32[]{:S(2)}) collective-permute-start(bf16[512,128]{1,0:T(8,128)(2,1)S(1)} %shard_map.152.refs_0_), channel_id=1, source_target_pairs={{0,6},{2,4},{4,2},{6,0},{8,14},{10,12},{12,10},{14,8},{16,22},{18,... | collective-permute-start | bytes 393224 | tf_op jit(solution)/shard_map/ppermute | solution.py:413
  142.4 0.9 copy-done.2
  143.3 0.4 shard_map.151.query_ref
  143.7 1.3 collective-permute-done.19.refs_1_
  145.1 1.9 %collective-permute-done.20.refs_2_ = bf16[512,128]{1,0:T(8,128)(2,1)S(1)} collective-permute-done((bf16[512,128]{1,0:T(8,128)(2,1)S(1)}, bf16[512,128]{1,0:T(8,128)(2,1)S(1)}, u32[]{:S(2)}, u32[]{:S(2)}) %collective-permute-start.20) | collective-permute-done | bytes 131104 | tf_op jit(solution)/shard_map/ppermute | solution.py:413
  147.0 3.7 %shard_map.153 = bf16[16,144,128]{2,1,0:T(8,128)(2,1)} custom-call(s32[16]{0:T(128)S(1)} %and_select_fusion.1.place_ref, bf16[1024,128]{1,0:T(8,128)(2,1)S(1)} %shard_map.151.query_ref, bf16[512,128]{1,0:T(8,128)(2,1)S(1)} %shard_map.152.refs_0_, bf16[512,128]{1,0:T(8,128)(2,1)S(1)} %collective-permute-done.19.refs_1_, ...), custom_call_target="tpu_custom_call" | custom-call | flops 1 | bytes 1 | tf_op jit(solution)/shard_map/pallas_call | solution.py:601
  150.7 5.3 %all-to-all-start.4 = ((bf16[16,144,128]{2,1,0:T(8,128)(2,1)}), bf16[16,144,128]{2,1,0:T(8,128)(2,1)S(1)}, u32[]{:S(2)}, u32[]{:S(2)}) async-start(bf16[16,144,128]{2,1,0:T(8,128)(2,1)} %shard_map.153), calls=%async_computation.4 | async-start | bytes 1179648 | tf_op jit(solution)/shard_map/all_to_all | solution.py:615
  157.7 0.7 iota_compare_fusion.6
  158.4 0.1 convert_reduce_fusion
  158.5 12.0 %all-to-all-done.4.pieces_ref = bf16[16,144,128]{2,1,0:T(8,128)(2,1)S(1)} async-done(((bf16[16,144,128]{2,1,0:T(8,128)(2,1)}), bf16[16,144,128]{2,1,0:T(8,128)(2,1)S(1)}, u32[]{:S(2)}, u32[]{:S(2)}) %all-to-all-start.4) | async-done | bytes 589856 | tf_op jit(solution)/shard_map/all_to_all | solution.py:615
  170.5 2.2 %copy-done = bf16[2048,1024]{1,0:T(8,128)(2,1)S(1)} copy-done((bf16[2048,1024]{1,0:T(8,128)(2,1)S(1)}, bf16[2048,1024]{1,0:T(8,128)(2,1)}, u32[]{:S(2)}) %copy-start) | copy-done | bytes 4194328
  172.7 0.8 shard_map.154
  173.6 0.1 fusion.1.spread_ref
  173.7 1.4 collective-permute-done.22.other_ref
  175.2 0.9 shard_map.155
  (89 shorter events, 1.3 us)
Async XLA Ops:
  0.0 21.2 %copy-start.24 = (s32[16]{0:T(128)S(1)}, s32[16]{0:T(128)}, u32[]{:S(2)}) copy-start(s32[16]{0:T(128)} %param.22) | copy-start | bytes 196
  0.0 22.8 %copy-start.25 = (s32[1,128]{1,0:T(1,128)S(1)}, s32[1,128]{1,0:T(1,128)}, u32[]{:S(2)}) copy-start(s32[1,128]{1,0:T(1,128)} %param.21) | copy-start | bytes 1540
  0.0 23.1 %collective-permute-start = (bf16[64,2048]{1,0:T(8,128)(2,1)}, bf16[64,2048]{1,0:T(8,128)(2,1)S(1)}, u32[]{:S(2)}, u32[]{:S(2)}) collective-permute-start(bf16[64,2048]{1,0:T(8,128)(2,1)} %refs_0_.2), channel_id=1, source_target_pairs={{0,8},{2,10},{4,12},{6,14},{8,0},{10,2},{12,4},{14,6},{16,24},{18,... | collective-permute-start | bytes 786440 | tf_op jit(solution)/shard_map/ppermute | solution.py:413
  3.0 22.5 %collective-permute-start.1 = (bf16[64,2048]{1,0:T(8,128)(2,1)}, bf16[64,2048]{1,0:T(8,128)(2,1)S(1)}, u32[]{:S(2)}, u32[]{:S(2)}) collective-permute-start(bf16[64,2048]{1,0:T(8,128)(2,1)} %refs_0_.2), channel_id=1, source_target_pairs={{0,16},{2,18},{4,20},{6,22},{8,24},{10,26},{12,28},{14,30},{16,0},... | collective-permute-start | bytes 786440 | tf_op jit(solution)/shard_map/ppermute | solution.py:413
  5.6 27.7 %collective-permute-start.2 = (bf16[64,2048]{1,0:T(8,128)(2,1)}, bf16[64,2048]{1,0:T(8,128)(2,1)S(1)}, u32[]{:S(2)}, u32[]{:S(2)}) collective-permute-start(bf16[64,2048]{1,0:T(8,128)(2,1)} %refs_0_.2), channel_id=1, source_target_pairs={{0,24},{2,26},{4,28},{6,30},{8,16},{10,18},{12,20},{14,22},{16,8},... | collective-permute-start | bytes 786440 | tf_op jit(solution)/shard_map/ppermute | solution.py:413
  6.3 31.0 %collective-permute-start.4 = (f32[1,512]{1,0:T(1,128)S(1)}, f32[1,512]{1,0:T(1,128)S(1)}, u32[]{:S(2)}, u32[]{:S(2)}) collective-permute-start(f32[1,512]{1,0:T(1,128)S(1)} %bitcast.12), channel_id=1, source_target_pairs={{0,1},{1,0},{2,3},{3,2},{4,5},{5,4},{6,7},{7,6},{8,9},{9,8},{10,11... | collective-permute-start | bytes 6152 | tf_op jit(solution)/shard_map/ppermute | solution.py:23
  12.1 21.1 %all-to-all-start = ((f32[16,2,512]{2,1,0:T(2,128)}), f32[16,2,512]{2,1,0:T(2,128)S(1)}, u32[]{:S(2)}, u32[]{:S(2)}) async-start(f32[16,2,512]{2,1,0:T(2,128)} %get-tuple-element.51), calls=%async_computation | async-start | bytes 131072 | tf_op jit(solution)/shard_map/all_to_all | solution.py:494
  19.2 18.7 %collective-permute-start.5 = (bf16[256,768]{1,0:T(8,128)(2,1)}, bf16[256,768]{1,0:T(8,128)(2,1)S(1)}, u32[]{:S(2)}, u32[]{:S(2)}) collective-permute-start(bf16[256,768]{1,0:T(8,128)(2,1)} %get-tuple-element.54), channel_id=1, source_target_pairs={{0,8},{2,10},{4,12},{6,14},{8,0},{10,2},{12,4},{14,6},{16,24},{18,... | collective-permute-start | bytes 1179656 | tf_op jit(solution)/shard_map/ppermute | solution.py:413
  22.1 53.9 %copy-start.22 = (s32[16]{0:T(128)}, s32[16]{0:T(128)S(1)}, u32[]{:S(2)}) copy-start(s32[16]{0:T(128)S(1)} %get-tuple-element.94) | copy-start | bytes 196
  23.1 24.6 %copy-start.19 = (bf16[64,2048]{1,0:T(8,128)(2,1)}, bf16[64,2048]{1,0:T(8,128)(2,1)S(1)}, u32[]{:S(2)}) copy-start(bf16[64,2048]{1,0:T(8,128)(2,1)S(1)} %collective-permute-done.refs_1_) | copy-start | bytes 786436
  23.1 39.5 %collective-permute-start.6 = (bf16[256,768]{1,0:T(8,128)(2,1)}, bf16[256,768]{1,0:T(8,128)(2,1)S(1)}, u32[]{:S(2)}, u32[]{:S(2)}) collective-permute-start(bf16[256,768]{1,0:T(8,128)(2,1)} %get-tuple-element.61), channel_id=1, source_target_pairs={{0,16},{2,18},{4,20},{6,22},{8,24},{10,26},{12,28},{14,30},{16,0},... | collective-permute-start | bytes 1179656 | tf_op jit(solution)/shard_map/ppermute | solution.py:413
  25.5 22.2 %copy-start.20 = (bf16[64,2048]{1,0:T(8,128)(2,1)}, bf16[64,2048]{1,0:T(8,128)(2,1)S(1)}, u32[]{:S(2)}) copy-start(bf16[64,2048]{1,0:T(8,128)(2,1)S(1)} %collective-permute-done.1.refs_2_) | copy-start | bytes 786436
  25.5 37.1 %collective-permute-start.7 = (bf16[256,768]{1,0:T(8,128)(2,1)}, bf16[256,768]{1,0:T(8,128)(2,1)S(1)}, u32[]{:S(2)}, u32[]{:S(2)}) collective-permute-start(bf16[256,768]{1,0:T(8,128)(2,1)} %get-tuple-element.62), channel_id=1, source_target_pairs={{0,24},{2,26},{4,28},{6,30},{8,16},{10,18},{12,20},{14,22},{16,8},... | collective-permute-start | bytes 1179656 | tf_op jit(solution)/shard_map/ppermute | solution.py:413
  33.3 0.6 copy-start.18
  33.3 14.4 %copy-start.21 = (bf16[64,2048]{1,0:T(8,128)(2,1)}, bf16[64,2048]{1,0:T(8,128)(2,1)S(1)}, u32[]{:S(2)}) copy-start(bf16[64,2048]{1,0:T(8,128)(2,1)S(1)} %collective-permute-done.2.refs_3_) | copy-start | bytes 786436
  36.6 2.1 %collective-permute-start.3 = (f32[256,512]{1,0:T(8,128)}, f32[256,512]{1,0:T(8,128)S(1)}, u32[]{:S(2)}, u32[]{:S(2)}) collective-permute-start(f32[256,512]{1,0:T(8,128)} %get-tuple-element.53), channel_id=1, source_target_pairs={{0,1},{1,0},{2,3},{3,2},{4,5},{5,4},{6,7},{7,6},{8,9},{9,8},{10,11... | collective-permute-start | bytes 1572872 | tf_op jit(solution)/shard_map/ppermute | solution.py:23
  37.9 63.4 %copy-start.8 = (bf16[256,768]{1,0:T(8,128)(2,1)}, bf16[256,768]{1,0:T(8,128)(2,1)S(1)}, u32[]{:S(2)}) copy-start(bf16[256,768]{1,0:T(8,128)(2,1)S(1)} %collective-permute-done.5.refs_9_) | copy-start | bytes 1179652
  38.7 0.8 copy-start.7
  42.4 33.7 %all-to-all-start.1 = ((bf16[16,32,512]{2,1,0:T(8,128)(2,1)}), bf16[16,32,512]{2,1,0:T(8,128)(2,1)S(1)}, u32[]{:S(2)}, u32[]{:S(2)}) async-start(bf16[16,32,512]{2,1,0:T(8,128)(2,1)} %get-tuple-element.58.gate_ref), calls=%async_computation.1 | async-start | bytes 1048576 | tf_op jit(solution)/shard_map/all_to_all | solution.py:526
  50.0 13.4 %collective-permute-start.10 = (bf16[4,64,512]{2,1,0:T(8,128)(2,1)}, bf16[4,64,512]{2,1,0:T(8,128)(2,1)S(1)}, u32[]{:S(2)}, u32[]{:S(2)}) collective-permute-start(bf16[4,64,512]{2,1,0:T(8,128)(2,1)} %get-tuple-element.70), channel_id=1, source_target_pairs={{0,6},{2,4},{4,2},{6,0},{8,14},{10,12},{12,10},{14,8},{16,22},{18,... | collective-permute-start | bytes 786440 | tf_op jit(solution)/shard_map/ppermute | solution.py:413
  52.8 15.5 %collective-permute-start.8 = (bf16[4,64,512]{2,1,0:T(8,128)(2,1)}, bf16[4,64,512]{2,1,0:T(8,128)(2,1)S(1)}, u32[]{:S(2)}, u32[]{:S(2)}) collective-permute-start(bf16[4,64,512]{2,1,0:T(8,128)(2,1)} %get-tuple-element.68), channel_id=1, source_target_pairs={{0,2},{2,0},{4,6},{6,4},{8,10},{10,8},{12,14},{14,12},{16,18},{18,... | collective-permute-start | bytes 786440 | tf_op jit(solution)/shard_map/ppermute | solution.py:413
  53.4 14.9 %collective-permute-start.9 = (bf16[4,64,512]{2,1,0:T(8,128)(2,1)}, bf16[4,64,512]{2,1,0:T(8,128)(2,1)S(1)}, u32[]{:S(2)}, u32[]{:S(2)}) collective-permute-start(bf16[4,64,512]{2,1,0:T(8,128)(2,1)} %get-tuple-element.69), channel_id=1, source_target_pairs={{0,4},{2,6},{4,0},{6,2},{8,12},{10,14},{12,8},{14,10},{16,20},{18,... | collective-permute-start | bytes 786440 | tf_op jit(solution)/shard_map/ppermute | solution.py:413
  62.6 38.8 %copy-start.9 = (bf16[256,768]{1,0:T(8,128)(2,1)}, bf16[256,768]{1,0:T(8,128)(2,1)S(1)}, u32[]{:S(2)}) copy-start(bf16[256,768]{1,0:T(8,128)(2,1)S(1)} %collective-permute-done.6.refs_10_) | copy-start | bytes 1179652
  62.6 38.7 %copy-start.10 = (bf16[256,768]{1,0:T(8,128)(2,1)}, bf16[256,768]{1,0:T(8,128)(2,1)S(1)}, u32[]{:S(2)}) copy-start(bf16[256,768]{1,0:T(8,128)(2,1)S(1)} %collective-permute-done.7.refs_11_) | copy-start | bytes 1179652
  63.3 38.0 %copy-start.11 = (bf16[4,64,512]{2,1,0:T(8,128)(2,1)}, bf16[4,64,512]{2,1,0:T(8,128)(2,1)S(1)}, u32[]{:S(2)}) copy-start(bf16[4,64,512]{2,1,0:T(8,128)(2,1)S(1)} %collective-permute-done.10.refs_3_) | copy-start | bytes 786436
  68.3 12.0 %copy-start.12 = (bf16[4,64,512]{2,1,0:T(8,128)(2,1)}, bf16[4,64,512]{2,1,0:T(8,128)(2,1)S(1)}, u32[]{:S(2)}) copy-start(bf16[4,64,512]{2,1,0:T(8,128)(2,1)S(1)} %collective-permute-done.8.refs_1_) | copy-start | bytes 786436
  68.3 12.1 %copy-start.13 = (bf16[4,64,512]{2,1,0:T(8,128)(2,1)}, bf16[4,64,512]{2,1,0:T(8,128)(2,1)S(1)}, u32[]{:S(2)}) copy-start(bf16[4,64,512]{2,1,0:T(8,128)(2,1)S(1)} %collective-permute-done.9.refs_2_) | copy-start | bytes 786436
  76.0 1.9 %copy-start.5 = (bf16[16,32,512]{2,1,0:T(8,128)(2,1)}, bf16[16,32,512]{2,1,0:T(8,128)(2,1)S(1)}, u32[]{:S(2)}) copy-start(bf16[16,32,512]{2,1,0:T(8,128)(2,1)S(1)} %all-to-all-done.1.arrived_ref) | copy-start | bytes 1572868
  76.0 4.3 %collective-permute-start.11 = (bf16[4,64,512]{2,1,0:T(8,128)(2,1)}, bf16[4,64,512]{2,1,0:T(8,128)(2,1)S(1)}, u32[]{:S(2)}, u32[]{:S(2)}) collective-permute-start(bf16[4,64,512]{2,1,0:T(8,128)(2,1)} %get-tuple-element.72.refs_0_), channel_id=1, source_target_pairs={{0,1},{1,0},{2,3},{3,2},{4,5},{5,4},{6,7},{7,6},{8,9},{9,8},{10,11... | collective-permute-start | bytes 786440 | tf_op jit(solution)/shard_map/ppermute | solution.py:23
  76.1 4.3 %collective-permute-start.12 = (bf16[4,64,512]{2,1,0:T(8,128)(2,1)S(1)}, bf16[4,64,512]{2,1,0:T(8,128)(2,1)S(1)}, u32[]{:S(2)}, u32[]{:S(2)}) collective-permute-start(bf16[4,64,512]{2,1,0:T(8,128)(2,1)S(1)} %collective-permute-done.8.refs_1_), channel_id=1, source_target_pairs={{0,1},{1,0},{2,3},{3,2},{4,5},{5,4},{6,7},{7,6},{8,9},{9,8},{10,11... | collective-permute-start | bytes 786440 | tf_op jit(solution)/shard_map/ppermute | solution.py:23
  76.6 3.8 %collective-permute-start.13 = (bf16[4,64,512]{2,1,0:T(8,128)(2,1)S(1)}, bf16[4,64,512]{2,1,0:T(8,128)(2,1)S(1)}, u32[]{:S(2)}, u32[]{:S(2)}) collective-permute-start(bf16[4,64,512]{2,1,0:T(8,128)(2,1)S(1)} %collective-permute-done.9.refs_2_), channel_id=1, source_target_pairs={{0,1},{1,0},{2,3},{3,2},{4,5},{5,4},{6,7},{7,6},{8,9},{9,8},{10,11... | collective-permute-start | bytes 786440 | tf_op jit(solution)/shard_map/ppermute | solution.py:23
  76.6 3.8 %collective-permute-start.14 = (bf16[4,64,512]{2,1,0:T(8,128)(2,1)S(1)}, bf16[4,64,512]{2,1,0:T(8,128)(2,1)S(1)}, u32[]{:S(2)}, u32[]{:S(2)}) collective-permute-start(bf16[4,64,512]{2,1,0:T(8,128)(2,1)S(1)} %collective-permute-done.10.refs_3_), channel_id=1, source_target_pairs={{0,1},{1,0},{2,3},{3,2},{4,5},{5,4},{6,7},{7,6},{8,9},{9,8},{10,11... | collective-permute-start | bytes 786440 | tf_op jit(solution)/shard_map/ppermute | solution.py:23
  80.3 18.2 %copy-start.14 = (bf16[4,64,512]{2,1,0:T(8,128)(2,1)}, bf16[4,64,512]{2,1,0:T(8,128)(2,1)S(1)}, u32[]{:S(2)}) copy-start(bf16[4,64,512]{2,1,0:T(8,128)(2,1)S(1)} %collective-permute-done.11.refs_4_) | copy-start | bytes 786436
  80.3 18.2 %copy-start.15 = (bf16[4,64,512]{2,1,0:T(8,128)(2,1)}, bf16[4,64,512]{2,1,0:T(8,128)(2,1)S(1)}, u32[]{:S(2)}) copy-start(bf16[4,64,512]{2,1,0:T(8,128)(2,1)S(1)} %collective-permute-done.12.refs_5_) | copy-start | bytes 786436
  80.4 18.2 %copy-start.16 = (bf16[4,64,512]{2,1,0:T(8,128)(2,1)}, bf16[4,64,512]{2,1,0:T(8,128)(2,1)S(1)}, u32[]{:S(2)}) copy-start(bf16[4,64,512]{2,1,0:T(8,128)(2,1)S(1)} %collective-permute-done.13.refs_6_) | copy-start | bytes 786436
  80.4 18.2 %copy-start.17 = (bf16[4,64,512]{2,1,0:T(8,128)(2,1)}, bf16[4,64,512]{2,1,0:T(8,128)(2,1)S(1)}, u32[]{:S(2)}) copy-start(bf16[4,64,512]{2,1,0:T(8,128)(2,1)S(1)} %collective-permute-done.14.refs_7_) | copy-start | bytes 786436
  98.6 2.8 %copy-start.4 = (bf16[4,256,512]{2,1,0:T(8,128)(2,1)}, bf16[4,256,512]{2,1,0:T(8,128)(2,1)S(1)}, u32[]{:S(2)}) copy-start(bf16[4,256,512]{2,1,0:T(8,128)(2,1)S(1)} %all_to_all.25) | copy-start | bytes 3145732
  98.6 2.7 %collective-permute-start.15 = (bf16[1024,512]{1,0:T(8,128)(2,1)S(1)}, bf16[1024,512]{1,0:T(8,128)(2,1)S(1)}, u32[]{:S(2)}, u32[]{:S(2)}) collective-permute-start(bf16[1024,512]{1,0:T(8,128)(2,1)S(1)} %bitcast.9), channel_id=1, source_target_pairs={{0,1},{1,0},{2,3},{3,2},{4,5},{5,4},{6,7},{7,6},{8,9},{9,8},{10,11... | collective-permute-start | bytes 3145736 | tf_op jit(solution)/shard_map/ppermute | solution.py:23
  101.3 1.0 copy-start.6
  102.3 40.1 %copy-start.23 = (s32[16]{0:T(128)S(1)}, s32[16]{0:T(128)}, u32[]{:S(2)}) copy-start(s32[16]{0:T(128)} %copy-done.22) | copy-start | bytes 196
  113.1 45.3 %copy-start.26 = (s32[1,128]{1,0:T(1,128)S(1)}, s32[1,128]{1,0:T(1,128)}, u32[]{:S(2)}) copy-start(s32[1,128]{1,0:T(1,128)} %param.21) | copy-start | bytes 1540
  113.1 29.3 %all-to-all-start.3 = ((bf16[4,1024,128]{2,1,0:T(8,128)(2,1)}), bf16[4,1024,128]{2,1,0:T(8,128)(2,1)S(1)}, u32[]{:S(2)}, u32[]{:S(2)}) async-start(bf16[4,1024,128]{2,1,0:T(8,128)(2,1)} %get-tuple-element.85), calls=%async_computation.3 | async-start | bytes 2097152 | tf_op jit(solution)/shard_map/all_to_all | solution.py:580
  116.8 17.7 %collective-permute-start.16 = (bf16[528,128]{1,0:T(8,128)(2,1)}, bf16[528,128]{1,0:T(8,128)(2,1)S(1)}, u32[]{:S(2)}, u32[]{:S(2)}) collective-permute-start(bf16[528,128]{1,0:T(8,128)(2,1)} %get-tuple-element.87), channel_id=1, source_target_pairs={{0,2},{2,0},{4,6},{6,4},{8,10},{10,8},{12,14},{14,12},{16,18},{18,... | collective-permute-start | bytes 405512 | tf_op jit(solution)/shard_map/ppermute | solution.py:413
  118.6 15.9 %collective-permute-start.17 = (bf16[528,128]{1,0:T(8,128)(2,1)}, bf16[528,128]{1,0:T(8,128)(2,1)S(1)}, u32[]{:S(2)}, u32[]{:S(2)}) collective-permute-start(bf16[528,128]{1,0:T(8,128)(2,1)} %get-tuple-element.88), channel_id=1, source_target_pairs={{0,4},{2,6},{4,0},{6,2},{8,12},{10,14},{12,8},{14,10},{16,20},{18,... | collective-permute-start | bytes 405512 | tf_op jit(solution)/shard_map/ppermute | solution.py:413
  120.1 17.4 %collective-permute-start.18 = (bf16[528,128]{1,0:T(8,128)(2,1)}, bf16[528,128]{1,0:T(8,128)(2,1)S(1)}, u32[]{:S(2)}, u32[]{:S(2)}) collective-permute-start(bf16[528,128]{1,0:T(8,128)(2,1)} %get-tuple-element.89), channel_id=1, source_target_pairs={{0,6},{2,4},{4,2},{6,0},{8,14},{10,12},{12,10},{14,8},{16,22},{18,... | collective-permute-start | bytes 405512 | tf_op jit(solution)/shard_map/ppermute | solution.py:413
  137.5 0.9 copy-start.1
  138.8 6.2 %collective-permute-start.19 = (bf16[512,128]{1,0:T(8,128)(2,1)S(1)}, bf16[512,128]{1,0:T(8,128)(2,1)S(1)}, u32[]{:S(2)}, u32[]{:S(2)}) collective-permute-start(bf16[512,128]{1,0:T(8,128)(2,1)S(1)} %shard_map.152.refs_0_), channel_id=1, source_target_pairs={{0,2},{2,0},{4,6},{6,4},{8,10},{10,8},{12,14},{14,12},{16,18},{18,... | collective-permute-start | bytes 393224 | tf_op jit(solution)/shard_map/ppermute | solution.py:413
  139.5 7.5 %collective-permute-start.20 = (bf16[512,128]{1,0:T(8,128)(2,1)S(1)}, bf16[512,128]{1,0:T(8,128)(2,1)S(1)}, u32[]{:S(2)}, u32[]{:S(2)}) collective-permute-start(bf16[512,128]{1,0:T(8,128)(2,1)S(1)} %shard_map.152.refs_0_), channel_id=1, source_target_pairs={{0,4},{2,6},{4,0},{6,2},{8,12},{10,14},{12,8},{14,10},{16,20},{18,... | collective-permute-start | bytes 393224 | tf_op jit(solution)/shard_map/ppermute | solution.py:413
  140.0 7.0 %collective-permute-start.21 = (bf16[512,128]{1,0:T(8,128)(2,1)S(1)}, bf16[512,128]{1,0:T(8,128)(2,1)S(1)}, u32[]{:S(2)}, u32[]{:S(2)}) collective-permute-start(bf16[512,128]{1,0:T(8,128)(2,1)S(1)} %shard_map.152.refs_0_), channel_id=1, source_target_pairs={{0,6},{2,4},{4,2},{6,0},{8,14},{10,12},{12,10},{14,8},{16,22},{18,... | collective-permute-start | bytes 393224 | tf_op jit(solution)/shard_map/ppermute | solution.py:413
  142.4 0.9 copy-start.2
  143.7 31.5 %copy-start.3 = (bf16[256,512]{1,0:T(8,128)(2,1)S(1)}, bf16[256,512]{1,0:T(8,128)(2,1)}, u32[]{:S(2)}) copy-start(bf16[256,512]{1,0:T(8,128)(2,1)} %get-tuple-element.92.encoded_ref) | copy-start | bytes 786436
  150.7 19.8 %all-to-all-start.4 = ((bf16[16,144,128]{2,1,0:T(8,128)(2,1)}), bf16[16,144,128]{2,1,0:T(8,128)(2,1)S(1)}, u32[]{:S(2)}, u32[]{:S(2)}) async-start(bf16[16,144,128]{2,1,0:T(8,128)(2,1)} %shard_map.153), calls=%async_computation.4 | async-start | bytes 1179648 | tf_op jit(solution)/shard_map/all_to_all | solution.py:615
  170.5 2.2 %copy-start = (bf16[2048,1024]{1,0:T(8,128)(2,1)S(1)}, bf16[2048,1024]{1,0:T(8,128)(2,1)}, u32[]{:S(2)}) copy-start(bf16[2048,1024]{1,0:T(8,128)(2,1)} %weight_ref.1) | copy-start | bytes 12582916
  173.5 1.6 collective-permute-start.22
where the time goes:
time: 177 us; the launch traced here: 176 us
  waiting for transfers between devices  63.6 us (36%)
  starting transfers between devices  45.3 us (26%)
  Pallas kernels  32.9 us (19%)
  blocking collectives  18.2 us (10%)
  local copies, waits for them, and re-layouts  8.92 us (5%)
  other arithmetic  5.14 us (3%)
  between operations  2.05 us (1%)
    ppermute x15, waiting for transfers between devices, over(): return lax.ppermute(value, 'seq', [(i, i ^ mask) for i in range(shards)])  34.9 us
    ppermute x15, starting transfers between devices, over(): return lax.ppermute(value, 'seq', [(i, i ^ mask) for i in range(shards)])  22.9 us
    all_to_all x1, blocking collectives, one_head_each(): lax.all_to_all(near_rows, 'seq', 0, 0, axis_index_groups=plane_groups, ti...  18.2 us
    all_to_all x1, waiting for transfers between devices, one_head_each(): pieces = lax.all_to_all(leaving, 'seq', 0, 0, tiled=True)  12 us
    pallas_call x1, Pallas kernels, one_head_each(): pl.pallas_call(functools.partial(inner_kernel, plane, layers), out_shape=...  10.8 us
    all_to_all x1, waiting for transfers between devices, one_head_each(): arrived = lax.all_to_all(leaving, 'seq', 0, 0, tiled=True)  7.73 us
    all_to_all x1, starting transfers between devices, one_head_each(): ends = lax.all_to_all(ends, 'seq', 0, 0, tiled=True)  7.1 us
    unnamed x54, local copies, waits for them, and re-layouts  6.5 us
  transfers between devices with their start and end apart: 27, of which 13 were waited for; matrix products, arithmetic and copies ran while one was open for 4% of the time, Pallas kernels for 9%

commit v1 on v0

--- a/solution.py
+++ b/solution.py
@@ -212,7 +212,8 @@
     up_own, refs = refs[:plane], refs[plane:]
     up_far, refs = refs[:plane], refs[plane:]
     pieces, refs = refs[:layers], refs[layers:]
-    query_ref, *pair_refs, pooled, up, weights, squares, pairs_held, sems, out_sems = refs
+    query_refs, pair_refs, refs = refs[:plane], refs[plane : 2 * plane], refs[2 * plane :]
+    pooled, up, weights, squares, queries_held, pairs_held, sems, out_sems = refs
     me, lane = seat()
     layer, cross = me // plane, lax.rem(me, plane)
     half = near_ref.shape[1]
@@ -254,7 +255,7 @@
         sums = jnp.dot(inner, weights[...], preferred_element_type=jnp.float32)
         sums = sums.astype(jnp.bfloat16)
         for head in range(plane):
-            query_ref[head, where, :] = sums[:, head * HEAD : (head + 1) * HEAD]
+            queries_held[head, where, :] = sums[:, head * HEAD : (head + 1) * HEAD]
         for number in range(2):
             start = (plane + number) * HEAD
             pairs_held[index, pl.ds(number * block, block), :] = sums[:, start : start + HEAD]
@@ -265,9 +266,9 @@
     both = jnp.concatenate([coarse, total - coarse], axis=0).astype(jnp.bfloat16)
     for index in range(plane):
         pairs_held[index, pl.ds(2 * block, both.shape[0]), :] = both
-    copy_all(
-        [(pairs_held.at[cross ^ mask], out_ref) for mask, out_ref in enumerate(pair_refs)], out_sems
-    )
+    outs = [(pairs_held.at[cross ^ mask], out_ref) for mask, out_ref in enumerate(pair_refs)]
+    outs += [(queries_held.at[cross ^ mask], out_ref) for mask, out_ref in enumerate(query_refs)]
+    copy_all(outs, out_sems)
 
 
 def added(refs, start, size):
@@ -298,16 +299,15 @@
             )
 
 
-def queries_kernel(features, got_ref, *refs):
-    pair_refs, (query_ref, queries) = refs[:-2], refs[-2:]
-    plane, rows, _ = got_ref.shape
+def queries_kernel(features, plane, *refs):
+    got_refs, pair_refs, (query_ref, queries) = refs[:plane], refs[plane:-2], refs[-2:]
+    rows = query_ref.shape[0]
     lines = rows // HEAD
     shards = rows // CH_OWN
     layers = shards // plane
     scale = row_scale(features, pair_refs, lines)
     for line in range(lines):
-        parts = [got_ref.at[index] for index in range(plane)]
-        scaled = added(parts, line * HEAD, HEAD) * scale[:, line : line + 1]
+        scaled = added(got_refs, line * HEAD, HEAD) * scale[:, line : line + 1]
         for start in range(0, HEAD, CH_OWN):
             index = (line * HEAD + start) // CH_OWN
             shard = (index % layers) * plane + index // layers
@@ -558,28 +558,28 @@
     block = total_rows // plane
     lines = total_rows // HEAD
     pair_rows = 2 * block + 2 * lines
-    query_sums, *pair_sums = pl.pallas_call(
+    partial_sums = pl.pallas_call(
         functools.partial(inner_kernel, plane, layers),
-        out_shape=(jax.ShapeDtypeStruct((plane, total_rows, HEAD), bf16),)
+        out_shape=(jax.ShapeDtypeStruct((total_rows, HEAD), bf16),) * plane
         + (jax.ShapeDtypeStruct((pair_rows, HEAD), bf16),) * plane,
         in_specs=[vmem()] * 2 + [in_place()] * (2 + 2 * plane + layers),
-        out_specs=(vmem(),) + (in_place(),) * plane,
+        out_specs=(in_place(),) * (2 * plane),
         scratch_shapes=[
             pltpu.VMEM((total_rows, width), bf16),
             pltpu.VMEM((width, features), bf16),
             pltpu.VMEM((features, (plane + 2) * HEAD), bf16),
             pltpu.VMEM((8, total_rows), f32),
+            pltpu.VMEM((plane, total_rows, HEAD), bf16),
             pltpu.VMEM((plane, pair_rows, HEAD), bf16),
             pltpu.SemaphoreType.DMA((2 + 2 * shards + layers,)),
-            pltpu.SemaphoreType.DMA((plane,)),
+            pltpu.SemaphoreType.DMA((2 * plane,)),
         ],
         cost_estimate=brief(),
         compiler_params=params(56),
     )(bias, own_gain, near, swapped(near), *up_own, *up_far, *pieces)
+    query_sums, pair_sums = partial_sums[:plane], partial_sums[plane:]
     got_pairs = [pair_sums[0]] + [over(pair_sums[mask], mask) for mask in range(1, plane)]
-    got_queries = lax.all_to_all(
-        query_sums, "seq", 0, 0, axis_index_groups=plane_groups, tiled=True
-    )
+    got_queries = [query_sums[0]] + [over(query_sums[mask], mask) for mask in range(1, plane)]
     pairs = pl.pallas_call(
         functools.partial(pairs_kernel, inner_width, lines),
         out_shape=jax.ShapeDtypeStruct((2 * block, HEAD), bf16),
@@ -590,14 +590,14 @@
     )(*got_pairs)
     whole_pairs = [pairs] + [over(pairs, mask) for mask in range(1, plane)]
     queries = pl.pallas_call(
-        functools.partial(queries_kernel, inner_width),
+        functools.partial(queries_kernel, inner_width, plane),
         out_shape=jax.ShapeDtypeStruct((total_rows, HEAD), bf16),
-        in_specs=[vmem()] * (1 + plane),
+        in_specs=[vmem()] * (2 * plane),
         out_specs=vmem(),
         scratch_shapes=[pltpu.VMEM((total_rows, HEAD), f32)],
         cost_estimate=brief(),
         compiler_params=params(10),
-    )(got_queries, *got_pairs)
+    )(*got_queries, *got_pairs)
     leaving = pl.pallas_call(
         functools.partial(attend_kernel, plane),
         out_shape=jax.ShapeDtypeStruct((shards, window, HEAD), bf16),

time: 177 us -> 170 us (0.960)
  waiting for transfers between devices: 63.6 us -> 58.6 us
  starting transfers between devices: 45.3 us -> 43.2 us
    ppermute x15 -> x18, waiting for transfers between devices: 34.9 us -> 28.5 us  [over(): return lax.ppermute(value, 'seq', [(i, i ^ mask) for i in range(shards)])]
    all_to_all x1 -> x0, starting transfers between devices: 3.71 us -> none  [one_head_each(): lax.all_to_all(query_sums, 'seq', 0, 0, axis_index_groups=plane_groups, t...]
    ppermute x15 -> x18, starting transfers between devices: 22.9 us -> 25.3 us  [over(): return lax.ppermute(value, 'seq', [(i, i ^ mask) for i in range(shards)])]
    unnamed x54 -> x56, local copies, waits for them, and re-layouts: 6.5 us -> 7.42 us
  transfers between devices with their start and end apart: 27 -> 29, of which waited for: 13 -> 13; matrix products, arithmetic and copies ran while one was open for 4% -> 4% of each run, Pallas kernels for 9% -> 10%
where the time goes in v1:
time: 170 us; the launch traced here: 169 us
  waiting for transfers between devices  58.6 us (34%)
  starting transfers between devices  43.2 us (25%)
  Pallas kernels  32.4 us (19%)
  blocking collectives  18.2 us (11%)
  local copies, waits for them, and re-layouts  9.85 us (6%)
  other arithmetic  5.03 us (3%)
  between operations  2.03 us (1%)
    ppermute x18, waiting for transfers between devices, over(): return lax.ppermute(value, 'seq', [(i, i ^ mask) for i in range(shards)])  28.5 us
    ppermute x18, starting transfers between devices, over(): return lax.ppermute(value, 'seq', [(i, i ^ mask) for i in range(shards)])  25.3 us
    all_to_all x1, blocking collectives, one_head_each(): lax.all_to_all(near_rows, 'seq', 0, 0, axis_index_groups=plane_groups, ti...  18.2 us
    all_to_all x1, waiting for transfers between devices, one_head_each(): pieces = lax.all_to_all(leaving, 'seq', 0, 0, tiled=True)  13.4 us
    pallas_call x1, Pallas kernels, one_head_each(): pl.pallas_call(functools.partial(inner_kernel, plane, layers), out_shape=...  10.2 us
    all_to_all x1, waiting for transfers between devices, one_head_each(): arrived = lax.all_to_all(leaving, 'seq', 0, 0, tiled=True)  7.71 us
    unnamed x56, local copies, waits for them, and re-layouts  7.42 us
    all_to_all x1, starting transfers between devices, one_head_each(): ends = lax.all_to_all(ends, 'seq', 0, 0, tiled=True)  7.1 us
  transfers between devices with their start and end apart: 29, of which 13 were waited for; matrix products, arithmetic and copies ran while one was open for 4% of the time, Pallas kernels for 10%

profile of v1, /device:TPU:0, one launch (start us, length us, event | category | flops | bytes accessed | tf_op | source)
XLA Modules:
  0.0 169.3 jit_solution(1191395432841348126)
XLA Ops:
  0.0 3.0 %collective-permute-start = (bf16[64,2048]{1,0:T(8,128)(2,1)}, bf16[64,2048]{1,0:T(8,128)(2,1)S(1)}, u32[]{:S(2)}, u32[]{:S(2)}) collective-permute-start(bf16[64,2048]{1,0:T(8,128)(2,1)} %refs_0_.2), channel_id=1, source_target_pairs={{0,8},{2,10},{4,12},{6,14},{8,0},{10,2},{12,4},{14,6},{16,24},{18,... | collective-permute-start | bytes 786440 | tf_op jit(solution)/shard_map/ppermute | solution.py:413
  3.0 2.6 %collective-permute-start.1 = (bf16[64,2048]{1,0:T(8,128)(2,1)}, bf16[64,2048]{1,0:T(8,128)(2,1)S(1)}, u32[]{:S(2)}, u32[]{:S(2)}) collective-permute-start(bf16[64,2048]{1,0:T(8,128)(2,1)} %refs_0_.2), channel_id=1, source_target_pairs={{0,16},{2,18},{4,20},{6,22},{8,24},{10,26},{12,28},{14,30},{16,0},... | collective-permute-start | bytes 786440 | tf_op jit(solution)/shard_map/ppermute | solution.py:413
  5.6 0.7 reshape.257
  6.4 5.7 %shard_map.145 = (f32[256,512]{1,0:T(8,128)}, f32[256,512]{1,0:T(8,128)}, f32[16,2,512]{2,1,0:T(2,128)}, bf16[256,768]{1,0:T(8,128)(2,1)}, bf16[256,768]{1,0:T(8...) custom-call(bf16[256,1024]{1,0:T(8,128)(2,1)} %bytes_ref.1, f32[1,1024]{1,0:T(1,128)} %bitcast.14, ...), custom_call_target="tpu_custom_call" | custom-call | flops 1 | bytes 1 | tf_op jit(solution)/shard_map/pallas_call | solution.py:460
  12.1 7.1 %all-to-all-start = ((f32[16,2,512]{2,1,0:T(2,128)}), f32[16,2,512]{2,1,0:T(2,128)S(1)}, u32[]{:S(2)}, u32[]{:S(2)}) async-start(f32[16,2,512]{2,1,0:T(2,128)} %get-tuple-element.54), calls=%async_computation | async-start | bytes 131072 | tf_op jit(solution)/shard_map/all_to_all | solution.py:494
  19.2 1.9 %collective-permute-start.5 = (bf16[256,768]{1,0:T(8,128)(2,1)}, bf16[256,768]{1,0:T(8,128)(2,1)S(1)}, u32[]{:S(2)}, u32[]{:S(2)}) collective-permute-start(bf16[256,768]{1,0:T(8,128)(2,1)} %get-tuple-element.57), channel_id=1, source_target_pairs={{0,8},{2,10},{4,12},{6,14},{8,0},{10,2},{12,4},{14,6},{16,24},{18,... | collective-permute-start | bytes 1179656 | tf_op jit(solution)/shard_map/ppermute | solution.py:413
  21.3 0.1 reduce
  21.4 0.7 fusion.6
  22.1 0.6 add_select_fusion
  22.8 0.2 select_reduce_fusion
  23.0 2.4 %collective-permute-start.6 = (bf16[256,768]{1,0:T(8,128)(2,1)}, bf16[256,768]{1,0:T(8,128)(2,1)S(1)}, u32[]{:S(2)}, u32[]{:S(2)}) collective-permute-start(bf16[256,768]{1,0:T(8,128)(2,1)} %get-tuple-element.64), channel_id=1, source_target_pairs={{0,16},{2,18},{4,20},{6,22},{8,24},{10,26},{12,28},{14,30},{16,0},... | collective-permute-start | bytes 1179656 | tf_op jit(solution)/shard_map/ppermute | solution.py:413
  25.4 2.3 %collective-permute-start.7 = (bf16[256,768]{1,0:T(8,128)(2,1)}, bf16[256,768]{1,0:T(8,128)(2,1)S(1)}, u32[]{:S(2)}, u32[]{:S(2)}) collective-permute-start(bf16[256,768]{1,0:T(8,128)(2,1)} %get-tuple-element.65), channel_id=1, source_target_pairs={{0,24},{2,26},{4,28},{6,30},{8,16},{10,18},{12,20},{14,22},{16,8},... | collective-permute-start | bytes 1179656 | tf_op jit(solution)/shard_map/ppermute | solution.py:413
  27.8 5.5 %all-to-all-done.ends_ref = f32[16,2,512]{2,1,0:T(2,128)S(1)} async-done(((f32[16,2,512]{2,1,0:T(2,128)}), f32[16,2,512]{2,1,0:T(2,128)S(1)}, u32[]{:S(2)}, u32[]{:S(2)}) %all-to-all-start) | async-done | bytes 65568 | tf_op jit(solution)/shard_map/all_to_all | solution.py:494
  33.3 0.6 copy-done.19
  33.9 2.7 %shard_map.146 = (bf16[256,512]{1,0:T(8,128)(2,1)}, f32[256,512]{1,0:T(8,128)}) custom-call(f32[256,512]{1,0:T(8,128)} %get-tuple-element.52.local_ref, f32[256,512]{1,0:T(8,128)} %get-tuple-element.53.through_ref, bf16[512,1024]{1,0:T(8,128)(2,1)} %mixer_ref.3, f32[16,2,512]{2,1,0:T(2,128)} %copy-done.19), custom_call_target="tpu_custom_call" | custom-call | flops 1 | bytes 1 | tf_op jit(solution)/shard_map/pallas_call | solution.py:497
  36.6 0.7 fusion.2.pick_ref
  37.3 0.6 broadcast_select_fusion.bias_ref
  37.9 0.8 collective-permute-done.3.other_ref
  38.7 0.8 copy-done.8
  39.5 2.9 %shard_map.147 = (bf16[256,512]{1,0:T(8,128)(2,1)}, bf16[16,32,512]{2,1,0:T(8,128)(2,1)}) custom-call(bf16[256,512]{1,0:T(8,128)(2,1)} %get-tuple-element.59.states_ref, bf16[512,1024]{1,0:T(8,128)(2,1)} %mixer_ref.3, f32[256,512]{1,0:T(8,128)} %copy-done.8, bf16[256,1024]{1,0:T(8,128)(2,1)} %bytes_ref.1, bf16[128,256]{1,0:T(8,128)(2,1)} %fusion.2.pick_ref), custom_call_target="tpu_custom_call" | custom-call | flops 1 | bytes 1 | tf_op jit(solution)/shard_map/pallas_call | solution.py:515
  42.4 5.1 %all-to-all-start.1 = ((bf16[16,32,512]{2,1,0:T(8,128)(2,1)}), bf16[16,32,512]{2,1,0:T(8,128)(2,1)S(1)}, u32[]{:S(2)}, u32[]{:S(2)}) async-start(bf16[16,32,512]{2,1,0:T(8,128)(2,1)} %get-tuple-element.61.gate_ref), calls=%async_computation.1 | async-start | bytes 1048576 | tf_op jit(solution)/shard_map/all_to_all | solution.py:526
  47.7 2.3 %shard_map.148 = (bf16[4,64,512]{2,1,0:T(8,128)(2,1)}, bf16[4,64,512]{2,1,0:T(8,128)(2,1)}, bf16[4,64,512]{2,1,0:T(8,128)(2,1)}, bf16[4,64,512]{2,1,0:T(8,128)(2,1)}) custom-call(bf16[16,32,512]{2,1,0:T(8,128)(2,1)} %get-tuple-element.61.gate_ref, bf16[64,2048]{1,0:T(8,128)(2,1)} %refs_0_.2, bf16[64,2048]{1,0:T(8,128)(2,1)} %copy-done.20, ...), custom_call_target="tpu_custom_call" | custom-call | flops 1 | bytes 1 | tf_op jit(solution)/shard_map/pallas_call | solution.py:527
  50.0 2.9 %collective-permute-start.10 = (bf16[4,64,512]{2,1,0:T(8,128)(2,1)}, bf16[4,64,512]{2,1,0:T(8,128)(2,1)S(1)}, u32[]{:S(2)}, u32[]{:S(2)}) collective-permute-start(bf16[4,64,512]{2,1,0:T(8,128)(2,1)} %get-tuple-element.73), channel_id=1, source_target_pairs={{0,6},{2,4},{4,2},{6,0},{8,14},{10,12},{12,10},{14,8},{16,22},{18,... | collective-permute-start | bytes 786440 | tf_op jit(solution)/shard_map/ppermute | solution.py:413
  52.9 0.6 collective-permute-start.8
  53.8 8.7 %collective-permute-done.6.refs_10_ = bf16[256,768]{1,0:T(8,128)(2,1)S(1)} collective-permute-done((bf16[256,768]{1,0:T(8,128)(2,1)}, bf16[256,768]{1,0:T(8,128)(2,1)S(1)}, u32[]{:S(2)}, u32[]{:S(2)}) %collective-permute-start.6) | collective-permute-done | bytes 393248 | tf_op jit(solution)/shard_map/ppermute | solution.py:413
  62.6 0.8 collective-permute-done.10.refs_3_
  63.3 5.0 %collective-permute-done.8.refs_1_ = bf16[4,64,512]{2,1,0:T(8,128)(2,1)S(1)} collective-permute-done((bf16[4,64,512]{2,1,0:T(8,128)(2,1)}, bf16[4,64,512]{2,1,0:T(8,128)(2,1)S(1)}, u32[]{:S(2)}, u32[]{:S(2)}) %collective-permute-start.8) | collective-permute-done | bytes 262176 | tf_op jit(solution)/shard_map/ppermute | solution.py:413
  68.3 7.7 %all-to-all-done.1.arrived_ref = bf16[16,32,512]{2,1,0:T(8,128)(2,1)S(1)} async-done(((bf16[16,32,512]{2,1,0:T(8,128)(2,1)}), bf16[16,32,512]{2,1,0:T(8,128)(2,1)S(1)}, u32[]{:S(2)}, u32[]{:S(2)}) %all-to-all-start.1) | async-done | bytes 524320 | tf_op jit(solution)/shard_map/all_to_all | solution.py:526
  76.1 0.5 collective-permute-start.12
  76.6 0.4 collective-permute-start.14
  77.1 0.8 fusion.pick_ref
  77.9 2.4 %shard_map.149 = bf16[4,256,512]{2,1,0:T(8,128)(2,1)} custom-call(bf16[256,512]{1,0:T(8,128)(2,1)} %fusion.pick_ref, bf16[16,32,512]{2,1,0:T(8,128)(2,1)} %copy-done.6), custom_call_target="tpu_custom_call" | custom-call | flops 1 | bytes 1 | tf_op jit(solution)/shard_map/pallas_call | solution.py:542
  80.4 18.2 %all_to_all.20 = bf16[4,256,512]{2,1,0:T(8,128)(2,1)S(1)} all-to-all(bf16[4,256,512]{2,1,0:T(8,128)(2,1)} %shard_map.149), channel_id=1, replica_groups={{0,2,4,6},{8,10,12,14},{16,18,20,22},{24,26,28,30},{1,3,5,7},{9,11,13,1..., dimensions={0} | all-to-all | bytes 2097152 | tf_op jit(solution)/shard_map/all_to_all | solution.py:553
  98.7 0.8 reshape.258
  99.4 0.6 constant_dynamic-slice_fusion
  100.0 1.3 collective-permute-done.15.far_ref
  101.3 1.0 copy-done.7
  102.3 10.2 %shard_map.150 = (bf16[1024,128]{1,0:T(8,128)(2,1)}, bf16[1024,128]{1,0:T(8,128)(2,1)}, bf16[1024,128]{1,0:T(8,128)(2,1)}, bf16[1024,128]{1,0:T(8,128)(2,1)}, bf...) custom-call(f32[1,1024]{1,0:T(1,128)} %broadcast_select_fusion.bias_ref,, ...), custom_call_target="tpu_custom_call" | custom-call | flops 1 | bytes 1 | tf_op jit(solution)/shard_map/pallas_call | solution.py:561
  112.5 1.0 collective-permute-start.16
  113.5 1.1 collective-permute-start.19
  114.6 0.9 collective-permute-start.20
  115.5 1.5 collective-permute-start.21
  117.0 0.6 collective-permute-start.17
  117.5 7.3 %collective-permute-done.19.refs_5_.refs_1_ = bf16[528,128]{1,0:T(8,128)(2,1)S(1)} collective-permute-done((bf16[528,128]{1,0:T(8,128)(2,1)}, bf16[528,128]{1,0:T(8,128)(2,1)S(1)}, u32[]{:S(2)}, u32[]{:S(2)}) %collective-permute-start.19) | collective-permute-done | bytes 135200 | tf_op jit(solution)/shard_map/ppermute | solution.py:413
  124.8 0.9 collective-permute-start.18
  125.7 1.9 %collective-permute-done.21.refs_7_.refs_3_ = bf16[528,128]{1,0:T(8,128)(2,1)S(1)} collective-permute-done((bf16[528,128]{1,0:T(8,128)(2,1)}, bf16[528,128]{1,0:T(8,128)(2,1)S(1)}, u32[]{:S(2)}, u32[]{:S(2)}) %collective-permute-start.21) | collective-permute-done | bytes 135200 | tf_op jit(solution)/shard_map/ppermute | solution.py:413
  127.6 0.9 copy-done.1
  128.5 0.4 shard_map.152.refs_0_
  128.9 0.4 collective-permute-start.22
  129.3 2.3 %collective-permute-start.23 = (bf16[512,128]{1,0:T(8,128)(2,1)S(1)}, bf16[512,128]{1,0:T(8,128)(2,1)S(1)}, u32[]{:S(2)}, u32[]{:S(2)}) collective-permute-start(bf16[512,128]{1,0:T(8,128)(2,1)S(1)} %shard_map.152.refs_0_), channel_id=1, source_target_pairs={{0,4},{2,6},{4,0},{6,2},{8,12},{10,14},{12,8},{14,10},{16,20},{18,... | collective-permute-start | bytes 393224 | tf_op jit(solution)/shard_map/ppermute | solution.py:413
  131.6 0.9 collective-permute-start.24
  132.5 3.4 %collective-permute-done.17.refs_2_ = bf16[1024,128]{1,0:T(8,128)(2,1)S(1)} collective-permute-done((bf16[1024,128]{1,0:T(8,128)(2,1)}, bf16[1024,128]{1,0:T(8,128)(2,1)S(1)}, u32[]{:S(2)}, u32[]{:S(2)}) %collective-permute-start.17) | collective-permute-done | bytes 262176 | tf_op jit(solution)/shard_map/ppermute | solution.py:413
  135.9 0.9 copy-done.2
  136.8 0.9 copy-done.4
  137.8 0.4 shard_map.151.query_ref
  138.2 1.4 collective-permute-done.23.refs_2_
  139.6 3.7 %shard_map.153 = bf16[16,144,128]{2,1,0:T(8,128)(2,1)} custom-call(s32[16]{0:T(128)S(1)} %and_select_fusion.1.place_ref, bf16[1024,128]{1,0:T(8,128)(2,1)S(1)} %shard_map.151.query_ref, bf16[512,128]{1,0:T(8,128)(2,1)S(1)} %shard_map.152.refs_0_, bf16[512,128]{1,0:T(8,128)(2,1)S(1)} %collective-permute-done.22.refs_1_, ...), custom_call_target="tpu_custom_call" | custom-call | flops 1 | bytes 1 | tf_op jit(solution)/shard_map/pallas_call | solution.py:601
  143.3 4.5 %all-to-all-start.3 = ((bf16[16,144,128]{2,1,0:T(8,128)(2,1)}), bf16[16,144,128]{2,1,0:T(8,128)(2,1)S(1)}, u32[]{:S(2)}, u32[]{:S(2)}) async-start(bf16[16,144,128]{2,1,0:T(8,128)(2,1)} %shard_map.153), calls=%async_computation.3 | async-start | bytes 1179648 | tf_op jit(solution)/shard_map/all_to_all | solution.py:615
  149.5 0.6 iota_compare_fusion.6
  150.3 13.4 %all-to-all-done.3.pieces_ref = bf16[16,144,128]{2,1,0:T(8,128)(2,1)S(1)} async-done(((bf16[16,144,128]{2,1,0:T(8,128)(2,1)}), bf16[16,144,128]{2,1,0:T(8,128)(2,1)S(1)}, u32[]{:S(2)}, u32[]{:S(2)}) %all-to-all-start.3) | async-done | bytes 589856 | tf_op jit(solution)/shard_map/all_to_all | solution.py:615
  163.7 2.2 %copy-done = bf16[2048,1024]{1,0:T(8,128)(2,1)S(1)} copy-done((bf16[2048,1024]{1,0:T(8,128)(2,1)S(1)}, bf16[2048,1024]{1,0:T(8,128)(2,1)}, u32[]{:S(2)}) %copy-start) | copy-done | bytes 4194328
  165.8 0.8 shard_map.154
  166.9 1.4 collective-permute-done.25.other_ref
  168.3 0.9 shard_map.155
  (95 shorter events, 1.6 us)
Async XLA Ops:
  0.0 21.2 %copy-start.25 = (s32[16]{0:T(128)S(1)}, s32[16]{0:T(128)}, u32[]{:S(2)}) copy-start(s32[16]{0:T(128)} %param.22) | copy-start | bytes 196
  0.0 22.7 %copy-start.26 = (s32[1,128]{1,0:T(1,128)S(1)}, s32[1,128]{1,0:T(1,128)}, u32[]{:S(2)}) copy-start(s32[1,128]{1,0:T(1,128)} %param.21) | copy-start | bytes 1540
  0.0 23.0 %collective-permute-start = (bf16[64,2048]{1,0:T(8,128)(2,1)}, bf16[64,2048]{1,0:T(8,128)(2,1)S(1)}, u32[]{:S(2)}, u32[]{:S(2)}) collective-permute-start(bf16[64,2048]{1,0:T(8,128)(2,1)} %refs_0_.2), channel_id=1, source_target_pairs={{0,8},{2,10},{4,12},{6,14},{8,0},{10,2},{12,4},{14,6},{16,24},{18,... | collective-permute-start | bytes 786440 | tf_op jit(solution)/shard_map/ppermute | solution.py:413
  3.0 22.4 %collective-permute-start.1 = (bf16[64,2048]{1,0:T(8,128)(2,1)}, bf16[64,2048]{1,0:T(8,128)(2,1)S(1)}, u32[]{:S(2)}, u32[]{:S(2)}) collective-permute-start(bf16[64,2048]{1,0:T(8,128)(2,1)} %refs_0_.2), channel_id=1, source_target_pairs={{0,16},{2,18},{4,20},{6,22},{8,24},{10,26},{12,28},{14,30},{16,0},... | collective-permute-start | bytes 786440 | tf_op jit(solution)/shard_map/ppermute | solution.py:413
  5.6 27.7 %collective-permute-start.2 = (bf16[64,2048]{1,0:T(8,128)(2,1)}, bf16[64,2048]{1,0:T(8,128)(2,1)S(1)}, u32[]{:S(2)}, u32[]{:S(2)}) collective-permute-start(bf16[64,2048]{1,0:T(8,128)(2,1)} %refs_0_.2), channel_id=1, source_target_pairs={{0,24},{2,26},{4,28},{6,30},{8,16},{10,18},{12,20},{14,22},{16,8},... | collective-permute-start | bytes 786440 | tf_op jit(solution)/shard_map/ppermute | solution.py:413
  6.3 31.0 %collective-permute-start.4 = (f32[1,512]{1,0:T(1,128)S(1)}, f32[1,512]{1,0:T(1,128)S(1)}, u32[]{:S(2)}, u32[]{:S(2)}) collective-permute-start(f32[1,512]{1,0:T(1,128)S(1)} %bitcast.12), channel_id=1, source_target_pairs={{0,1},{1,0},{2,3},{3,2},{4,5},{5,4},{6,7},{7,6},{8,9},{9,8},{10,11... | collective-permute-start | bytes 6152 | tf_op jit(solution)/shard_map/ppermute | solution.py:23
  12.1 21.1 %all-to-all-start = ((f32[16,2,512]{2,1,0:T(2,128)}), f32[16,2,512]{2,1,0:T(2,128)S(1)}, u32[]{:S(2)}, u32[]{:S(2)}) async-start(f32[16,2,512]{2,1,0:T(2,128)} %get-tuple-element.54), calls=%async_computation | async-start | bytes 131072 | tf_op jit(solution)/shard_map/all_to_all | solution.py:494
  19.2 18.7 %collective-permute-start.5 = (bf16[256,768]{1,0:T(8,128)(2,1)}, bf16[256,768]{1,0:T(8,128)(2,1)S(1)}, u32[]{:S(2)}, u32[]{:S(2)}) collective-permute-start(bf16[256,768]{1,0:T(8,128)(2,1)} %get-tuple-element.57), channel_id=1, source_target_pairs={{0,8},{2,10},{4,12},{6,14},{8,0},{10,2},{12,4},{14,6},{16,24},{18,... | collective-permute-start | bytes 1179656 | tf_op jit(solution)/shard_map/ppermute | solution.py:413
  22.1 54.0 %copy-start.23 = (s32[16]{0:T(128)}, s32[16]{0:T(128)S(1)}, u32[]{:S(2)}) copy-start(s32[16]{0:T(128)S(1)} %get-tuple-element.100) | copy-start | bytes 196
  23.0 24.7 %copy-start.20 = (bf16[64,2048]{1,0:T(8,128)(2,1)}, bf16[64,2048]{1,0:T(8,128)(2,1)S(1)}, u32[]{:S(2)}) copy-start(bf16[64,2048]{1,0:T(8,128)(2,1)S(1)} %collective-permute-done.refs_1_) | copy-start | bytes 786436
  23.0 39.5 %collective-permute-start.6 = (bf16[256,768]{1,0:T(8,128)(2,1)}, bf16[256,768]{1,0:T(8,128)(2,1)S(1)}, u32[]{:S(2)}, u32[]{:S(2)}) collective-permute-start(bf16[256,768]{1,0:T(8,128)(2,1)} %get-tuple-element.64), channel_id=1, source_target_pairs={{0,16},{2,18},{4,20},{6,22},{8,24},{10,26},{12,28},{14,30},{16,0},... | collective-permute-start | bytes 1179656 | tf_op jit(solution)/shard_map/ppermute | solution.py:413
  25.4 22.3 %copy-start.21 = (bf16[64,2048]{1,0:T(8,128)(2,1)}, bf16[64,2048]{1,0:T(8,128)(2,1)S(1)}, u32[]{:S(2)}) copy-start(bf16[64,2048]{1,0:T(8,128)(2,1)S(1)} %collective-permute-done.1.refs_2_) | copy-start | bytes 786436
  25.4 37.1 %collective-permute-start.7 = (bf16[256,768]{1,0:T(8,128)(2,1)}, bf16[256,768]{1,0:T(8,128)(2,1)S(1)}, u32[]{:S(2)}, u32[]{:S(2)}) collective-permute-start(bf16[256,768]{1,0:T(8,128)(2,1)} %get-tuple-element.65), channel_id=1, source_target_pairs={{0,24},{2,26},{4,28},{6,30},{8,16},{10,18},{12,20},{14,22},{16,8},... | collective-permute-start | bytes 1179656 | tf_op jit(solution)/shard_map/ppermute | solution.py:413
  33.3 0.6 copy-start.19
  33.3 14.4 %copy-start.22 = (bf16[64,2048]{1,0:T(8,128)(2,1)}, bf16[64,2048]{1,0:T(8,128)(2,1)S(1)}, u32[]{:S(2)}) copy-start(bf16[64,2048]{1,0:T(8,128)(2,1)S(1)} %collective-permute-done.2.refs_3_) | copy-start | bytes 786436
  36.6 2.1 %collective-permute-start.3 = (f32[256,512]{1,0:T(8,128)}, f32[256,512]{1,0:T(8,128)S(1)}, u32[]{:S(2)}, u32[]{:S(2)}) collective-permute-start(f32[256,512]{1,0:T(8,128)} %get-tuple-element.56), channel_id=1, source_target_pairs={{0,1},{1,0},{2,3},{3,2},{4,5},{5,4},{6,7},{7,6},{8,9},{9,8},{10,11... | collective-permute-start | bytes 1572872 | tf_op jit(solution)/shard_map/ppermute | solution.py:23
  37.9 63.4 %copy-start.9 = (bf16[256,768]{1,0:T(8,128)(2,1)}, bf16[256,768]{1,0:T(8,128)(2,1)S(1)}, u32[]{:S(2)}) copy-start(bf16[256,768]{1,0:T(8,128)(2,1)S(1)} %collective-permute-done.5.refs_9_) | copy-start | bytes 1179652
  38.7 0.8 copy-start.8
  42.4 33.7 %all-to-all-start.1 = ((bf16[16,32,512]{2,1,0:T(8,128)(2,1)}), bf16[16,32,512]{2,1,0:T(8,128)(2,1)S(1)}, u32[]{:S(2)}, u32[]{:S(2)}) async-start(bf16[16,32,512]{2,1,0:T(8,128)(2,1)} %get-tuple-element.61.gate_ref), calls=%async_computation.1 | async-start | bytes 1048576 | tf_op jit(solution)/shard_map/all_to_all | solution.py:526
  50.0 13.4 %collective-permute-start.10 = (bf16[4,64,512]{2,1,0:T(8,128)(2,1)}, bf16[4,64,512]{2,1,0:T(8,128)(2,1)S(1)}, u32[]{:S(2)}, u32[]{:S(2)}) collective-permute-start(bf16[4,64,512]{2,1,0:T(8,128)(2,1)} %get-tuple-element.73), channel_id=1, source_target_pairs={{0,6},{2,4},{4,2},{6,0},{8,14},{10,12},{12,10},{14,8},{16,22},{18,... | collective-permute-start | bytes 786440 | tf_op jit(solution)/shard_map/ppermute | solution.py:413
  52.9 15.5 %collective-permute-start.8 = (bf16[4,64,512]{2,1,0:T(8,128)(2,1)}, bf16[4,64,512]{2,1,0:T(8,128)(2,1)S(1)}, u32[]{:S(2)}, u32[]{:S(2)}) collective-permute-start(bf16[4,64,512]{2,1,0:T(8,128)(2,1)} %get-tuple-element.71), channel_id=1, source_target_pairs={{0,2},{2,0},{4,6},{6,4},{8,10},{10,8},{12,14},{14,12},{16,18},{18,... | collective-permute-start | bytes 786440 | tf_op jit(solution)/shard_map/ppermute | solution.py:413
  53.4 14.9 %collective-permute-start.9 = (bf16[4,64,512]{2,1,0:T(8,128)(2,1)}, bf16[4,64,512]{2,1,0:T(8,128)(2,1)S(1)}, u32[]{:S(2)}, u32[]{:S(2)}) collective-permute-start(bf16[4,64,512]{2,1,0:T(8,128)(2,1)} %get-tuple-element.72), channel_id=1, source_target_pairs={{0,4},{2,6},{4,0},{6,2},{8,12},{10,14},{12,8},{14,10},{16,20},{18,... | collective-permute-start | bytes 786440 | tf_op jit(solution)/shard_map/ppermute | solution.py:413
  62.6 38.7 %copy-start.10 = (bf16[256,768]{1,0:T(8,128)(2,1)}, bf16[256,768]{1,0:T(8,128)(2,1)S(1)}, u32[]{:S(2)}) copy-start(bf16[256,768]{1,0:T(8,128)(2,1)S(1)} %collective-permute-done.6.refs_10_) | copy-start | bytes 1179652
  62.6 38.7 %copy-start.11 = (bf16[256,768]{1,0:T(8,128)(2,1)}, bf16[256,768]{1,0:T(8,128)(2,1)S(1)}, u32[]{:S(2)}) copy-start(bf16[256,768]{1,0:T(8,128)(2,1)S(1)} %collective-permute-done.7.refs_11_) | copy-start | bytes 1179652
  63.3 38.0 %copy-start.12 = (bf16[4,64,512]{2,1,0:T(8,128)(2,1)}, bf16[4,64,512]{2,1,0:T(8,128)(2,1)S(1)}, u32[]{:S(2)}) copy-start(bf16[4,64,512]{2,1,0:T(8,128)(2,1)S(1)} %collective-permute-done.10.refs_3_) | copy-start | bytes 786436
  68.3 12.0 %copy-start.13 = (bf16[4,64,512]{2,1,0:T(8,128)(2,1)}, bf16[4,64,512]{2,1,0:T(8,128)(2,1)S(1)}, u32[]{:S(2)}) copy-start(bf16[4,64,512]{2,1,0:T(8,128)(2,1)S(1)} %collective-permute-done.8.refs_1_) | copy-start | bytes 786436
  68.3 12.0 %copy-start.14 = (bf16[4,64,512]{2,1,0:T(8,128)(2,1)}, bf16[4,64,512]{2,1,0:T(8,128)(2,1)S(1)}, u32[]{:S(2)}) copy-start(bf16[4,64,512]{2,1,0:T(8,128)(2,1)S(1)} %collective-permute-done.9.refs_2_) | copy-start | bytes 786436
  76.0 1.9 %copy-start.6 = (bf16[16,32,512]{2,1,0:T(8,128)(2,1)}, bf16[16,32,512]{2,1,0:T(8,128)(2,1)S(1)}, u32[]{:S(2)}) copy-start(bf16[16,32,512]{2,1,0:T(8,128)(2,1)S(1)} %all-to-all-done.1.arrived_ref) | copy-start | bytes 1572868
  76.0 4.3 %collective-permute-start.11 = (bf16[4,64,512]{2,1,0:T(8,128)(2,1)}, bf16[4,64,512]{2,1,0:T(8,128)(2,1)S(1)}, u32[]{:S(2)}, u32[]{:S(2)}) collective-permute-start(bf16[4,64,512]{2,1,0:T(8,128)(2,1)} %get-tuple-element.75.refs_0_), channel_id=1, source_target_pairs={{0,1},{1,0},{2,3},{3,2},{4,5},{5,4},{6,7},{7,6},{8,9},{9,8},{10,11... | collective-permute-start | bytes 786440 | tf_op jit(solution)/shard_map/ppermute | solution.py:23
  76.1 4.3 %collective-permute-start.12 = (bf16[4,64,512]{2,1,0:T(8,128)(2,1)S(1)}, bf16[4,64,512]{2,1,0:T(8,128)(2,1)S(1)}, u32[]{:S(2)}, u32[]{:S(2)}) collective-permute-start(bf16[4,64,512]{2,1,0:T(8,128)(2,1)S(1)} %collective-permute-done.8.refs_1_), channel_id=1, source_target_pairs={{0,1},{1,0},{2,3},{3,2},{4,5},{5,4},{6,7},{7,6},{8,9},{9,8},{10,11... | collective-permute-start | bytes 786440 | tf_op jit(solution)/shard_map/ppermute | solution.py:23
  76.6 3.8 %collective-permute-start.13 = (bf16[4,64,512]{2,1,0:T(8,128)(2,1)S(1)}, bf16[4,64,512]{2,1,0:T(8,128)(2,1)S(1)}, u32[]{:S(2)}, u32[]{:S(2)}) collective-permute-start(bf16[4,64,512]{2,1,0:T(8,128)(2,1)S(1)} %collective-permute-done.9.refs_2_), channel_id=1, source_target_pairs={{0,1},{1,0},{2,3},{3,2},{4,5},{5,4},{6,7},{7,6},{8,9},{9,8},{10,11... | collective-permute-start | bytes 786440 | tf_op jit(solution)/shard_map/ppermute | solution.py:23
  76.6 3.8 %collective-permute-start.14 = (bf16[4,64,512]{2,1,0:T(8,128)(2,1)S(1)}, bf16[4,64,512]{2,1,0:T(8,128)(2,1)S(1)}, u32[]{:S(2)}, u32[]{:S(2)}) collective-permute-start(bf16[4,64,512]{2,1,0:T(8,128)(2,1)S(1)} %collective-permute-done.10.refs_3_), channel_id=1, source_target_pairs={{0,1},{1,0},{2,3},{3,2},{4,5},{5,4},{6,7},{7,6},{8,9},{9,8},{10,11... | collective-permute-start | bytes 786440 | tf_op jit(solution)/shard_map/ppermute | solution.py:23
  80.3 18.2 %copy-start.15 = (bf16[4,64,512]{2,1,0:T(8,128)(2,1)}, bf16[4,64,512]{2,1,0:T(8,128)(2,1)S(1)}, u32[]{:S(2)}) copy-start(bf16[4,64,512]{2,1,0:T(8,128)(2,1)S(1)} %collective-permute-done.11.refs_4_) | copy-start | bytes 786436
  80.3 18.2 %copy-start.16 = (bf16[4,64,512]{2,1,0:T(8,128)(2,1)}, bf16[4,64,512]{2,1,0:T(8,128)(2,1)S(1)}, u32[]{:S(2)}) copy-start(bf16[4,64,512]{2,1,0:T(8,128)(2,1)S(1)} %collective-permute-done.12.refs_5_) | copy-start | bytes 786436
  80.4 18.2 %copy-start.17 = (bf16[4,64,512]{2,1,0:T(8,128)(2,1)}, bf16[4,64,512]{2,1,0:T(8,128)(2,1)S(1)}, u32[]{:S(2)}) copy-start(bf16[4,64,512]{2,1,0:T(8,128)(2,1)S(1)} %collective-permute-done.13.refs_6_) | copy-start | bytes 786436
  80.4 18.2 %copy-start.18 = (bf16[4,64,512]{2,1,0:T(8,128)(2,1)}, bf16[4,64,512]{2,1,0:T(8,128)(2,1)S(1)}, u32[]{:S(2)}) copy-start(bf16[4,64,512]{2,1,0:T(8,128)(2,1)S(1)} %collective-permute-done.14.refs_7_) | copy-start | bytes 786436
  98.6 2.8 %copy-start.5 = (bf16[4,256,512]{2,1,0:T(8,128)(2,1)}, bf16[4,256,512]{2,1,0:T(8,128)(2,1)S(1)}, u32[]{:S(2)}) copy-start(bf16[4,256,512]{2,1,0:T(8,128)(2,1)S(1)} %all_to_all.20) | copy-start | bytes 3145732
  98.6 2.7 %collective-permute-start.15 = (bf16[1024,512]{1,0:T(8,128)(2,1)S(1)}, bf16[1024,512]{1,0:T(8,128)(2,1)S(1)}, u32[]{:S(2)}, u32[]{:S(2)}) collective-permute-start(bf16[1024,512]{1,0:T(8,128)(2,1)S(1)} %bitcast.9), channel_id=1, source_target_pairs={{0,1},{1,0},{2,3},{3,2},{4,5},{5,4},{6,7},{7,6},{8,9},{9,8},{10,11... | collective-permute-start | bytes 3145736 | tf_op jit(solution)/shard_map/ppermute | solution.py:23
  99.4 33.0 %copy-start.24 = (s32[16]{0:T(128)S(1)}, s32[16]{0:T(128)}, u32[]{:S(2)}) copy-start(s32[16]{0:T(128)} %copy-done.23) | copy-start | bytes 196
  101.3 1.0 copy-start.7
  102.3 47.9 %copy-start.27 = (s32[1,128]{1,0:T(1,128)S(1)}, s32[1,128]{1,0:T(1,128)}, u32[]{:S(2)}) copy-start(s32[1,128]{1,0:T(1,128)} %param.21) | copy-start | bytes 1540
  112.5 19.1 %collective-permute-start.16 = (bf16[1024,128]{1,0:T(8,128)(2,1)}, bf16[1024,128]{1,0:T(8,128)(2,1)S(1)}, u32[]{:S(2)}, u32[]{:S(2)}) collective-permute-start(bf16[1024,128]{1,0:T(8,128)(2,1)} %get-tuple-element.89), channel_id=1, source_target_pairs={{0,2},{2,0},{4,6},{6,4},{8,10},{10,8},{12,14},{14,12},{16,18},{18,... | collective-permute-start | bytes 786440 | tf_op jit(solution)/shard_map/ppermute | solution.py:413
  113.5 11.4 %collective-permute-start.19 = (bf16[528,128]{1,0:T(8,128)(2,1)}, bf16[528,128]{1,0:T(8,128)(2,1)S(1)}, u32[]{:S(2)}, u32[]{:S(2)}) collective-permute-start(bf16[528,128]{1,0:T(8,128)(2,1)} %get-tuple-element.93), channel_id=1, source_target_pairs={{0,2},{2,0},{4,6},{6,4},{8,10},{10,8},{12,14},{14,12},{16,18},{18,... | collective-permute-start | bytes 405512 | tf_op jit(solution)/shard_map/ppermute | solution.py:413
  114.6 11.1 %collective-permute-start.20 = (bf16[528,128]{1,0:T(8,128)(2,1)}, bf16[528,128]{1,0:T(8,128)(2,1)S(1)}, u32[]{:S(2)}, u32[]{:S(2)}) collective-permute-start(bf16[528,128]{1,0:T(8,128)(2,1)} %get-tuple-element.94), channel_id=1, source_target_pairs={{0,4},{2,6},{4,0},{6,2},{8,12},{10,14},{12,8},{14,10},{16,20},{18,... | collective-permute-start | bytes 405512 | tf_op jit(solution)/shard_map/ppermute | solution.py:413
  115.5 12.1 %collective-permute-start.21 = (bf16[528,128]{1,0:T(8,128)(2,1)}, bf16[528,128]{1,0:T(8,128)(2,1)S(1)}, u32[]{:S(2)}, u32[]{:S(2)}) collective-permute-start(bf16[528,128]{1,0:T(8,128)(2,1)} %get-tuple-element.95), channel_id=1, source_target_pairs={{0,6},{2,4},{4,2},{6,0},{8,14},{10,12},{12,10},{14,8},{16,22},{18,... | collective-permute-start | bytes 405512 | tf_op jit(solution)/shard_map/ppermute | solution.py:413
  117.0 18.9 %collective-permute-start.17 = (bf16[1024,128]{1,0:T(8,128)(2,1)}, bf16[1024,128]{1,0:T(8,128)(2,1)S(1)}, u32[]{:S(2)}, u32[]{:S(2)}) collective-permute-start(bf16[1024,128]{1,0:T(8,128)(2,1)} %get-tuple-element.90), channel_id=1, source_target_pairs={{0,4},{2,6},{4,0},{6,2},{8,12},{10,14},{12,8},{14,10},{16,20},{18,... | collective-permute-start | bytes 786440 | tf_op jit(solution)/shard_map/ppermute | solution.py:413
  124.8 11.1 %collective-permute-start.18 = (bf16[1024,128]{1,0:T(8,128)(2,1)}, bf16[1024,128]{1,0:T(8,128)(2,1)S(1)}, u32[]{:S(2)}, u32[]{:S(2)}) collective-permute-start(bf16[1024,128]{1,0:T(8,128)(2,1)} %get-tuple-element.91), channel_id=1, source_target_pairs={{0,6},{2,4},{4,2},{6,0},{8,14},{10,12},{12,10},{14,8},{16,22},{18,... | collective-permute-start | bytes 786440 | tf_op jit(solution)/shard_map/ppermute | solution.py:413
  127.6 0.9 copy-start.1
  128.9 9.3 %collective-permute-start.22 = (bf16[512,128]{1,0:T(8,128)(2,1)S(1)}, bf16[512,128]{1,0:T(8,128)(2,1)S(1)}, u32[]{:S(2)}, u32[]{:S(2)}) collective-permute-start(bf16[512,128]{1,0:T(8,128)(2,1)S(1)} %shard_map.152.refs_0_), channel_id=1, source_target_pairs={{0,2},{2,0},{4,6},{6,4},{8,10},{10,8},{12,14},{14,12},{16,18},{18,... | collective-permute-start | bytes 393224 | tf_op jit(solution)/shard_map/ppermute | solution.py:413
  129.3 10.3 %collective-permute-start.23 = (bf16[512,128]{1,0:T(8,128)(2,1)S(1)}, bf16[512,128]{1,0:T(8,128)(2,1)S(1)}, u32[]{:S(2)}, u32[]{:S(2)}) collective-permute-start(bf16[512,128]{1,0:T(8,128)(2,1)S(1)} %shard_map.152.refs_0_), channel_id=1, source_target_pairs={{0,4},{2,6},{4,0},{6,2},{8,12},{10,14},{12,8},{14,10},{16,20},{18,... | collective-permute-start | bytes 393224 | tf_op jit(solution)/shard_map/ppermute | solution.py:413
  131.6 8.0 %collective-permute-start.24 = (bf16[512,128]{1,0:T(8,128)(2,1)S(1)}, bf16[512,128]{1,0:T(8,128)(2,1)S(1)}, u32[]{:S(2)}, u32[]{:S(2)}) collective-permute-start(bf16[512,128]{1,0:T(8,128)(2,1)S(1)} %shard_map.152.refs_0_), channel_id=1, source_target_pairs={{0,6},{2,4},{4,2},{6,0},{8,14},{10,12},{12,10},{14,8},{16,22},{18,... | collective-permute-start | bytes 393224 | tf_op jit(solution)/shard_map/ppermute | solution.py:413
  135.9 0.9 copy-start.2
  136.8 0.9 copy-start.4
  138.2 30.2 %copy-start.3 = (bf16[256,512]{1,0:T(8,128)(2,1)S(1)}, bf16[256,512]{1,0:T(8,128)(2,1)}, u32[]{:S(2)}) copy-start(bf16[256,512]{1,0:T(8,128)(2,1)} %get-tuple-element.98.encoded_ref) | copy-start | bytes 786436
  143.3 20.4 %all-to-all-start.3 = ((bf16[16,144,128]{2,1,0:T(8,128)(2,1)}), bf16[16,144,128]{2,1,0:T(8,128)(2,1)S(1)}, u32[]{:S(2)}, u32[]{:S(2)}) async-start(bf16[16,144,128]{2,1,0:T(8,128)(2,1)} %shard_map.153), calls=%async_computation.3 | async-start | bytes 1179648 | tf_op jit(solution)/shard_map/all_to_all | solution.py:615
  163.7 2.2 %copy-start = (bf16[2048,1024]{1,0:T(8,128)(2,1)S(1)}, bf16[2048,1024]{1,0:T(8,128)(2,1)}, u32[]{:S(2)}) copy-start(bf16[2048,1024]{1,0:T(8,128)(2,1)} %weight_ref.1) | copy-start | bytes 12582916
  166.7 1.6 collective-permute-start.25

commit v2 on v1

--- a/solution.py
+++ b/solution.py
@@ -203,12 +203,13 @@
 def own_kernel(pick_ref, arrived_ref, out_ref):
     shards, slots, half = arrived_ref.shape
     rows = arrived_ref[...].reshape(shards * slots, half)
-    own = jnp.dot(pick_ref[...], rows, preferred_element_type=jnp.float32).astype(jnp.bfloat16)
-    for index in range(out_ref.shape[0]):
-        out_ref[index] = own
-
-
-def inner_kernel(plane, layers, bias_ref, gain_ref, near_ref, far_ref, *refs):
+    own = jnp.dot(pick_ref[...], rows, preferred_element_type=jnp.float32)
+    out_ref[...] = own.astype(jnp.bfloat16)
+
+
+def inner_kernel(plane, layers, bias_ref, gain_ref, *refs):
+    near, refs = refs[:plane], refs[plane:]
+    far, refs = refs[:plane], refs[plane:]
     up_own, refs = refs[:plane], refs[plane:]
     up_far, refs = refs[:plane], refs[plane:]
     pieces, refs = refs[:layers], refs[layers:]
@@ -216,12 +217,13 @@
     pooled, up, weights, squares, queries_held, pairs_held, sems, out_sems = refs
     me, lane = seat()
     layer, cross = me // plane, lax.rem(me, plane)
-    half = near_ref.shape[1]
+    near_rows, half = near[0].shape
     up_rows, up_half = up_own[0].shape[1:]
-    pairs = [
-        (near_ref, pooled.at[:, lanes(lane, half)]),
-        (far_ref, pooled.at[:, lanes(1 - lane, half)]),
-    ]
+    pairs = []
+    for mask in range(plane):
+        where = rows_at(cross ^ mask, near_rows)
+        pairs.append((near[mask], pooled.at[where, lanes(lane, half)]))
+        pairs.append((far[mask], pooled.at[where, lanes(1 - lane, half)]))
     for step in range(layers):
         for mask in range(plane):
             where = rows_at((layer ^ step) * plane + (cross ^ mask), up_rows)
@@ -407,7 +409,6 @@
     weight_rows = query_weight.shape[0]
     f32, bf16 = jnp.float32, jnp.bfloat16
     layer, cross = me // plane, me % plane
-    plane_groups = [[first * plane + step for step in range(plane)] for first in range(layers)]
 
     def over(value, mask):
         return lax.ppermute(value, "seq", [(i, i ^ mask) for i in range(shards)])
@@ -541,7 +542,7 @@
     arrived, pieces, up_own = lax.optimization_barrier((arrived, pieces, up_own))
     near_rows = pl.pallas_call(
         own_kernel,
-        out_shape=jax.ShapeDtypeStruct((plane, layers * CH_OWN, half), bf16),
+        out_shape=jax.ShapeDtypeStruct((layers * CH_OWN, half), bf16),
         in_specs=[vmem()] * 2,
         out_specs=vmem(),
         cost_estimate=brief(),
@@ -550,9 +551,8 @@
     near_rows, up_far = lax.optimization_barrier(
         (near_rows, [swapped(piece) for piece in up_own])
     )
-    near = lax.all_to_all(
-        near_rows, "seq", 0, 0, axis_index_groups=plane_groups, tiled=True
-    ).reshape(total_rows, half)
+    near = [near_rows] + [over(near_rows, mask) for mask in range(1, plane)]
+    far = [swapped(piece) for piece in near]
 
     features = own_gain.shape[1]
     block = total_rows // plane
@@ -562,7 +562,7 @@
         functools.partial(inner_kernel, plane, layers),
         out_shape=(jax.ShapeDtypeStruct((total_rows, HEAD), bf16),) * plane
         + (jax.ShapeDtypeStruct((pair_rows, HEAD), bf16),) * plane,
-        in_specs=[vmem()] * 2 + [in_place()] * (2 + 2 * plane + layers),
+        in_specs=[vmem()] * 2 + [in_place()] * (4 * plane + layers),
         out_specs=(in_place(),) * (2 * plane),
         scratch_shapes=[
             pltpu.VMEM((total_rows, width), bf16),
@@ -571,12 +571,12 @@
             pltpu.VMEM((8, total_rows), f32),
             pltpu.VMEM((plane, total_rows, HEAD), bf16),
             pltpu.VMEM((plane, pair_rows, HEAD), bf16),
-            pltpu.SemaphoreType.DMA((2 + 2 * shards + layers,)),
+            pltpu.SemaphoreType.DMA((2 * plane + 2 * shards + layers,)),
             pltpu.SemaphoreType.DMA((2 * plane,)),
         ],
         cost_estimate=brief(),
         compiler_params=params(56),
-    )(bias, own_gain, near, swapped(near), *up_own, *up_far, *pieces)
+    )(bias, own_gain, *near, *far, *up_own, *up_far, *pieces)
     query_sums, pair_sums = partial_sums[:plane], partial_sums[plane:]
     got_pairs = [pair_sums[0]] + [over(pair_sums[mask], mask) for mask in range(1, plane)]
     got_queries = [query_sums[0]] + [over(query_sums[mask], mask) for mask in range(1, plane)]

time: 170 us -> 166 us (0.976)
  blocking collectives: 18.2 us -> 0 us
  starting transfers between devices: 43.2 us -> 50.5 us
  waiting for transfers between devices: 58.6 us -> 65.6 us
    all_to_all x1 -> x0, blocking collectives: 18.2 us -> none  [one_head_each(): lax.all_to_all(near_rows, 'seq', 0, 0, axis_index_groups=plane_groups, ti...]
    ppermute x18 -> x21, waiting for transfers between devices: 28.5 us -> 36.9 us  [over(): return lax.ppermute(value, 'seq', [(i, i ^ mask) for i in range(shards)])]
    ppermute x18 -> x21, starting transfers between devices: 25.3 us -> 30.9 us  [over(): return lax.ppermute(value, 'seq', [(i, i ^ mask) for i in range(shards)])]
    ppermute x8 -> x11, waiting for transfers between devices: 3.5 us -> 2.8 us  [swapped(): return lax.ppermute(value, 'mp', [(0, 1), (1, 0)])]
  transfers between devices with their start and end apart: 29 -> 35, of which waited for: 13 -> 17; matrix products, arithmetic and copies ran while one was open for 4% -> 5% of each run, Pallas kernels for 10% -> 10%
where the time goes in v2:
time: 166 us; the launch traced here: 165 us
  waiting for transfers between devices  65.6 us (40%)
  starting transfers between devices  50.5 us (30%)
  Pallas kernels  32.2 us (19%)
  local copies, waits for them, and re-layouts  8.85 us (5%)
  other arithmetic  5.21 us (3%)
  between operations  2.45 us (1%)
    ppermute x21, waiting for transfers between devices, over(): return lax.ppermute(value, 'seq', [(i, i ^ mask) for i in range(shards)])  36.9 us
    ppermute x21, starting transfers between devices, over(): return lax.ppermute(value, 'seq', [(i, i ^ mask) for i in range(shards)])  30.9 us
    all_to_all x1, waiting for transfers between devices, one_head_each(): pieces = lax.all_to_all(leaving, 'seq', 0, 0, tiled=True)  12.7 us
    pallas_call x1, Pallas kernels, one_head_each(): pl.pallas_call(functools.partial(inner_kernel, plane, layers), out_shape=...  10.3 us
    all_to_all x1, waiting for transfers between devices, one_head_each(): arrived = lax.all_to_all(leaving, 'seq', 0, 0, tiled=True)  7.72 us
    all_to_all x1, starting transfers between devices, one_head_each(): ends = lax.all_to_all(ends, 'seq', 0, 0, tiled=True)  7.1 us
    unnamed x56, local copies, waits for them, and re-layouts  6.47 us
    all_to_all x1, starting transfers between devices, one_head_each(): pieces = lax.all_to_all(leaving, 'seq', 0, 0, tiled=True)  5.88 us
  transfers between devices with their start and end apart: 35, of which 17 were waited for; matrix products, arithmetic and copies ran while one was open for 5% of the time, Pallas kernels for 10%

profile of v2, /device:TPU:0, one launch (start us, length us, event | category | flops | bytes accessed | tf_op | source)
XLA Modules:
  0.0 164.8 jit_solution(2808613978128042593)
XLA Ops:
  0.0 3.0 %collective-permute-start = (bf16[64,2048]{1,0:T(8,128)(2,1)}, bf16[64,2048]{1,0:T(8,128)(2,1)S(1)}, u32[]{:S(2)}, u32[]{:S(2)}) collective-permute-start(bf16[64,2048]{1,0:T(8,128)(2,1)} %refs_0_.2), channel_id=1, source_target_pairs={{0,8},{2,10},{4,12},{6,14},{8,0},{10,2},{12,4},{14,6},{16,24},{18,... | collective-permute-start | bytes 786440 | tf_op jit(solution)/shard_map/ppermute | solution.py:414
  3.0 2.6 %collective-permute-start.1 = (bf16[64,2048]{1,0:T(8,128)(2,1)}, bf16[64,2048]{1,0:T(8,128)(2,1)S(1)}, u32[]{:S(2)}, u32[]{:S(2)}) collective-permute-start(bf16[64,2048]{1,0:T(8,128)(2,1)} %refs_0_.2), channel_id=1, source_target_pairs={{0,16},{2,18},{4,20},{6,22},{8,24},{10,26},{12,28},{14,30},{16,0},... | collective-permute-start | bytes 786440 | tf_op jit(solution)/shard_map/ppermute | solution.py:414
  5.6 0.7 reshape.254
  6.4 5.7 %shard_map.145 = (f32[256,512]{1,0:T(8,128)}, f32[256,512]{1,0:T(8,128)}, f32[16,2,512]{2,1,0:T(2,128)}, bf16[256,768]{1,0:T(8,128)(2,1)}, bf16[256,768]{1,0:T(8...) custom-call(bf16[256,1024]{1,0:T(8,128)(2,1)} %bytes_ref.1, f32[1,1024]{1,0:T(1,128)} %bitcast.11, ...), custom_call_target="tpu_custom_call" | custom-call | flops 1 | bytes 1 | tf_op jit(solution)/shard_map/pallas_call | solution.py:461
  12.1 7.1 %all-to-all-start = ((f32[16,2,512]{2,1,0:T(2,128)}), f32[16,2,512]{2,1,0:T(2,128)S(1)}, u32[]{:S(2)}, u32[]{:S(2)}) async-start(f32[16,2,512]{2,1,0:T(2,128)} %get-tuple-element.54), calls=%async_computation | async-start | bytes 131072 | tf_op jit(solution)/shard_map/all_to_all | solution.py:495
  19.2 1.9 %collective-permute-start.5 = (bf16[256,768]{1,0:T(8,128)(2,1)}, bf16[256,768]{1,0:T(8,128)(2,1)S(1)}, u32[]{:S(2)}, u32[]{:S(2)}) collective-permute-start(bf16[256,768]{1,0:T(8,128)(2,1)} %get-tuple-element.57), channel_id=1, source_target_pairs={{0,8},{2,10},{4,12},{6,14},{8,0},{10,2},{12,4},{14,6},{16,24},{18,... | collective-permute-start | bytes 1179656 | tf_op jit(solution)/shard_map/ppermute | solution.py:414
  21.4 0.7 fusion.6
  22.2 0.7 add_select_fusion
  23.2 2.4 %collective-permute-start.6 = (bf16[256,768]{1,0:T(8,128)(2,1)}, bf16[256,768]{1,0:T(8,128)(2,1)S(1)}, u32[]{:S(2)}, u32[]{:S(2)}) collective-permute-start(bf16[256,768]{1,0:T(8,128)(2,1)} %get-tuple-element.64), channel_id=1, source_target_pairs={{0,16},{2,18},{4,20},{6,22},{8,24},{10,26},{12,28},{14,30},{16,0},... | collective-permute-start | bytes 1179656 | tf_op jit(solution)/shard_map/ppermute | solution.py:414
  25.7 2.1 %collective-permute-start.7 = (bf16[256,768]{1,0:T(8,128)(2,1)}, bf16[256,768]{1,0:T(8,128)(2,1)S(1)}, u32[]{:S(2)}, u32[]{:S(2)}) collective-permute-start(bf16[256,768]{1,0:T(8,128)(2,1)} %get-tuple-element.65), channel_id=1, source_target_pairs={{0,24},{2,26},{4,28},{6,30},{8,16},{10,18},{12,20},{14,22},{16,8},... | collective-permute-start | bytes 1179656 | tf_op jit(solution)/shard_map/ppermute | solution.py:414
  27.8 5.5 %all-to-all-done.ends_ref = f32[16,2,512]{2,1,0:T(2,128)S(1)} async-done(((f32[16,2,512]{2,1,0:T(2,128)}), f32[16,2,512]{2,1,0:T(2,128)S(1)}, u32[]{:S(2)}, u32[]{:S(2)}) %all-to-all-start) | async-done | bytes 65568 | tf_op jit(solution)/shard_map/all_to_all | solution.py:495
  33.3 0.6 copy-done.19
  33.9 2.7 %shard_map.146 = (bf16[256,512]{1,0:T(8,128)(2,1)}, f32[256,512]{1,0:T(8,128)}) custom-call(f32[256,512]{1,0:T(8,128)} %get-tuple-element.52.local_ref, f32[256,512]{1,0:T(8,128)} %get-tuple-element.53.through_ref, bf16[512,1024]{1,0:T(8,128)(2,1)} %mixer_ref.3, f32[16,2,512]{2,1,0:T(2,128)} %copy-done.19), custom_call_target="tpu_custom_call" | custom-call | flops 1 | bytes 1 | tf_op jit(solution)/shard_map/pallas_call | solution.py:498
  36.6 0.7 fusion.2.pick_ref
  37.3 0.6 broadcast_select_fusion.bias_ref
  37.9 0.8 collective-permute-done.3.other_ref
  38.7 0.8 copy-done.6
  39.5 2.9 %shard_map.147 = (bf16[256,512]{1,0:T(8,128)(2,1)}, bf16[16,32,512]{2,1,0:T(8,128)(2,1)}) custom-call(bf16[256,512]{1,0:T(8,128)(2,1)} %get-tuple-element.59.states_ref, bf16[512,1024]{1,0:T(8,128)(2,1)} %mixer_ref.3, f32[256,512]{1,0:T(8,128)} %copy-done.6, bf16[256,1024]{1,0:T(8,128)(2,1)} %bytes_ref.1, bf16[128,256]{1,0:T(8,128)(2,1)} %fusion.2.pick_ref), custom_call_target="tpu_custom_call" | custom-call | flops 1 | bytes 1 | tf_op jit(solution)/shard_map/pallas_call | solution.py:516
  42.4 5.0 %all-to-all-start.1 = ((bf16[16,32,512]{2,1,0:T(8,128)(2,1)}), bf16[16,32,512]{2,1,0:T(8,128)(2,1)S(1)}, u32[]{:S(2)}, u32[]{:S(2)}) async-start(bf16[16,32,512]{2,1,0:T(8,128)(2,1)} %get-tuple-element.61.gate_ref), calls=%async_computation.1 | async-start | bytes 1048576 | tf_op jit(solution)/shard_map/all_to_all | solution.py:527
  47.7 2.2 %shard_map.148 = (bf16[4,64,512]{2,1,0:T(8,128)(2,1)}, bf16[4,64,512]{2,1,0:T(8,128)(2,1)}, bf16[4,64,512]{2,1,0:T(8,128)(2,1)}, bf16[4,64,512]{2,1,0:T(8,128)(2,1)}) custom-call(bf16[16,32,512]{2,1,0:T(8,128)(2,1)} %get-tuple-element.61.gate_ref, bf16[64,2048]{1,0:T(8,128)(2,1)} %refs_0_.2, bf16[64,2048]{1,0:T(8,128)(2,1)} %copy-done.20, ...), custom_call_target="tpu_custom_call" | custom-call | flops 1 | bytes 1 | tf_op jit(solution)/shard_map/pallas_call | solution.py:528
  50.0 2.9 %collective-permute-start.10 = (bf16[4,64,512]{2,1,0:T(8,128)(2,1)}, bf16[4,64,512]{2,1,0:T(8,128)(2,1)S(1)}, u32[]{:S(2)}, u32[]{:S(2)}) collective-permute-start(bf16[4,64,512]{2,1,0:T(8,128)(2,1)} %get-tuple-element.73), channel_id=1, source_target_pairs={{0,6},{2,4},{4,2},{6,0},{8,14},{10,12},{12,10},{14,8},{16,22},{18,... | collective-permute-start | bytes 786440 | tf_op jit(solution)/shard_map/ppermute | solution.py:414
  52.8 0.6 collective-permute-start.8
  53.8 8.7 %collective-permute-done.6.refs_18_ = bf16[256,768]{1,0:T(8,128)(2,1)S(1)} collective-permute-done((bf16[256,768]{1,0:T(8,128)(2,1)}, bf16[256,768]{1,0:T(8,128)(2,1)S(1)}, u32[]{:S(2)}, u32[]{:S(2)}) %collective-permute-start.6) | collective-permute-done | bytes 393248 | tf_op jit(solution)/shard_map/ppermute | solution.py:414
  62.6 0.8 collective-permute-done.10.refs_11_
  63.3 5.0 %collective-permute-done.8.refs_9_ = bf16[4,64,512]{2,1,0:T(8,128)(2,1)S(1)} collective-permute-done((bf16[4,64,512]{2,1,0:T(8,128)(2,1)}, bf16[4,64,512]{2,1,0:T(8,128)(2,1)S(1)}, u32[]{:S(2)}, u32[]{:S(2)}) %collective-permute-start.8) | collective-permute-done | bytes 262176 | tf_op jit(solution)/shard_map/ppermute | solution.py:414
  68.3 7.7 %all-to-all-done.1.arrived_ref = bf16[16,32,512]{2,1,0:T(8,128)(2,1)S(1)} async-done(((bf16[16,32,512]{2,1,0:T(8,128)(2,1)}), bf16[16,32,512]{2,1,0:T(8,128)(2,1)S(1)}, u32[]{:S(2)}, u32[]{:S(2)}) %all-to-all-start.1) | async-done | bytes 524320 | tf_op jit(solution)/shard_map/all_to_all | solution.py:527
  76.0 0.5 collective-permute-start.12
  76.6 0.5 collective-permute-start.14
  77.1 0.8 fusion.pick_ref
  77.9 2.1 %shard_map.149.refs_0_ = bf16[256,512]{1,0:T(8,128)(2,1)} custom-call(bf16[256,512]{1,0:T(8,128)(2,1)} %fusion.pick_ref, bf16[16,32,512]{2,1,0:T(8,128)(2,1)} %copy-done.5), custom_call_target="tpu_custom_call" | custom-call | flops 1 | bytes 1 | tf_op jit(solution)/shard_map/pallas_call | solution.py:543
  80.1 0.6 collective-permute-start.15
  80.7 0.9 collective-permute-start.16
  81.6 2.0 %collective-permute-start.17 = (bf16[256,512]{1,0:T(8,128)(2,1)}, bf16[256,512]{1,0:T(8,128)(2,1)}, u32[]{:S(2)}, u32[]{:S(2)}) collective-permute-start(bf16[256,512]{1,0:T(8,128)(2,1)} %shard_map.149.refs_0_), channel_id=1, source_target_pairs={{0,6},{2,4},{4,2},{6,0},{8,14},{10,12},{12,10},{14,8},{16,22},{18,... | collective-permute-start | bytes 786440 | tf_op jit(solution)/shard_map/ppermute | solution.py:414
  83.6 5.9 %collective-permute-done.15.refs_1_ = bf16[256,512]{1,0:T(8,128)(2,1)S(1)} collective-permute-done((bf16[256,512]{1,0:T(8,128)(2,1)}, bf16[256,512]{1,0:T(8,128)(2,1)S(1)}, u32[]{:S(2)}, u32[]{:S(2)}) %collective-permute-start.15) | collective-permute-done | bytes 262176 | tf_op jit(solution)/shard_map/ppermute | solution.py:414
  90.0 4.6 %collective-permute-done.17.refs_3_ = bf16[256,512]{1,0:T(8,128)(2,1)} collective-permute-done((bf16[256,512]{1,0:T(8,128)(2,1)}, bf16[256,512]{1,0:T(8,128)(2,1)}, u32[]{:S(2)}, u32[]{:S(2)}) %collective-permute-start.17) | collective-permute-done | bytes 262176 | tf_op jit(solution)/shard_map/ppermute | solution.py:414
  94.6 0.7 reshape.255
  95.4 0.6 constant_dynamic-slice_fusion
  96.0 0.5 collective-permute-done.21.refs_7_
  96.6 10.3 %shard_map.150 = (bf16[1024,128]{1,0:T(8,128)(2,1)}, bf16[1024,128]{1,0:T(8,128)(2,1)}, bf16[1024,128]{1,0:T(8,128)(2,1)}, bf16[1024,128]{1,0:T(8,128)(2,1)}, bf...) custom-call(f32[1,1024]{1,0:T(1,128)} %broadcast_select_fusion.bias_ref,, ...), custom_call_target="tpu_custom_call" | custom-call | flops 1 | bytes 1 | tf_op jit(solution)/shard_map/pallas_call | solution.py:561
  106.9 1.7 %collective-permute-start.22 = (bf16[1024,128]{1,0:T(8,128)(2,1)}, bf16[1024,128]{1,0:T(8,128)(2,1)S(1)}, u32[]{:S(2)}, u32[]{:S(2)}) collective-permute-start(bf16[1024,128]{1,0:T(8,128)(2,1)} %get-tuple-element.89), channel_id=1, source_target_pairs={{0,2},{2,0},{4,6},{6,4},{8,10},{10,8},{12,14},{14,12},{16,18},{18,... | collective-permute-start | bytes 786440 | tf_op jit(solution)/shard_map/ppermute | solution.py:414
  109.0 1.1 collective-permute-start.26
  110.1 2.0 %collective-permute-start.27 = (bf16[528,128]{1,0:T(8,128)(2,1)}, bf16[528,128]{1,0:T(8,128)(2,1)S(1)}, u32[]{:S(2)}, u32[]{:S(2)}) collective-permute-start(bf16[528,128]{1,0:T(8,128)(2,1)} %get-tuple-element.95), channel_id=1, source_target_pairs={{0,6},{2,4},{4,2},{6,0},{8,14},{10,12},{12,10},{14,8},{16,22},{18,... | collective-permute-start | bytes 405512 | tf_op jit(solution)/shard_map/ppermute | solution.py:414
  112.2 0.9 collective-permute-start.23
  113.1 6.2 %collective-permute-done.25.refs_5_.refs_1_ = bf16[528,128]{1,0:T(8,128)(2,1)S(1)} collective-permute-done((bf16[528,128]{1,0:T(8,128)(2,1)}, bf16[528,128]{1,0:T(8,128)(2,1)S(1)}, u32[]{:S(2)}, u32[]{:S(2)}) %collective-permute-start.25) | collective-permute-done | bytes 135200 | tf_op jit(solution)/shard_map/ppermute | solution.py:414
  119.2 2.0 %collective-permute-start.24 = (bf16[1024,128]{1,0:T(8,128)(2,1)}, bf16[1024,128]{1,0:T(8,128)(2,1)S(1)}, u32[]{:S(2)}, u32[]{:S(2)}) collective-permute-start(bf16[1024,128]{1,0:T(8,128)(2,1)} %get-tuple-element.91), channel_id=1, source_target_pairs={{0,6},{2,4},{4,2},{6,0},{8,14},{10,12},{12,10},{14,8},{16,22},{18,... | collective-permute-start | bytes 786440 | tf_op jit(solution)/shard_map/ppermute | solution.py:414
  121.3 1.1 collective-permute-done.27.refs_7_.refs_3_
  122.4 0.9 copy-done.1
  123.7 1.4 collective-permute-start.28
  125.0 1.3 collective-permute-start.29
  126.4 0.9 collective-permute-start.30
  127.2 1.1 collective-permute-done.23.refs_2_
  128.3 1.2 collective-permute-done.24.refs_3_
  129.5 0.9 copy-done.2
  130.4 0.9 copy-done.4
  131.4 0.4 shard_map.151.query_ref
  131.8 2.3 %collective-permute-done.29.refs_2_ = bf16[512,128]{1,0:T(8,128)(2,1)S(1)} collective-permute-done((bf16[512,128]{1,0:T(8,128)(2,1)S(1)}, bf16[512,128]{1,0:T(8,128)(2,1)S(1)}, u32[]{:S(2)}, u32[]{:S(2)}) %collective-permute-start.29) | collective-permute-done | bytes 131104 | tf_op jit(solution)/shard_map/ppermute | solution.py:414
  134.1 3.7 %shard_map.153 = bf16[16,144,128]{2,1,0:T(8,128)(2,1)} custom-call(s32[16]{0:T(128)S(1)} %and_select_fusion.1.place_ref, bf16[1024,128]{1,0:T(8,128)(2,1)S(1)} %shard_map.151.query_ref, bf16[512,128]{1,0:T(8,128)(2,1)S(1)} %shard_map.152.refs_0_, bf16[512,128]{1,0:T(8,128)(2,1)S(1)} %collective-permute-done.28.refs_1_, ...), custom_call_target="tpu_custom_call" | custom-call | flops 1 | bytes 1 | tf_op jit(solution)/shard_map/pallas_call | solution.py:601
  137.7 5.9 %all-to-all-start.2 = ((bf16[16,144,128]{2,1,0:T(8,128)(2,1)}), bf16[16,144,128]{2,1,0:T(8,128)(2,1)S(1)}, u32[]{:S(2)}, u32[]{:S(2)}) async-start(bf16[16,144,128]{2,1,0:T(8,128)(2,1)} %shard_map.153), calls=%async_computation.2 | async-start | bytes 1179648 | tf_op jit(solution)/shard_map/all_to_all | solution.py:615
  145.7 0.6 iota_compare_fusion.6
  146.5 12.7 %all-to-all-done.2.pieces_ref = bf16[16,144,128]{2,1,0:T(8,128)(2,1)S(1)} async-done(((bf16[16,144,128]{2,1,0:T(8,128)(2,1)}), bf16[16,144,128]{2,1,0:T(8,128)(2,1)S(1)}, u32[]{:S(2)}, u32[]{:S(2)}) %all-to-all-start.2) | async-done | bytes 589856 | tf_op jit(solution)/shard_map/all_to_all | solution.py:615
  159.2 2.2 %copy-done = bf16[2048,1024]{1,0:T(8,128)(2,1)S(1)} copy-done((bf16[2048,1024]{1,0:T(8,128)(2,1)S(1)}, bf16[2048,1024]{1,0:T(8,128)(2,1)}, u32[]{:S(2)}) %copy-start) | copy-done | bytes 4194328
  161.3 0.8 shard_map.154
  162.4 1.4 collective-permute-done.31.other_ref
  163.8 0.9 shard_map.155
  (106 shorter events, 3.1 us)
Async XLA Ops:
  0.0 21.2 %copy-start.25 = (s32[16]{0:T(128)S(1)}, s32[16]{0:T(128)}, u32[]{:S(2)}) copy-start(s32[16]{0:T(128)} %param.22) | copy-start | bytes 196
  0.0 22.9 %copy-start.26 = (s32[1,128]{1,0:T(1,128)S(1)}, s32[1,128]{1,0:T(1,128)}, u32[]{:S(2)}) copy-start(s32[1,128]{1,0:T(1,128)} %param.21) | copy-start | bytes 1540
  0.0 23.2 %collective-permute-start = (bf16[64,2048]{1,0:T(8,128)(2,1)}, bf16[64,2048]{1,0:T(8,128)(2,1)S(1)}, u32[]{:S(2)}, u32[]{:S(2)}) collective-permute-start(bf16[64,2048]{1,0:T(8,128)(2,1)} %refs_0_.2), channel_id=1, source_target_pairs={{0,8},{2,10},{4,12},{6,14},{8,0},{10,2},{12,4},{14,6},{16,24},{18,... | collective-permute-start | bytes 786440 | tf_op jit(solution)/shard_map/ppermute | solution.py:414
  3.0 22.6 %collective-permute-start.1 = (bf16[64,2048]{1,0:T(8,128)(2,1)}, bf16[64,2048]{1,0:T(8,128)(2,1)S(1)}, u32[]{:S(2)}, u32[]{:S(2)}) collective-permute-start(bf16[64,2048]{1,0:T(8,128)(2,1)} %refs_0_.2), channel_id=1, source_target_pairs={{0,16},{2,18},{4,20},{6,22},{8,24},{10,26},{12,28},{14,30},{16,0},... | collective-permute-start | bytes 786440 | tf_op jit(solution)/shard_map/ppermute | solution.py:414
  5.6 27.7 %collective-permute-start.2 = (bf16[64,2048]{1,0:T(8,128)(2,1)}, bf16[64,2048]{1,0:T(8,128)(2,1)S(1)}, u32[]{:S(2)}, u32[]{:S(2)}) collective-permute-start(bf16[64,2048]{1,0:T(8,128)(2,1)} %refs_0_.2), channel_id=1, source_target_pairs={{0,24},{2,26},{4,28},{6,30},{8,16},{10,18},{12,20},{14,22},{16,8},... | collective-permute-start | bytes 786440 | tf_op jit(solution)/shard_map/ppermute | solution.py:414
  6.3 31.0 %collective-permute-start.4 = (f32[1,512]{1,0:T(1,128)S(1)}, f32[1,512]{1,0:T(1,128)S(1)}, u32[]{:S(2)}, u32[]{:S(2)}) collective-permute-start(f32[1,512]{1,0:T(1,128)S(1)} %bitcast.9), channel_id=1, source_target_pairs={{0,1},{1,0},{2,3},{3,2},{4,5},{5,4},{6,7},{7,6},{8,9},{9,8},{10,11... | collective-permute-start | bytes 6152 | tf_op jit(solution)/shard_map/ppermute | solution.py:23
  12.1 21.1 %all-to-all-start = ((f32[16,2,512]{2,1,0:T(2,128)}), f32[16,2,512]{2,1,0:T(2,128)S(1)}, u32[]{:S(2)}, u32[]{:S(2)}) async-start(f32[16,2,512]{2,1,0:T(2,128)} %get-tuple-element.54), calls=%async_computation | async-start | bytes 131072 | tf_op jit(solution)/shard_map/all_to_all | solution.py:495
  19.2 18.7 %collective-permute-start.5 = (bf16[256,768]{1,0:T(8,128)(2,1)}, bf16[256,768]{1,0:T(8,128)(2,1)S(1)}, u32[]{:S(2)}, u32[]{:S(2)}) collective-permute-start(bf16[256,768]{1,0:T(8,128)(2,1)} %get-tuple-element.57), channel_id=1, source_target_pairs={{0,8},{2,10},{4,12},{6,14},{8,0},{10,2},{12,4},{14,6},{16,24},{18,... | collective-permute-start | bytes 1179656 | tf_op jit(solution)/shard_map/ppermute | solution.py:414
  22.2 31.4 %copy-start.23 = (s32[16]{0:T(128)}, s32[16]{0:T(128)S(1)}, u32[]{:S(2)}) copy-start(s32[16]{0:T(128)S(1)} %get-tuple-element.100) | copy-start | bytes 196
  23.2 24.5 %copy-start.20 = (bf16[64,2048]{1,0:T(8,128)(2,1)}, bf16[64,2048]{1,0:T(8,128)(2,1)S(1)}, u32[]{:S(2)}) copy-start(bf16[64,2048]{1,0:T(8,128)(2,1)S(1)} %collective-permute-done.refs_1_) | copy-start | bytes 786436
  23.2 39.3 %collective-permute-start.6 = (bf16[256,768]{1,0:T(8,128)(2,1)}, bf16[256,768]{1,0:T(8,128)(2,1)S(1)}, u32[]{:S(2)}, u32[]{:S(2)}) collective-permute-start(bf16[256,768]{1,0:T(8,128)(2,1)} %get-tuple-element.64), channel_id=1, source_target_pairs={{0,16},{2,18},{4,20},{6,22},{8,24},{10,26},{12,28},{14,30},{16,0},... | collective-permute-start | bytes 1179656 | tf_op jit(solution)/shard_map/ppermute | solution.py:414
  25.7 22.1 %copy-start.21 = (bf16[64,2048]{1,0:T(8,128)(2,1)}, bf16[64,2048]{1,0:T(8,128)(2,1)S(1)}, u32[]{:S(2)}) copy-start(bf16[64,2048]{1,0:T(8,128)(2,1)S(1)} %collective-permute-done.1.refs_2_) | copy-start | bytes 786436
  25.7 36.9 %collective-permute-start.7 = (bf16[256,768]{1,0:T(8,128)(2,1)}, bf16[256,768]{1,0:T(8,128)(2,1)S(1)}, u32[]{:S(2)}, u32[]{:S(2)}) collective-permute-start(bf16[256,768]{1,0:T(8,128)(2,1)} %get-tuple-element.65), channel_id=1, source_target_pairs={{0,24},{2,26},{4,28},{6,30},{8,16},{10,18},{12,20},{14,22},{16,8},... | collective-permute-start | bytes 1179656 | tf_op jit(solution)/shard_map/ppermute | solution.py:414
  33.3 0.6 copy-start.19
  33.3 14.4 %copy-start.22 = (bf16[64,2048]{1,0:T(8,128)(2,1)}, bf16[64,2048]{1,0:T(8,128)(2,1)S(1)}, u32[]{:S(2)}) copy-start(bf16[64,2048]{1,0:T(8,128)(2,1)S(1)} %collective-permute-done.2.refs_3_) | copy-start | bytes 786436
  36.6 2.1 %collective-permute-start.3 = (f32[256,512]{1,0:T(8,128)}, f32[256,512]{1,0:T(8,128)S(1)}, u32[]{:S(2)}, u32[]{:S(2)}) collective-permute-start(f32[256,512]{1,0:T(8,128)} %get-tuple-element.56), channel_id=1, source_target_pairs={{0,1},{1,0},{2,3},{3,2},{4,5},{5,4},{6,7},{7,6},{8,9},{9,8},{10,11... | collective-permute-start | bytes 1572872 | tf_op jit(solution)/shard_map/ppermute | solution.py:23
  37.9 58.6 %copy-start.7 = (bf16[256,768]{1,0:T(8,128)(2,1)}, bf16[256,768]{1,0:T(8,128)(2,1)S(1)}, u32[]{:S(2)}) copy-start(bf16[256,768]{1,0:T(8,128)(2,1)S(1)} %collective-permute-done.5.refs_17_) | copy-start | bytes 1179652
  38.7 0.8 copy-start.6
  42.4 33.6 %all-to-all-start.1 = ((bf16[16,32,512]{2,1,0:T(8,128)(2,1)}), bf16[16,32,512]{2,1,0:T(8,128)(2,1)S(1)}, u32[]{:S(2)}, u32[]{:S(2)}) async-start(bf16[16,32,512]{2,1,0:T(8,128)(2,1)} %get-tuple-element.61.gate_ref), calls=%async_computation.1 | async-start | bytes 1048576 | tf_op jit(solution)/shard_map/all_to_all | solution.py:527
  50.0 13.4 %collective-permute-start.10 = (bf16[4,64,512]{2,1,0:T(8,128)(2,1)}, bf16[4,64,512]{2,1,0:T(8,128)(2,1)S(1)}, u32[]{:S(2)}, u32[]{:S(2)}) collective-permute-start(bf16[4,64,512]{2,1,0:T(8,128)(2,1)} %get-tuple-element.73), channel_id=1, source_target_pairs={{0,6},{2,4},{4,2},{6,0},{8,14},{10,12},{12,10},{14,8},{16,22},{18,... | collective-permute-start | bytes 786440 | tf_op jit(solution)/shard_map/ppermute | solution.py:414
  52.8 15.5 %collective-permute-start.8 = (bf16[4,64,512]{2,1,0:T(8,128)(2,1)}, bf16[4,64,512]{2,1,0:T(8,128)(2,1)S(1)}, u32[]{:S(2)}, u32[]{:S(2)}) collective-permute-start(bf16[4,64,512]{2,1,0:T(8,128)(2,1)} %get-tuple-element.71), channel_id=1, source_target_pairs={{0,2},{2,0},{4,6},{6,4},{8,10},{10,8},{12,14},{14,12},{16,18},{18,... | collective-permute-start | bytes 786440 | tf_op jit(solution)/shard_map/ppermute | solution.py:414
  53.4 14.9 %collective-permute-start.9 = (bf16[4,64,512]{2,1,0:T(8,128)(2,1)}, bf16[4,64,512]{2,1,0:T(8,128)(2,1)S(1)}, u32[]{:S(2)}, u32[]{:S(2)}) collective-permute-start(bf16[4,64,512]{2,1,0:T(8,128)(2,1)} %get-tuple-element.72), channel_id=1, source_target_pairs={{0,4},{2,6},{4,0},{6,2},{8,12},{10,14},{12,8},{14,10},{16,20},{18,... | collective-permute-start | bytes 786440 | tf_op jit(solution)/shard_map/ppermute | solution.py:414
  62.6 34.0 %copy-start.8 = (bf16[256,768]{1,0:T(8,128)(2,1)}, bf16[256,768]{1,0:T(8,128)(2,1)S(1)}, u32[]{:S(2)}) copy-start(bf16[256,768]{1,0:T(8,128)(2,1)S(1)} %collective-permute-done.6.refs_18_) | copy-start | bytes 1179652
  62.6 34.0 %copy-start.9 = (bf16[256,768]{1,0:T(8,128)(2,1)}, bf16[256,768]{1,0:T(8,128)(2,1)S(1)}, u32[]{:S(2)}) copy-start(bf16[256,768]{1,0:T(8,128)(2,1)S(1)} %collective-permute-done.7.refs_19_) | copy-start | bytes 1179652
  63.3 33.2 %copy-start.10 = (bf16[4,64,512]{2,1,0:T(8,128)(2,1)}, bf16[4,64,512]{2,1,0:T(8,128)(2,1)S(1)}, u32[]{:S(2)}) copy-start(bf16[4,64,512]{2,1,0:T(8,128)(2,1)S(1)} %collective-permute-done.10.refs_11_) | copy-start | bytes 786436
  68.3 28.2 %copy-start.11 = (bf16[4,64,512]{2,1,0:T(8,128)(2,1)}, bf16[4,64,512]{2,1,0:T(8,128)(2,1)S(1)}, u32[]{:S(2)}) copy-start(bf16[4,64,512]{2,1,0:T(8,128)(2,1)S(1)} %collective-permute-done.8.refs_9_) | copy-start | bytes 786436
  68.3 28.2 %copy-start.12 = (bf16[4,64,512]{2,1,0:T(8,128)(2,1)}, bf16[4,64,512]{2,1,0:T(8,128)(2,1)S(1)}, u32[]{:S(2)}) copy-start(bf16[4,64,512]{2,1,0:T(8,128)(2,1)S(1)} %collective-permute-done.9.refs_10_) | copy-start | bytes 786436
  76.0 1.9 %copy-start.5 = (bf16[16,32,512]{2,1,0:T(8,128)(2,1)}, bf16[16,32,512]{2,1,0:T(8,128)(2,1)S(1)}, u32[]{:S(2)}) copy-start(bf16[16,32,512]{2,1,0:T(8,128)(2,1)S(1)} %all-to-all-done.1.arrived_ref) | copy-start | bytes 1572868
  76.0 4.0 %collective-permute-start.11 = (bf16[4,64,512]{2,1,0:T(8,128)(2,1)}, bf16[4,64,512]{2,1,0:T(8,128)(2,1)S(1)}, u32[]{:S(2)}, u32[]{:S(2)}) collective-permute-start(bf16[4,64,512]{2,1,0:T(8,128)(2,1)} %get-tuple-element.75.refs_8_), channel_id=1, source_target_pairs={{0,1},{1,0},{2,3},{3,2},{4,5},{5,4},{6,7},{7,6},{8,9},{9,8},{10,11... | collective-permute-start | bytes 786440 | tf_op jit(solution)/shard_map/ppermute | solution.py:23
  76.0 4.0 %collective-permute-start.12 = (bf16[4,64,512]{2,1,0:T(8,128)(2,1)S(1)}, bf16[4,64,512]{2,1,0:T(8,128)(2,1)S(1)}, u32[]{:S(2)}, u32[]{:S(2)}) collective-permute-start(bf16[4,64,512]{2,1,0:T(8,128)(2,1)S(1)} %collective-permute-done.8.refs_9_), channel_id=1, source_target_pairs={{0,1},{1,0},{2,3},{3,2},{4,5},{5,4},{6,7},{7,6},{8,9},{9,8},{10,11... | collective-permute-start | bytes 786440 | tf_op jit(solution)/shard_map/ppermute | solution.py:23
  76.6 3.5 %collective-permute-start.13 = (bf16[4,64,512]{2,1,0:T(8,128)(2,1)S(1)}, bf16[4,64,512]{2,1,0:T(8,128)(2,1)S(1)}, u32[]{:S(2)}, u32[]{:S(2)}) collective-permute-start(bf16[4,64,512]{2,1,0:T(8,128)(2,1)S(1)} %collective-permute-done.9.refs_10_), channel_id=1, source_target_pairs={{0,1},{1,0},{2,3},{3,2},{4,5},{5,4},{6,7},{7,6},{8,9},{9,8},{10,11... | collective-permute-start | bytes 786440 | tf_op jit(solution)/shard_map/ppermute | solution.py:23
  76.6 3.5 %collective-permute-start.14 = (bf16[4,64,512]{2,1,0:T(8,128)(2,1)S(1)}, bf16[4,64,512]{2,1,0:T(8,128)(2,1)S(1)}, u32[]{:S(2)}, u32[]{:S(2)}) collective-permute-start(bf16[4,64,512]{2,1,0:T(8,128)(2,1)S(1)} %collective-permute-done.10.refs_11_), channel_id=1, source_target_pairs={{0,1},{1,0},{2,3},{3,2},{4,5},{5,4},{6,7},{7,6},{8,9},{9,8},{10,11... | collective-permute-start | bytes 786440 | tf_op jit(solution)/shard_map/ppermute | solution.py:23
  80.0 16.5 %copy-start.13 = (bf16[4,64,512]{2,1,0:T(8,128)(2,1)}, bf16[4,64,512]{2,1,0:T(8,128)(2,1)S(1)}, u32[]{:S(2)}) copy-start(bf16[4,64,512]{2,1,0:T(8,128)(2,1)S(1)} %collective-permute-done.11.refs_12_) | copy-start | bytes 786436
  80.0 16.5 %copy-start.14 = (bf16[4,64,512]{2,1,0:T(8,128)(2,1)}, bf16[4,64,512]{2,1,0:T(8,128)(2,1)S(1)}, u32[]{:S(2)}) copy-start(bf16[4,64,512]{2,1,0:T(8,128)(2,1)S(1)} %collective-permute-done.12.refs_13_) | copy-start | bytes 786436
  80.0 16.5 %copy-start.15 = (bf16[4,64,512]{2,1,0:T(8,128)(2,1)}, bf16[4,64,512]{2,1,0:T(8,128)(2,1)S(1)}, u32[]{:S(2)}) copy-start(bf16[4,64,512]{2,1,0:T(8,128)(2,1)S(1)} %collective-permute-done.13.refs_14_) | copy-start | bytes 786436
  80.1 16.5 %copy-start.16 = (bf16[4,64,512]{2,1,0:T(8,128)(2,1)}, bf16[4,64,512]{2,1,0:T(8,128)(2,1)S(1)}, u32[]{:S(2)}) copy-start(bf16[4,64,512]{2,1,0:T(8,128)(2,1)S(1)} %collective-permute-done.14.refs_15_) | copy-start | bytes 786436
  80.1 9.5 %collective-permute-start.15 = (bf16[256,512]{1,0:T(8,128)(2,1)}, bf16[256,512]{1,0:T(8,128)(2,1)S(1)}, u32[]{:S(2)}, u32[]{:S(2)}) collective-permute-start(bf16[256,512]{1,0:T(8,128)(2,1)} %shard_map.149.refs_0_), channel_id=1, source_target_pairs={{0,2},{2,0},{4,6},{6,4},{8,10},{10,8},{12,14},{14,12},{16,18},{18,... | collective-permute-start | bytes 786440 | tf_op jit(solution)/shard_map/ppermute | solution.py:414
  80.7 9.0 %collective-permute-start.16 = (bf16[256,512]{1,0:T(8,128)(2,1)}, bf16[256,512]{1,0:T(8,128)(2,1)S(1)}, u32[]{:S(2)}, u32[]{:S(2)}) collective-permute-start(bf16[256,512]{1,0:T(8,128)(2,1)} %shard_map.149.refs_0_), channel_id=1, source_target_pairs={{0,4},{2,6},{4,0},{6,2},{8,12},{10,14},{12,8},{14,10},{16,20},{18,... | collective-permute-start | bytes 786440 | tf_op jit(solution)/shard_map/ppermute | solution.py:414
  81.6 13.0 %collective-permute-start.17 = (bf16[256,512]{1,0:T(8,128)(2,1)}, bf16[256,512]{1,0:T(8,128)(2,1)}, u32[]{:S(2)}, u32[]{:S(2)}) collective-permute-start(bf16[256,512]{1,0:T(8,128)(2,1)} %shard_map.149.refs_0_), channel_id=1, source_target_pairs={{0,6},{2,4},{4,2},{6,0},{8,14},{10,12},{12,10},{14,8},{16,22},{18,... | collective-permute-start | bytes 786440 | tf_op jit(solution)/shard_map/ppermute | solution.py:414
  83.6 12.4 %collective-permute-start.18 = (bf16[256,512]{1,0:T(8,128)(2,1)}, bf16[256,512]{1,0:T(8,128)(2,1)}, u32[]{:S(2)}, u32[]{:S(2)}) collective-permute-start(bf16[256,512]{1,0:T(8,128)(2,1)} %shard_map.149.refs_0_), channel_id=1, source_target_pairs={{0,1},{1,0},{2,3},{3,2},{4,5},{5,4},{6,7},{7,6},{8,9},{9,8},{10,11... | collective-permute-start | bytes 786440 | tf_op jit(solution)/shard_map/ppermute | solution.py:23
  89.5 7.1 %copy-start.17 = (bf16[256,512]{1,0:T(8,128)(2,1)}, bf16[256,512]{1,0:T(8,128)(2,1)S(1)}, u32[]{:S(2)}) copy-start(bf16[256,512]{1,0:T(8,128)(2,1)S(1)} %collective-permute-done.15.refs_1_) | copy-start | bytes 786436
  89.5 6.5 %collective-permute-start.19 = (bf16[256,512]{1,0:T(8,128)(2,1)S(1)}, bf16[256,512]{1,0:T(8,128)(2,1)}, u32[]{:S(2)}, u32[]{:S(2)}) collective-permute-start(bf16[256,512]{1,0:T(8,128)(2,1)S(1)} %collective-permute-done.15.refs_1_), channel_id=1, source_target_pairs={{0,1},{1,0},{2,3},{3,2},{4,5},{5,4},{6,7},{7,6},{8,9},{9,8},{10,11... | collective-permute-start | bytes 786440 | tf_op jit(solution)/shard_map/ppermute | solution.py:23
  89.7 6.9 %copy-start.18 = (bf16[256,512]{1,0:T(8,128)(2,1)}, bf16[256,512]{1,0:T(8,128)(2,1)S(1)}, u32[]{:S(2)}) copy-start(bf16[256,512]{1,0:T(8,128)(2,1)S(1)} %collective-permute-done.16.refs_2_) | copy-start | bytes 786436
  89.7 6.3 %collective-permute-start.20 = (bf16[256,512]{1,0:T(8,128)(2,1)S(1)}, bf16[256,512]{1,0:T(8,128)(2,1)}, u32[]{:S(2)}, u32[]{:S(2)}) collective-permute-start(bf16[256,512]{1,0:T(8,128)(2,1)S(1)} %collective-permute-done.16.refs_2_), channel_id=1, source_target_pairs={{0,1},{1,0},{2,3},{3,2},{4,5},{5,4},{6,7},{7,6},{8,9},{9,8},{10,11... | collective-permute-start | bytes 786440 | tf_op jit(solution)/shard_map/ppermute | solution.py:23
  94.6 1.9 %collective-permute-start.21 = (bf16[256,512]{1,0:T(8,128)(2,1)}, bf16[256,512]{1,0:T(8,128)(2,1)}, u32[]{:S(2)}, u32[]{:S(2)}) collective-permute-start(bf16[256,512]{1,0:T(8,128)(2,1)} %collective-permute-done.17.refs_3_), channel_id=1, source_target_pairs={{0,1},{1,0},{2,3},{3,2},{4,5},{5,4},{6,7},{7,6},{8,9},{9,8},{10,11... | collective-permute-start | bytes 786440 | tf_op jit(solution)/shard_map/ppermute | solution.py:23
  95.4 31.9 %copy-start.24 = (s32[16]{0:T(128)S(1)}, s32[16]{0:T(128)}, u32[]{:S(2)}) copy-start(s32[16]{0:T(128)} %copy-done.23) | copy-start | bytes 196
  96.6 49.7 %copy-start.27 = (s32[1,128]{1,0:T(1,128)S(1)}, s32[1,128]{1,0:T(1,128)}, u32[]{:S(2)}) copy-start(s32[1,128]{1,0:T(1,128)} %param.21) | copy-start | bytes 1540
  106.9 19.5 %collective-permute-start.22 = (bf16[1024,128]{1,0:T(8,128)(2,1)}, bf16[1024,128]{1,0:T(8,128)(2,1)S(1)}, u32[]{:S(2)}, u32[]{:S(2)}) collective-permute-start(bf16[1024,128]{1,0:T(8,128)(2,1)} %get-tuple-element.89), channel_id=1, source_target_pairs={{0,2},{2,0},{4,6},{6,4},{8,10},{10,8},{12,14},{14,12},{16,18},{18,... | collective-permute-start | bytes 786440 | tf_op jit(solution)/shard_map/ppermute | solution.py:414
  108.7 10.6 %collective-permute-start.25 = (bf16[528,128]{1,0:T(8,128)(2,1)}, bf16[528,128]{1,0:T(8,128)(2,1)S(1)}, u32[]{:S(2)}, u32[]{:S(2)}) collective-permute-start(bf16[528,128]{1,0:T(8,128)(2,1)} %get-tuple-element.93), channel_id=1, source_target_pairs={{0,2},{2,0},{4,6},{6,4},{8,10},{10,8},{12,14},{14,12},{16,18},{18,... | collective-permute-start | bytes 405512 | tf_op jit(solution)/shard_map/ppermute | solution.py:414
  109.0 12.2 %collective-permute-start.26 = (bf16[528,128]{1,0:T(8,128)(2,1)}, bf16[528,128]{1,0:T(8,128)(2,1)S(1)}, u32[]{:S(2)}, u32[]{:S(2)}) collective-permute-start(bf16[528,128]{1,0:T(8,128)(2,1)} %get-tuple-element.94), channel_id=1, source_target_pairs={{0,4},{2,6},{4,0},{6,2},{8,12},{10,14},{12,8},{14,10},{16,20},{18,... | collective-permute-start | bytes 405512 | tf_op jit(solution)/shard_map/ppermute | solution.py:414
  110.1 12.2 %collective-permute-start.27 = (bf16[528,128]{1,0:T(8,128)(2,1)}, bf16[528,128]{1,0:T(8,128)(2,1)S(1)}, u32[]{:S(2)}, u32[]{:S(2)}) collective-permute-start(bf16[528,128]{1,0:T(8,128)(2,1)} %get-tuple-element.95), channel_id=1, source_target_pairs={{0,6},{2,4},{4,2},{6,0},{8,14},{10,12},{12,10},{14,8},{16,22},{18,... | collective-permute-start | bytes 405512 | tf_op jit(solution)/shard_map/ppermute | solution.py:414
  112.2 16.1 %collective-permute-start.23 = (bf16[1024,128]{1,0:T(8,128)(2,1)}, bf16[1024,128]{1,0:T(8,128)(2,1)S(1)}, u32[]{:S(2)}, u32[]{:S(2)}) collective-permute-start(bf16[1024,128]{1,0:T(8,128)(2,1)} %get-tuple-element.90), channel_id=1, source_target_pairs={{0,4},{2,6},{4,0},{6,2},{8,12},{10,14},{12,8},{14,10},{16,20},{18,... | collective-permute-start | bytes 786440 | tf_op jit(solution)/shard_map/ppermute | solution.py:414
  119.2 10.2 %collective-permute-start.24 = (bf16[1024,128]{1,0:T(8,128)(2,1)}, bf16[1024,128]{1,0:T(8,128)(2,1)S(1)}, u32[]{:S(2)}, u32[]{:S(2)}) collective-permute-start(bf16[1024,128]{1,0:T(8,128)(2,1)} %get-tuple-element.91), channel_id=1, source_target_pairs={{0,6},{2,4},{4,2},{6,0},{8,14},{10,12},{12,10},{14,8},{16,22},{18,... | collective-permute-start | bytes 786440 | tf_op jit(solution)/shard_map/ppermute | solution.py:414
  122.4 0.9 copy-start.1
  123.7 8.1 %collective-permute-start.28 = (bf16[512,128]{1,0:T(8,128)(2,1)S(1)}, bf16[512,128]{1,0:T(8,128)(2,1)S(1)}, u32[]{:S(2)}, u32[]{:S(2)}) collective-permute-start(bf16[512,128]{1,0:T(8,128)(2,1)S(1)} %shard_map.152.refs_0_), channel_id=1, source_target_pairs={{0,2},{2,0},{4,6},{6,4},{8,10},{10,8},{12,14},{14,12},{16,18},{18,... | collective-permute-start | bytes 393224 | tf_op jit(solution)/shard_map/ppermute | solution.py:414
  125.0 9.0 %collective-permute-start.29 = (bf16[512,128]{1,0:T(8,128)(2,1)S(1)}, bf16[512,128]{1,0:T(8,128)(2,1)S(1)}, u32[]{:S(2)}, u32[]{:S(2)}) collective-permute-start(bf16[512,128]{1,0:T(8,128)(2,1)S(1)} %shard_map.152.refs_0_), channel_id=1, source_target_pairs={{0,4},{2,6},{4,0},{6,2},{8,12},{10,14},{12,8},{14,10},{16,20},{18,... | collective-permute-start | bytes 393224 | tf_op jit(solution)/shard_map/ppermute | solution.py:414
  126.4 7.7 %collective-permute-start.30 = (bf16[512,128]{1,0:T(8,128)(2,1)S(1)}, bf16[512,128]{1,0:T(8,128)(2,1)S(1)}, u32[]{:S(2)}, u32[]{:S(2)}) collective-permute-start(bf16[512,128]{1,0:T(8,128)(2,1)S(1)} %shard_map.152.refs_0_), channel_id=1, source_target_pairs={{0,6},{2,4},{4,2},{6,0},{8,14},{10,12},{12,10},{14,8},{16,22},{18,... | collective-permute-start | bytes 393224 | tf_op jit(solution)/shard_map/ppermute | solution.py:414
  129.5 0.9 copy-start.2
  130.4 0.9 copy-start.4
  131.8 32.1 %copy-start.3 = (bf16[256,512]{1,0:T(8,128)(2,1)S(1)}, bf16[256,512]{1,0:T(8,128)(2,1)}, u32[]{:S(2)}) copy-start(bf16[256,512]{1,0:T(8,128)(2,1)} %get-tuple-element.98.encoded_ref) | copy-start | bytes 786436
  137.7 21.4 %all-to-all-start.2 = ((bf16[16,144,128]{2,1,0:T(8,128)(2,1)}), bf16[16,144,128]{2,1,0:T(8,128)(2,1)S(1)}, u32[]{:S(2)}, u32[]{:S(2)}) async-start(bf16[16,144,128]{2,1,0:T(8,128)(2,1)} %shard_map.153), calls=%async_computation.2 | async-start | bytes 1179648 | tf_op jit(solution)/shard_map/all_to_all | solution.py:615
  159.2 2.2 %copy-start = (bf16[2048,1024]{1,0:T(8,128)(2,1)S(1)}, bf16[2048,1024]{1,0:T(8,128)(2,1)}, u32[]{:S(2)}) copy-start(bf16[2048,1024]{1,0:T(8,128)(2,1)} %weight_ref.1) | copy-start | bytes 12582916
  162.2 1.6 %collective-permute-start.31 = (f32[144,512]{1,0:T(8,128)S(1)}, f32[144,512]{1,0:T(8,128)S(1)}, u32[]{:S(2)}, u32[]{:S(2)}) collective-permute-start(f32[144,512]{1,0:T(8,128)S(1)} %get-tuple-element.97), channel_id=1, source_target_pairs={{0,1},{1,0},{2,3},{3,2},{4,5},{5,4},{6,7},{7,6},{8,9},{9,8},{10,11... | collective-permute-start | bytes 884744 | tf_op jit(solution)/shard_map/ppermute | solution.py:23

commit v3 on v2

--- a/solution.py
+++ b/solution.py
@@ -456,7 +456,13 @@
     spread = (jnp.arange(window, dtype=jnp.int32)[None, :] == result_row[:, None]).astype(bf16)
 
     up_half = inner_half // plane
-    up_layers = [up_weight] + [over(up_weight, plane * step) for step in range(1, layers)]
+    up_layers = [up_weight]
+    for bit in range(layers.bit_length() - 2, -1, -1):
+        up_layers += [over(piece, plane << bit) for piece in up_layers]
+    order = [0]
+    for bit in range(layers.bit_length() - 2, -1, -1):
+        order += [step ^ (1 << bit) for step in order]
+    up_layers = [up_layers[order.index(step)] for step in range(layers)]
 
     local, through, ends, *pair_cuts = pl.pallas_call(
         functools.partial(scan_kernel, plane, layers),
@@ -493,7 +499,9 @@
         value_weight,
     )
     ends = lax.all_to_all(ends, "seq", 0, 0, tiled=True)
-    ends, up_layers = lax.optimization_barrier((ends, up_layers))
+    ends, up_layers[1], up_layers[2] = lax.optimization_barrier(
+        (ends, up_layers[1], up_layers[2])
+    )
     pieces = [pair_cuts[0]] + [over(pair_cuts[step], plane * step) for step in range(1, layers)]
     states, other_part = pl.pallas_call(
         states_kernel,
@@ -512,7 +520,9 @@
         jnp.concatenate([own_bias, far_bias], axis=1),
         jnp.concatenate([far_bias, own_bias], axis=1),
     )
-    far_part, bias, pieces[1] = lax.optimization_barrier((swapped(other_part), bias, pieces[1]))
+    far_part, bias, own_gain, near_pick, pieces[1], up_layers[3] = lax.optimization_barrier(
+        (swapped(other_part), bias, own_gain, near_pick, pieces[1], up_layers[3])
+    )
     encoded, leaving = pl.pallas_call(
         functools.partial(pool_kernel, plane),
         out_shape=(

time: 166 us -> 179 us (1.078)
  waiting for transfers between devices: 65.6 us -> 79.3 us
    ppermute x21, waiting for transfers between devices: 36.9 us -> 61.2 us  [over(): return lax.ppermute(value, 'seq', [(i, i ^ mask) for i in range(shards)])]
    all_to_all x1, waiting for transfers between devices: 7.72 us -> 0.01 us  [one_head_each(): arrived = lax.all_to_all(leaving, 'seq', 0, 0, tiled=True)]
    all_to_all x1, starting transfers between devices: 5.88 us -> 10.2 us  [one_head_each(): pieces = lax.all_to_all(leaving, 'seq', 0, 0, tiled=True)]
    all_to_all x1, starting transfers between devices: 7.1 us -> 3.97 us  [one_head_each(): ends = lax.all_to_all(ends, 'seq', 0, 0, tiled=True)]
    all_to_all x1, waiting for transfers between devices: 5.49 us -> 2.55 us  [one_head_each(): ends = lax.all_to_all(ends, 'seq', 0, 0, tiled=True)]
    unnamed x56 -> x66, local copies, waits for them, and re-layouts: 6.47 us -> 7.38 us
  transfers between devices with their start and end apart: 35 -> 35, of which waited for: 17 -> 14; matrix products, arithmetic and copies ran while one was open for 5% -> 4% of each run, Pallas kernels for 10% -> 8%
where the time goes in v3:
time: 179 us; the launch traced here: 178 us
  waiting for transfers between devices  79.3 us (44%)
  starting transfers between devices  50.2 us (28%)
  Pallas kernels  32.2 us (18%)
  local copies, waits for them, and re-layouts  9.04 us (5%)
  other arithmetic  5.19 us (3%)
  between operations  2.52 us (1%)
    ppermute x21, waiting for transfers between devices, over(): return lax.ppermute(value, 'seq', [(i, i ^ mask) for i in range(shards)])  61.2 us
    ppermute x21, starting transfers between devices, over(): return lax.ppermute(value, 'seq', [(i, i ^ mask) for i in range(shards)])  30.5 us
    all_to_all x1, waiting for transfers between devices, one_head_each(): pieces = lax.all_to_all(leaving, 'seq', 0, 0, tiled=True)  12.7 us
    pallas_call x1, Pallas kernels, one_head_each(): pl.pallas_call(functools.partial(inner_kernel, plane, layers), out_shape=...  10.2 us
    all_to_all x1, starting transfers between devices, one_head_each(): pieces = lax.all_to_all(leaving, 'seq', 0, 0, tiled=True)  10.2 us
    unnamed x66, local copies, waits for them, and re-layouts  7.38 us
    pallas_call x1, Pallas kernels, one_head_each(): pl.pallas_call(functools.partial(scan_kernel, plane, layers), out_shape=(...  5.75 us
    all_to_all x1, starting transfers between devices, one_head_each(): ends = lax.all_to_all(ends, 'seq', 0, 0, tiled=True)  3.97 us
  transfers between devices with their start and end apart: 35, of which 14 were waited for; matrix products, arithmetic and copies ran while one was open for 4% of the time, Pallas kernels for 8%

profile of v3, /device:TPU:0, one launch (start us, length us, event | category | flops | bytes accessed | tf_op | source)
XLA Modules:
  0.0 178.4 jit_solution(14214076527319832372)
XLA Ops:
  0.0 4.1 %collective-permute-start.1 = (bf16[64,2048]{1,0:T(8,128)(2,1)}, bf16[64,2048]{1,0:T(8,128)(2,1)S(1)}, u32[]{:S(2)}, u32[]{:S(2)}) collective-permute-start(bf16[64,2048]{1,0:T(8,128)(2,1)} %refs_0_.3), channel_id=1, source_target_pairs={{0,16},{2,18},{4,20},{6,22},{8,24},{10,26},{12,28},{14,30},{16,0},... | collective-permute-start | bytes 786440 | tf_op jit(solution)/shard_map/ppermute | solution.py:414
  4.1 1.6 collective-permute-start
  5.7 0.7 reshape.254
  6.5 5.8 %shard_map.145 = (f32[256,512]{1,0:T(8,128)}, f32[256,512]{1,0:T(8,128)}, f32[16,2,512]{2,1,0:T(2,128)}, bf16[256,768]{1,0:T(8,128)(2,1)}, bf16[256,768]{1,0:T(8...) custom-call(bf16[256,1024]{1,0:T(8,128)(2,1)} %bytes_ref.1, f32[1,1024]{1,0:T(1,128)} %bitcast.11, ...), custom_call_target="tpu_custom_call" | custom-call | flops 1 | bytes 1 | tf_op jit(solution)/shard_map/pallas_call | solution.py:467
  12.3 4.0 %all-to-all-start = ((f32[16,2,512]{2,1,0:T(2,128)}), f32[16,2,512]{2,1,0:T(2,128)S(1)}, u32[]{:S(2)}, u32[]{:S(2)}) async-start(f32[16,2,512]{2,1,0:T(2,128)} %get-tuple-element.55), calls=%async_computation | async-start | bytes 131072 | tf_op jit(solution)/shard_map/all_to_all | solution.py:501
  16.2 1.9 %collective-permute-start.4 = (bf16[256,768]{1,0:T(8,128)(2,1)}, bf16[256,768]{1,0:T(8,128)(2,1)S(1)}, u32[]{:S(2)}, u32[]{:S(2)}) collective-permute-start(bf16[256,768]{1,0:T(8,128)(2,1)} %get-tuple-element.58), channel_id=1, source_target_pairs={{0,8},{2,10},{4,12},{6,14},{8,0},{10,2},{12,4},{14,6},{16,24},{18,... | collective-permute-start | bytes 1179656 | tf_op jit(solution)/shard_map/ppermute | solution.py:414
  18.5 0.7 fusion.6
  19.7 0.8 fusion.pick_ref
  20.6 0.7 add_select_fusion
  21.4 2.6 %all-to-all-done.ends_ref = f32[16,2,512]{2,1,0:T(2,128)S(1)} async-done(((f32[16,2,512]{2,1,0:T(2,128)}), f32[16,2,512]{2,1,0:T(2,128)S(1)}, u32[]{:S(2)}, u32[]{:S(2)}) %all-to-all-start) | async-done | bytes 65568 | tf_op jit(solution)/shard_map/all_to_all | solution.py:501
  24.0 0.6 copy-done.24
  24.6 2.7 %shard_map.146 = (bf16[256,512]{1,0:T(8,128)(2,1)}, f32[256,512]{1,0:T(8,128)}) custom-call(f32[256,512]{1,0:T(8,128)} %get-tuple-element.53.local_ref, f32[256,512]{1,0:T(8,128)} %get-tuple-element.54.through_ref, bf16[512,1024]{1,0:T(8,128)(2,1)} %mixer_ref.3, f32[16,2,512]{2,1,0:T(2,128)} %copy-done.24), custom_call_target="tpu_custom_call" | custom-call | flops 1 | bytes 1 | tf_op jit(solution)/shard_map/pallas_call | solution.py:506
  27.5 0.8 collective-permute-start.5
  28.3 0.7 fusion.2.pick_ref
  29.0 0.6 constant_dynamic-slice_fusion
  29.6 0.6 broadcast_select_fusion.bias_ref
  30.2 6.1 %collective-permute-done.5.refs_3_ = bf16[64,2048]{1,0:T(8,128)(2,1)S(1)} collective-permute-done((bf16[64,2048]{1,0:T(8,128)(2,1)S(1)}, bf16[64,2048]{1,0:T(8,128)(2,1)S(1)}, u32[]{:S(2)}, u32[]{:S(2)}) %collective-permute-start.5) | collective-permute-done | bytes 262176 | tf_op jit(solution)/shard_map/ppermute | solution.py:414
  36.3 0.8 copy-done.6
  37.1 2.9 %shard_map.147 = (bf16[256,512]{1,0:T(8,128)(2,1)}, bf16[16,32,512]{2,1,0:T(8,128)(2,1)}) custom-call(bf16[256,512]{1,0:T(8,128)(2,1)} %get-tuple-element.62.states_ref, bf16[512,1024]{1,0:T(8,128)(2,1)} %mixer_ref.3, f32[256,512]{1,0:T(8,128)} %copy-done.6, bf16[256,1024]{1,0:T(8,128)(2,1)} %bytes_ref.1, bf16[128,256]{1,0:T(8,128)(2,1)} %fusion.2.pick_ref), custom_call_target="tpu_custom_call" | custom-call | flops 1 | bytes 1 | tf_op jit(solution)/shard_map/pallas_call | solution.py:526
  40.0 3.8 %all-to-all-start.1 = ((bf16[16,32,512]{2,1,0:T(8,128)(2,1)}), bf16[16,32,512]{2,1,0:T(8,128)(2,1)S(1)}, u32[]{:S(2)}, u32[]{:S(2)}) async-start(bf16[16,32,512]{2,1,0:T(8,128)(2,1)} %get-tuple-element.64.gate_ref), calls=%async_computation.1 | async-start | bytes 1048576 | tf_op jit(solution)/shard_map/all_to_all | solution.py:537
  43.8 2.9 %collective-permute-start.6 = (bf16[256,768]{1,0:T(8,128)(2,1)S(1)}, bf16[256,768]{1,0:T(8,128)(2,1)S(1)}, u32[]{:S(2)}, u32[]{:S(2)}) collective-permute-start(bf16[256,768]{1,0:T(8,128)(2,1)S(1)} %copy-done.32), channel_id=1, source_target_pairs={{0,16},{2,18},{4,20},{6,22},{8,24},{10,26},{12,28},{14,30},{16,0},... | collective-permute-start | bytes 1179656 | tf_op jit(solution)/shard_map/ppermute | solution.py:414
  46.7 1.5 collective-permute-start.7
  48.1 2.3 %shard_map.148 = (bf16[4,64,512]{2,1,0:T(8,128)(2,1)}, bf16[4,64,512]{2,1,0:T(8,128)(2,1)}, bf16[4,64,512]{2,1,0:T(8,128)(2,1)}, bf16[4,64,512]{2,1,0:T(8,128)(2,1)}) custom-call(bf16[16,32,512]{2,1,0:T(8,128)(2,1)} %get-tuple-element.64.gate_ref, bf16[64,2048]{1,0:T(8,128)(2,1)} %refs_0_.3, bf16[64,2048]{1,0:T(8,128)(2,1)} %copy-done.26, ...), custom_call_target="tpu_custom_call" | custom-call | flops 1 | bytes 1 | tf_op jit(solution)/shard_map/pallas_call | solution.py:538
  50.4 2.4 %collective-permute-start.10 = (bf16[4,64,512]{2,1,0:T(8,128)(2,1)}, bf16[4,64,512]{2,1,0:T(8,128)(2,1)S(1)}, u32[]{:S(2)}, u32[]{:S(2)}) collective-permute-start(bf16[4,64,512]{2,1,0:T(8,128)(2,1)} %get-tuple-element.75), channel_id=1, source_target_pairs={{0,6},{2,4},{4,2},{6,0},{8,14},{10,12},{12,10},{14,8},{16,22},{18,... | collective-permute-start | bytes 786440 | tf_op jit(solution)/shard_map/ppermute | solution.py:414
  52.9 0.6 collective-permute-start.8
  53.4 0.6 collective-permute-start.9
  54.0 30.4 %collective-permute-done.6.refs_18_ = bf16[256,768]{1,0:T(8,128)(2,1)S(1)} collective-permute-done((bf16[256,768]{1,0:T(8,128)(2,1)S(1)}, bf16[256,768]{1,0:T(8,128)(2,1)S(1)}, u32[]{:S(2)}, u32[]{:S(2)}) %collective-permute-start.6) | collective-permute-done | bytes 393248 | tf_op jit(solution)/shard_map/ppermute | solution.py:414
  84.6 0.5 collective-permute-start.12
  85.1 0.4 collective-permute-start.14
  85.6 2.1 %shard_map.149.refs_0_ = bf16[256,512]{1,0:T(8,128)(2,1)} custom-call(bf16[256,512]{1,0:T(8,128)(2,1)} %fusion.pick_ref, bf16[16,32,512]{2,1,0:T(8,128)(2,1)} %copy-done.5), custom_call_target="tpu_custom_call" | custom-call | flops 1 | bytes 1 | tf_op jit(solution)/shard_map/pallas_call | solution.py:553
  87.8 1.5 collective-permute-start.15
  89.3 1.5 collective-permute-start.16
  90.8 0.5 collective-permute-start.17
  91.3 5.9 %collective-permute-done.15.refs_1_ = bf16[256,512]{1,0:T(8,128)(2,1)S(1)} collective-permute-done((bf16[256,512]{1,0:T(8,128)(2,1)}, bf16[256,512]{1,0:T(8,128)(2,1)S(1)}, u32[]{:S(2)}, u32[]{:S(2)}) %collective-permute-start.15) | collective-permute-done | bytes 262176 | tf_op jit(solution)/shard_map/ppermute | solution.py:414
  97.2 5.9 %collective-permute-done.16.refs_2_ = bf16[256,512]{1,0:T(8,128)(2,1)S(1)} collective-permute-done((bf16[256,512]{1,0:T(8,128)(2,1)}, bf16[256,512]{1,0:T(8,128)(2,1)S(1)}, u32[]{:S(2)}, u32[]{:S(2)}) %collective-permute-start.16) | collective-permute-done | bytes 262176 | tf_op jit(solution)/shard_map/ppermute | solution.py:414
  103.2 0.5 collective-permute-start.21
  103.7 1.0 collective-permute-done.20.refs_6_
  105.4 0.7 copy-done.23
  106.1 10.2 %shard_map.150 = (bf16[1024,128]{1,0:T(8,128)(2,1)}, bf16[1024,128]{1,0:T(8,128)(2,1)}, bf16[1024,128]{1,0:T(8,128)(2,1)}, bf16[1024,128]{1,0:T(8,128)(2,1)}, bf...) custom-call(f32[1,1024]{1,0:T(1,128)} %broadcast_select_fusion.bias_ref,, ...), custom_call_target="tpu_custom_call" | custom-call | flops 1 | bytes 1 | tf_op jit(solution)/shard_map/pallas_call | solution.py:571
  116.3 0.7 collective-permute-start.22
  117.0 1.4 collective-permute-start.25
  118.4 1.5 collective-permute-start.26
  119.9 0.6 collective-permute-start.27
  120.5 1.4 collective-permute-start.23
  121.9 6.7 %collective-permute-done.25.refs_5_.refs_1_ = bf16[528,128]{1,0:T(8,128)(2,1)S(1)} collective-permute-done((bf16[528,128]{1,0:T(8,128)(2,1)}, bf16[528,128]{1,0:T(8,128)(2,1)S(1)}, u32[]{:S(2)}, u32[]{:S(2)}) %collective-permute-start.25) | collective-permute-done | bytes 135200 | tf_op jit(solution)/shard_map/ppermute | solution.py:414
  128.6 1.5 collective-permute-start.24
  130.1 2.5 %collective-permute-done.27.refs_7_.refs_3_ = bf16[528,128]{1,0:T(8,128)(2,1)S(1)} collective-permute-done((bf16[528,128]{1,0:T(8,128)(2,1)}, bf16[528,128]{1,0:T(8,128)(2,1)S(1)}, u32[]{:S(2)}, u32[]{:S(2)}) %collective-permute-start.27) | collective-permute-done | bytes 135200 | tf_op jit(solution)/shard_map/ppermute | solution.py:414
  132.5 0.9 copy-done.1
  133.4 0.4 shard_map.152.refs_0_
  133.8 0.5 collective-permute-start.28
  134.4 3.0 %collective-permute-start.30 = (bf16[512,128]{1,0:T(8,128)(2,1)S(1)}, bf16[512,128]{1,0:T(8,128)(2,1)S(1)}, u32[]{:S(2)}, u32[]{:S(2)}) collective-permute-start(bf16[512,128]{1,0:T(8,128)(2,1)S(1)} %shard_map.152.refs_0_), channel_id=1, source_target_pairs={{0,6},{2,4},{4,2},{6,0},{8,14},{10,12},{12,10},{14,8},{16,22},{18,... | collective-permute-start | bytes 393224 | tf_op jit(solution)/shard_map/ppermute | solution.py:414
  137.4 1.5 collective-permute-done.23.refs_2_
  139.0 0.9 copy-done.2
  139.9 0.9 copy-done.4
  140.9 0.4 shard_map.151.query_ref
  141.3 2.1 %collective-permute-done.29.refs_2_ = bf16[512,128]{1,0:T(8,128)(2,1)S(1)} collective-permute-done((bf16[512,128]{1,0:T(8,128)(2,1)S(1)}, bf16[512,128]{1,0:T(8,128)(2,1)S(1)}, u32[]{:S(2)}, u32[]{:S(2)}) %collective-permute-start.29) | collective-permute-done | bytes 131104 | tf_op jit(solution)/shard_map/ppermute | solution.py:414
  143.4 3.7 %shard_map.153 = bf16[16,144,128]{2,1,0:T(8,128)(2,1)} custom-call(s32[16]{0:T(128)S(1)} %and_select_fusion.1.place_ref, bf16[1024,128]{1,0:T(8,128)(2,1)S(1)} %shard_map.151.query_ref, bf16[512,128]{1,0:T(8,128)(2,1)S(1)} %shard_map.152.refs_0_, bf16[512,128]{1,0:T(8,128)(2,1)S(1)} %collective-permute-done.28.refs_1_, ...), custom_call_target="tpu_custom_call" | custom-call | flops 1 | bytes 1 | tf_op jit(solution)/shard_map/pallas_call | solution.py:611
  147.1 10.2 %all-to-all-start.2 = ((bf16[16,144,128]{2,1,0:T(8,128)(2,1)}), bf16[16,144,128]{2,1,0:T(8,128)(2,1)S(1)}, u32[]{:S(2)}, u32[]{:S(2)}) async-start(bf16[16,144,128]{2,1,0:T(8,128)(2,1)} %shard_map.153), calls=%async_computation.2 | async-start | bytes 1179648 | tf_op jit(solution)/shard_map/all_to_all | solution.py:625
  159.3 0.6 iota_compare_fusion.6
  160.1 12.7 %all-to-all-done.2.pieces_ref = bf16[16,144,128]{2,1,0:T(8,128)(2,1)S(1)} async-done(((bf16[16,144,128]{2,1,0:T(8,128)(2,1)}), bf16[16,144,128]{2,1,0:T(8,128)(2,1)S(1)}, u32[]{:S(2)}, u32[]{:S(2)}) %all-to-all-start.2) | async-done | bytes 589856 | tf_op jit(solution)/shard_map/all_to_all | solution.py:625
  172.8 2.2 %copy-done = bf16[2048,1024]{1,0:T(8,128)(2,1)S(1)} copy-done((bf16[2048,1024]{1,0:T(8,128)(2,1)S(1)}, bf16[2048,1024]{1,0:T(8,128)(2,1)}, u32[]{:S(2)}) %copy-start) | copy-done | bytes 4194328
  175.0 0.8 shard_map.154
  176.0 1.4 collective-permute-done.31.other_ref
  177.5 0.9 shard_map.155
  (116 shorter events, 2.6 us)
Async XLA Ops:
  0.0 18.2 %copy-start.29 = (s32[16]{0:T(128)S(1)}, s32[16]{0:T(128)}, u32[]{:S(2)}) copy-start(s32[16]{0:T(128)} %param.22) | copy-start | bytes 196
  0.0 21.4 %copy-start.30 = (s32[1,128]{1,0:T(1,128)S(1)}, s32[1,128]{1,0:T(1,128)}, u32[]{:S(2)}) copy-start(s32[1,128]{1,0:T(1,128)} %param.21) | copy-start | bytes 1540
  0.0 29.0 %copy-start.28 = (f32[4096]{0:T(1024)S(1)}, f32[4096]{0:T(1024)}, u32[]{:S(2)}) copy-start(f32[4096]{0:T(1024)} %param.25) | copy-start | bytes 49156
  0.0 24.0 %collective-permute-start.1 = (bf16[64,2048]{1,0:T(8,128)(2,1)}, bf16[64,2048]{1,0:T(8,128)(2,1)S(1)}, u32[]{:S(2)}, u32[]{:S(2)}) collective-permute-start(bf16[64,2048]{1,0:T(8,128)(2,1)} %refs_0_.3), channel_id=1, source_target_pairs={{0,16},{2,18},{4,20},{6,22},{8,24},{10,26},{12,28},{14,30},{16,0},... | collective-permute-start | bytes 786440 | tf_op jit(solution)/shard_map/ppermute | solution.py:414
  4.1 19.9 %collective-permute-start = (bf16[64,2048]{1,0:T(8,128)(2,1)}, bf16[64,2048]{1,0:T(8,128)(2,1)S(1)}, u32[]{:S(2)}, u32[]{:S(2)}) collective-permute-start(bf16[64,2048]{1,0:T(8,128)(2,1)} %refs_0_.3), channel_id=1, source_target_pairs={{0,8},{2,10},{4,12},{6,14},{8,0},{10,2},{12,4},{14,6},{16,24},{18,... | collective-permute-start | bytes 786440 | tf_op jit(solution)/shard_map/ppermute | solution.py:414
  6.4 23.2 %collective-permute-start.3 = (f32[1,512]{1,0:T(1,128)S(1)}, f32[1,512]{1,0:T(1,128)S(1)}, u32[]{:S(2)}, u32[]{:S(2)}) collective-permute-start(f32[1,512]{1,0:T(1,128)S(1)} %bitcast.9), channel_id=1, source_target_pairs={{0,1},{1,0},{2,3},{3,2},{4,5},{5,4},{6,7},{7,6},{8,9},{9,8},{10,11... | collective-permute-start | bytes 6152 | tf_op jit(solution)/shard_map/ppermute | solution.py:23
  12.2 31.5 %copy-start.32 = (bf16[256,768]{1,0:T(8,128)(2,1)S(1)}, bf16[256,768]{1,0:T(8,128)(2,1)}, u32[]{:S(2)}) copy-start(bf16[256,768]{1,0:T(8,128)(2,1)} %get-tuple-element.67) | copy-start | bytes 1179652
  12.2 34.4 %copy-start.31 = (bf16[256,768]{1,0:T(8,128)(2,1)S(1)}, bf16[256,768]{1,0:T(8,128)(2,1)}, u32[]{:S(2)}) copy-start(bf16[256,768]{1,0:T(8,128)(2,1)} %get-tuple-element.68) | copy-start | bytes 1179652
  12.3 11.7 %all-to-all-start = ((f32[16,2,512]{2,1,0:T(2,128)}), f32[16,2,512]{2,1,0:T(2,128)S(1)}, u32[]{:S(2)}, u32[]{:S(2)}) async-start(f32[16,2,512]{2,1,0:T(2,128)} %get-tuple-element.55), calls=%async_computation | async-start | bytes 131072 | tf_op jit(solution)/shard_map/all_to_all | solution.py:501
  16.2 14.0 %collective-permute-start.4 = (bf16[256,768]{1,0:T(8,128)(2,1)}, bf16[256,768]{1,0:T(8,128)(2,1)S(1)}, u32[]{:S(2)}, u32[]{:S(2)}) collective-permute-start(bf16[256,768]{1,0:T(8,128)(2,1)} %get-tuple-element.58), channel_id=1, source_target_pairs={{0,8},{2,10},{4,12},{6,14},{8,0},{10,2},{12,4},{14,6},{16,24},{18,... | collective-permute-start | bytes 1179656 | tf_op jit(solution)/shard_map/ppermute | solution.py:414
  24.0 24.1 %copy-start.25 = (bf16[64,2048]{1,0:T(8,128)(2,1)}, bf16[64,2048]{1,0:T(8,128)(2,1)S(1)}, u32[]{:S(2)}) copy-start(bf16[64,2048]{1,0:T(8,128)(2,1)S(1)} %collective-permute-done.1.refs_2_) | copy-start | bytes 786436
  24.0 24.1 %copy-start.26 = (bf16[64,2048]{1,0:T(8,128)(2,1)}, bf16[64,2048]{1,0:T(8,128)(2,1)S(1)}, u32[]{:S(2)}) copy-start(bf16[64,2048]{1,0:T(8,128)(2,1)S(1)} %collective-permute-done.refs_1_) | copy-start | bytes 786436
  27.3 9.0 %collective-permute-start.2 = (f32[256,512]{1,0:T(8,128)}, f32[256,512]{1,0:T(8,128)S(1)}, u32[]{:S(2)}, u32[]{:S(2)}) collective-permute-start(f32[256,512]{1,0:T(8,128)} %get-tuple-element.57), channel_id=1, source_target_pairs={{0,1},{1,0},{2,3},{3,2},{4,5},{5,4},{6,7},{7,6},{8,9},{9,8},{10,11... | collective-permute-start | bytes 1572872 | tf_op jit(solution)/shard_map/ppermute | solution.py:23
  27.5 8.8 %collective-permute-start.5 = (bf16[64,2048]{1,0:T(8,128)(2,1)S(1)}, bf16[64,2048]{1,0:T(8,128)(2,1)S(1)}, u32[]{:S(2)}, u32[]{:S(2)}) collective-permute-start(bf16[64,2048]{1,0:T(8,128)(2,1)S(1)} %collective-permute-done.1.refs_2_), channel_id=1, source_target_pairs={{0,8},{2,10},{4,12},{6,14},{8,0},{10,2},{12,4},{14,6},{16,24},{18,... | collective-permute-start | bytes 786440 | tf_op jit(solution)/shard_map/ppermute | solution.py:414
  30.2 74.9 %copy-start.7 = (bf16[256,768]{1,0:T(8,128)(2,1)}, bf16[256,768]{1,0:T(8,128)(2,1)S(1)}, u32[]{:S(2)}) copy-start(bf16[256,768]{1,0:T(8,128)(2,1)S(1)} %collective-permute-done.4.refs_17_) | copy-start | bytes 1179652
  36.3 11.9 %copy-start.27 = (bf16[64,2048]{1,0:T(8,128)(2,1)}, bf16[64,2048]{1,0:T(8,128)(2,1)S(1)}, u32[]{:S(2)}) copy-start(bf16[64,2048]{1,0:T(8,128)(2,1)S(1)} %collective-permute-done.5.refs_3_) | copy-start | bytes 786436
  40.0 44.5 %all-to-all-start.1 = ((bf16[16,32,512]{2,1,0:T(8,128)(2,1)}), bf16[16,32,512]{2,1,0:T(8,128)(2,1)S(1)}, u32[]{:S(2)}, u32[]{:S(2)}) async-start(bf16[16,32,512]{2,1,0:T(8,128)(2,1)} %get-tuple-element.64.gate_ref), calls=%async_computation.1 | async-start | bytes 1048576 | tf_op jit(solution)/shard_map/all_to_all | solution.py:537
  43.8 40.6 %collective-permute-start.6 = (bf16[256,768]{1,0:T(8,128)(2,1)S(1)}, bf16[256,768]{1,0:T(8,128)(2,1)S(1)}, u32[]{:S(2)}, u32[]{:S(2)}) collective-permute-start(bf16[256,768]{1,0:T(8,128)(2,1)S(1)} %copy-done.32), channel_id=1, source_target_pairs={{0,16},{2,18},{4,20},{6,22},{8,24},{10,26},{12,28},{14,30},{16,0},... | collective-permute-start | bytes 1179656 | tf_op jit(solution)/shard_map/ppermute | solution.py:414
  46.7 37.7 %collective-permute-start.7 = (bf16[256,768]{1,0:T(8,128)(2,1)S(1)}, bf16[256,768]{1,0:T(8,128)(2,1)S(1)}, u32[]{:S(2)}, u32[]{:S(2)}) collective-permute-start(bf16[256,768]{1,0:T(8,128)(2,1)S(1)} %copy-done.31), channel_id=1, source_target_pairs={{0,24},{2,26},{4,28},{6,30},{8,16},{10,18},{12,20},{14,22},{16,8},... | collective-permute-start | bytes 1179656 | tf_op jit(solution)/shard_map/ppermute | solution.py:414
  50.4 34.0 %collective-permute-start.10 = (bf16[4,64,512]{2,1,0:T(8,128)(2,1)}, bf16[4,64,512]{2,1,0:T(8,128)(2,1)S(1)}, u32[]{:S(2)}, u32[]{:S(2)}) collective-permute-start(bf16[4,64,512]{2,1,0:T(8,128)(2,1)} %get-tuple-element.75), channel_id=1, source_target_pairs={{0,6},{2,4},{4,2},{6,0},{8,14},{10,12},{12,10},{14,8},{16,22},{18,... | collective-permute-start | bytes 786440 | tf_op jit(solution)/shard_map/ppermute | solution.py:414
  52.9 31.6 %collective-permute-start.8 = (bf16[4,64,512]{2,1,0:T(8,128)(2,1)}, bf16[4,64,512]{2,1,0:T(8,128)(2,1)S(1)}, u32[]{:S(2)}, u32[]{:S(2)}) collective-permute-start(bf16[4,64,512]{2,1,0:T(8,128)(2,1)} %get-tuple-element.73), channel_id=1, source_target_pairs={{0,2},{2,0},{4,6},{6,4},{8,10},{10,8},{12,14},{14,12},{16,18},{18,... | collective-permute-start | bytes 786440 | tf_op jit(solution)/shard_map/ppermute | solution.py:414
  53.4 31.0 %collective-permute-start.9 = (bf16[4,64,512]{2,1,0:T(8,128)(2,1)}, bf16[4,64,512]{2,1,0:T(8,128)(2,1)S(1)}, u32[]{:S(2)}, u32[]{:S(2)}) collective-permute-start(bf16[4,64,512]{2,1,0:T(8,128)(2,1)} %get-tuple-element.74), channel_id=1, source_target_pairs={{0,4},{2,6},{4,0},{6,2},{8,12},{10,14},{12,8},{14,10},{16,20},{18,... | collective-permute-start | bytes 786440 | tf_op jit(solution)/shard_map/ppermute | solution.py:414
  84.4 20.7 %copy-start.8 = (bf16[256,768]{1,0:T(8,128)(2,1)}, bf16[256,768]{1,0:T(8,128)(2,1)S(1)}, u32[]{:S(2)}) copy-start(bf16[256,768]{1,0:T(8,128)(2,1)S(1)} %collective-permute-done.6.refs_18_) | copy-start | bytes 1179652
  84.4 20.7 %copy-start.9 = (bf16[256,768]{1,0:T(8,128)(2,1)}, bf16[256,768]{1,0:T(8,128)(2,1)S(1)}, u32[]{:S(2)}) copy-start(bf16[256,768]{1,0:T(8,128)(2,1)S(1)} %collective-permute-done.7.refs_19_) | copy-start | bytes 1179652
  84.4 20.7 %copy-start.10 = (bf16[4,64,512]{2,1,0:T(8,128)(2,1)}, bf16[4,64,512]{2,1,0:T(8,128)(2,1)S(1)}, u32[]{:S(2)}) copy-start(bf16[4,64,512]{2,1,0:T(8,128)(2,1)S(1)} %collective-permute-done.10.refs_11_) | copy-start | bytes 786436
  84.4 20.6 %copy-start.11 = (bf16[4,64,512]{2,1,0:T(8,128)(2,1)}, bf16[4,64,512]{2,1,0:T(8,128)(2,1)S(1)}, u32[]{:S(2)}) copy-start(bf16[4,64,512]{2,1,0:T(8,128)(2,1)S(1)} %collective-permute-done.8.refs_9_) | copy-start | bytes 786436
  84.4 20.6 %copy-start.12 = (bf16[4,64,512]{2,1,0:T(8,128)(2,1)}, bf16[4,64,512]{2,1,0:T(8,128)(2,1)S(1)}, u32[]{:S(2)}) copy-start(bf16[4,64,512]{2,1,0:T(8,128)(2,1)S(1)} %collective-permute-done.9.refs_10_) | copy-start | bytes 786436
  84.5 1.1 copy-start.5
  84.5 3.2 %collective-permute-start.11 = (bf16[4,64,512]{2,1,0:T(8,128)(2,1)}, bf16[4,64,512]{2,1,0:T(8,128)(2,1)S(1)}, u32[]{:S(2)}, u32[]{:S(2)}) collective-permute-start(bf16[4,64,512]{2,1,0:T(8,128)(2,1)} %get-tuple-element.77.refs_8_), channel_id=1, source_target_pairs={{0,1},{1,0},{2,3},{3,2},{4,5},{5,4},{6,7},{7,6},{8,9},{9,8},{10,11... | collective-permute-start | bytes 786440 | tf_op jit(solution)/shard_map/ppermute | solution.py:23
  84.6 3.1 %collective-permute-start.12 = (bf16[4,64,512]{2,1,0:T(8,128)(2,1)S(1)}, bf16[4,64,512]{2,1,0:T(8,128)(2,1)S(1)}, u32[]{:S(2)}, u32[]{:S(2)}) collective-permute-start(bf16[4,64,512]{2,1,0:T(8,128)(2,1)S(1)} %collective-permute-done.8.refs_9_), channel_id=1, source_target_pairs={{0,1},{1,0},{2,3},{3,2},{4,5},{5,4},{6,7},{7,6},{8,9},{9,8},{10,11... | collective-permute-start | bytes 786440 | tf_op jit(solution)/shard_map/ppermute | solution.py:23
  85.1 2.7 %collective-permute-start.13 = (bf16[4,64,512]{2,1,0:T(8,128)(2,1)S(1)}, bf16[4,64,512]{2,1,0:T(8,128)(2,1)S(1)}, u32[]{:S(2)}, u32[]{:S(2)}) collective-permute-start(bf16[4,64,512]{2,1,0:T(8,128)(2,1)S(1)} %collective-permute-done.9.refs_10_), channel_id=1, source_target_pairs={{0,1},{1,0},{2,3},{3,2},{4,5},{5,4},{6,7},{7,6},{8,9},{9,8},{10,11... | collective-permute-start | bytes 786440 | tf_op jit(solution)/shard_map/ppermute | solution.py:23
  85.1 2.6 %collective-permute-start.14 = (bf16[4,64,512]{2,1,0:T(8,128)(2,1)S(1)}, bf16[4,64,512]{2,1,0:T(8,128)(2,1)S(1)}, u32[]{:S(2)}, u32[]{:S(2)}) collective-permute-start(bf16[4,64,512]{2,1,0:T(8,128)(2,1)S(1)} %collective-permute-done.10.refs_11_), channel_id=1, source_target_pairs={{0,1},{1,0},{2,3},{3,2},{4,5},{5,4},{6,7},{7,6},{8,9},{9,8},{10,11... | collective-permute-start | bytes 786440 | tf_op jit(solution)/shard_map/ppermute | solution.py:23
  87.7 17.4 %copy-start.13 = (bf16[4,64,512]{2,1,0:T(8,128)(2,1)}, bf16[4,64,512]{2,1,0:T(8,128)(2,1)S(1)}, u32[]{:S(2)}) copy-start(bf16[4,64,512]{2,1,0:T(8,128)(2,1)S(1)} %collective-permute-done.11.refs_12_) | copy-start | bytes 786436
  87.7 17.4 %copy-start.14 = (bf16[4,64,512]{2,1,0:T(8,128)(2,1)}, bf16[4,64,512]{2,1,0:T(8,128)(2,1)S(1)}, u32[]{:S(2)}) copy-start(bf16[4,64,512]{2,1,0:T(8,128)(2,1)S(1)} %collective-permute-done.12.refs_13_) | copy-start | bytes 786436
  87.7 17.4 %copy-start.15 = (bf16[4,64,512]{2,1,0:T(8,128)(2,1)}, bf16[4,64,512]{2,1,0:T(8,128)(2,1)S(1)}, u32[]{:S(2)}) copy-start(bf16[4,64,512]{2,1,0:T(8,128)(2,1)S(1)} %collective-permute-done.13.refs_14_) | copy-start | bytes 786436
  87.8 17.4 %copy-start.16 = (bf16[4,64,512]{2,1,0:T(8,128)(2,1)}, bf16[4,64,512]{2,1,0:T(8,128)(2,1)S(1)}, u32[]{:S(2)}) copy-start(bf16[4,64,512]{2,1,0:T(8,128)(2,1)S(1)} %collective-permute-done.14.refs_15_) | copy-start | bytes 786436
  87.8 9.4 %collective-permute-start.15 = (bf16[256,512]{1,0:T(8,128)(2,1)}, bf16[256,512]{1,0:T(8,128)(2,1)S(1)}, u32[]{:S(2)}, u32[]{:S(2)}) collective-permute-start(bf16[256,512]{1,0:T(8,128)(2,1)} %shard_map.149.refs_0_), channel_id=1, source_target_pairs={{0,2},{2,0},{4,6},{6,4},{8,10},{10,8},{12,14},{14,12},{16,18},{18,... | collective-permute-start | bytes 786440 | tf_op jit(solution)/shard_map/ppermute | solution.py:414
  89.3 13.8 %collective-permute-start.16 = (bf16[256,512]{1,0:T(8,128)(2,1)}, bf16[256,512]{1,0:T(8,128)(2,1)S(1)}, u32[]{:S(2)}, u32[]{:S(2)}) collective-permute-start(bf16[256,512]{1,0:T(8,128)(2,1)} %shard_map.149.refs_0_), channel_id=1, source_target_pairs={{0,4},{2,6},{4,0},{6,2},{8,12},{10,14},{12,8},{14,10},{16,20},{18,... | collective-permute-start | bytes 786440 | tf_op jit(solution)/shard_map/ppermute | solution.py:414
  90.8 12.4 %collective-permute-start.17 = (bf16[256,512]{1,0:T(8,128)(2,1)}, bf16[256,512]{1,0:T(8,128)(2,1)S(1)}, u32[]{:S(2)}, u32[]{:S(2)}) collective-permute-start(bf16[256,512]{1,0:T(8,128)(2,1)} %shard_map.149.refs_0_), channel_id=1, source_target_pairs={{0,6},{2,4},{4,2},{6,0},{8,14},{10,12},{12,10},{14,8},{16,22},{18,... | collective-permute-start | bytes 786440 | tf_op jit(solution)/shard_map/ppermute | solution.py:414
  91.3 12.3 %collective-permute-start.18 = (bf16[256,512]{1,0:T(8,128)(2,1)}, bf16[256,512]{1,0:T(8,128)(2,1)S(1)}, u32[]{:S(2)}, u32[]{:S(2)}) collective-permute-start(bf16[256,512]{1,0:T(8,128)(2,1)} %shard_map.149.refs_0_), channel_id=1, source_target_pairs={{0,1},{1,0},{2,3},{3,2},{4,5},{5,4},{6,7},{7,6},{8,9},{9,8},{10,11... | collective-permute-start | bytes 786440 | tf_op jit(solution)/shard_map/ppermute | solution.py:23
  97.2 7.9 %copy-start.17 = (bf16[256,512]{1,0:T(8,128)(2,1)}, bf16[256,512]{1,0:T(8,128)(2,1)S(1)}, u32[]{:S(2)}) copy-start(bf16[256,512]{1,0:T(8,128)(2,1)S(1)} %collective-permute-done.15.refs_1_) | copy-start | bytes 786436
  97.2 6.5 %collective-permute-start.19 = (bf16[256,512]{1,0:T(8,128)(2,1)S(1)}, bf16[256,512]{1,0:T(8,128)(2,1)S(1)}, u32[]{:S(2)}, u32[]{:S(2)}) collective-permute-start(bf16[256,512]{1,0:T(8,128)(2,1)S(1)} %collective-permute-done.15.refs_1_), channel_id=1, source_target_pairs={{0,1},{1,0},{2,3},{3,2},{4,5},{5,4},{6,7},{7,6},{8,9},{9,8},{10,11... | collective-permute-start | bytes 786440 | tf_op jit(solution)/shard_map/ppermute | solution.py:23
  103.1 2.0 %copy-start.18 = (bf16[256,512]{1,0:T(8,128)(2,1)}, bf16[256,512]{1,0:T(8,128)(2,1)S(1)}, u32[]{:S(2)}) copy-start(bf16[256,512]{1,0:T(8,128)(2,1)S(1)} %collective-permute-done.16.refs_2_) | copy-start | bytes 786436
  103.1 1.5 collective-permute-start.20
  103.1 2.0 %copy-start.19 = (bf16[256,512]{1,0:T(8,128)(2,1)}, bf16[256,512]{1,0:T(8,128)(2,1)S(1)}, u32[]{:S(2)}) copy-start(bf16[256,512]{1,0:T(8,128)(2,1)S(1)} %collective-permute-done.17.refs_3_) | copy-start | bytes 786436
  103.2 1.9 %collective-permute-start.21 = (bf16[256,512]{1,0:T(8,128)(2,1)S(1)}, bf16[256,512]{1,0:T(8,128)(2,1)S(1)}, u32[]{:S(2)}, u32[]{:S(2)}) collective-permute-start(bf16[256,512]{1,0:T(8,128)(2,1)S(1)} %collective-permute-done.17.refs_3_), channel_id=1, source_target_pairs={{0,1},{1,0},{2,3},{3,2},{4,5},{5,4},{6,7},{7,6},{8,9},{9,8},{10,11... | collective-permute-start | bytes 786440 | tf_op jit(solution)/shard_map/ppermute | solution.py:23
  103.7 1.5 copy-start.20
  103.7 1.5 copy-start.21
  116.3 18.1 %collective-permute-start.22 = (bf16[1024,128]{1,0:T(8,128)(2,1)}, bf16[1024,128]{1,0:T(8,128)(2,1)S(1)}, u32[]{:S(2)}, u32[]{:S(2)}) collective-permute-start(bf16[1024,128]{1,0:T(8,128)(2,1)} %get-tuple-element.91), channel_id=1, source_target_pairs={{0,2},{2,0},{4,6},{6,4},{8,10},{10,8},{12,14},{14,12},{16,18},{18,... | collective-permute-start | bytes 786440 | tf_op jit(solution)/shard_map/ppermute | solution.py:414
  117.0 11.6 %collective-permute-start.25 = (bf16[528,128]{1,0:T(8,128)(2,1)}, bf16[528,128]{1,0:T(8,128)(2,1)S(1)}, u32[]{:S(2)}, u32[]{:S(2)}) collective-permute-start(bf16[528,128]{1,0:T(8,128)(2,1)} %get-tuple-element.95), channel_id=1, source_target_pairs={{0,2},{2,0},{4,6},{6,4},{8,10},{10,8},{12,14},{14,12},{16,18},{18,... | collective-permute-start | bytes 405512 | tf_op jit(solution)/shard_map/ppermute | solution.py:414
  118.4 11.7 %collective-permute-start.26 = (bf16[528,128]{1,0:T(8,128)(2,1)}, bf16[528,128]{1,0:T(8,128)(2,1)S(1)}, u32[]{:S(2)}, u32[]{:S(2)}) collective-permute-start(bf16[528,128]{1,0:T(8,128)(2,1)} %get-tuple-element.96), channel_id=1, source_target_pairs={{0,4},{2,6},{4,0},{6,2},{8,12},{10,14},{12,8},{14,10},{16,20},{18,... | collective-permute-start | bytes 405512 | tf_op jit(solution)/shard_map/ppermute | solution.py:414
  119.9 12.7 %collective-permute-start.27 = (bf16[528,128]{1,0:T(8,128)(2,1)}, bf16[528,128]{1,0:T(8,128)(2,1)S(1)}, u32[]{:S(2)}, u32[]{:S(2)}) collective-permute-start(bf16[528,128]{1,0:T(8,128)(2,1)} %get-tuple-element.97), channel_id=1, source_target_pairs={{0,6},{2,4},{4,2},{6,0},{8,14},{10,12},{12,10},{14,8},{16,22},{18,... | collective-permute-start | bytes 405512 | tf_op jit(solution)/shard_map/ppermute | solution.py:414
  120.5 18.4 %collective-permute-start.23 = (bf16[1024,128]{1,0:T(8,128)(2,1)}, bf16[1024,128]{1,0:T(8,128)(2,1)S(1)}, u32[]{:S(2)}, u32[]{:S(2)}) collective-permute-start(bf16[1024,128]{1,0:T(8,128)(2,1)} %get-tuple-element.92), channel_id=1, source_target_pairs={{0,4},{2,6},{4,0},{6,2},{8,12},{10,14},{12,8},{14,10},{16,20},{18,... | collective-permute-start | bytes 786440 | tf_op jit(solution)/shard_map/ppermute | solution.py:414
  128.6 10.4 %collective-permute-start.24 = (bf16[1024,128]{1,0:T(8,128)(2,1)}, bf16[1024,128]{1,0:T(8,128)(2,1)S(1)}, u32[]{:S(2)}, u32[]{:S(2)}) collective-permute-start(bf16[1024,128]{1,0:T(8,128)(2,1)} %get-tuple-element.93), channel_id=1, source_target_pairs={{0,6},{2,4},{4,2},{6,0},{8,14},{10,12},{12,10},{14,8},{16,22},{18,... | collective-permute-start | bytes 786440 | tf_op jit(solution)/shard_map/ppermute | solution.py:414
  132.5 0.9 copy-start.1
  133.8 7.5 %collective-permute-start.28 = (bf16[512,128]{1,0:T(8,128)(2,1)S(1)}, bf16[512,128]{1,0:T(8,128)(2,1)S(1)}, u32[]{:S(2)}, u32[]{:S(2)}) collective-permute-start(bf16[512,128]{1,0:T(8,128)(2,1)S(1)} %shard_map.152.refs_0_), channel_id=1, source_target_pairs={{0,2},{2,0},{4,6},{6,4},{8,10},{10,8},{12,14},{14,12},{16,18},{18,... | collective-permute-start | bytes 393224 | tf_op jit(solution)/shard_map/ppermute | solution.py:414
  134.4 9.0 %collective-permute-start.29 = (bf16[512,128]{1,0:T(8,128)(2,1)S(1)}, bf16[512,128]{1,0:T(8,128)(2,1)S(1)}, u32[]{:S(2)}, u32[]{:S(2)}) collective-permute-start(bf16[512,128]{1,0:T(8,128)(2,1)S(1)} %shard_map.152.refs_0_), channel_id=1, source_target_pairs={{0,4},{2,6},{4,0},{6,2},{8,12},{10,14},{12,8},{14,10},{16,20},{18,... | collective-permute-start | bytes 393224 | tf_op jit(solution)/shard_map/ppermute | solution.py:414
  134.4 9.0 %collective-permute-start.30 = (bf16[512,128]{1,0:T(8,128)(2,1)S(1)}, bf16[512,128]{1,0:T(8,128)(2,1)S(1)}, u32[]{:S(2)}, u32[]{:S(2)}) collective-permute-start(bf16[512,128]{1,0:T(8,128)(2,1)S(1)} %shard_map.152.refs_0_), channel_id=1, source_target_pairs={{0,6},{2,4},{4,2},{6,0},{8,14},{10,12},{12,10},{14,8},{16,22},{18,... | collective-permute-start | bytes 393224 | tf_op jit(solution)/shard_map/ppermute | solution.py:414
  139.0 0.9 copy-start.2
  139.9 0.9 copy-start.4
  141.3 36.2 %copy-start.3 = (bf16[256,512]{1,0:T(8,128)(2,1)S(1)}, bf16[256,512]{1,0:T(8,128)(2,1)}, u32[]{:S(2)}) copy-start(bf16[256,512]{1,0:T(8,128)(2,1)} %get-tuple-element.100.encoded_ref) | copy-start | bytes 786436
  147.1 25.7 %all-to-all-start.2 = ((bf16[16,144,128]{2,1,0:T(8,128)(2,1)}), bf16[16,144,128]{2,1,0:T(8,128)(2,1)S(1)}, u32[]{:S(2)}, u32[]{:S(2)}) async-start(bf16[16,144,128]{2,1,0:T(8,128)(2,1)} %shard_map.153), calls=%async_computation.2 | async-start | bytes 1179648 | tf_op jit(solution)/shard_map/all_to_all | solution.py:625
  172.8 2.2 %copy-start = (bf16[2048,1024]{1,0:T(8,128)(2,1)S(1)}, bf16[2048,1024]{1,0:T(8,128)(2,1)}, u32[]{:S(2)}) copy-start(bf16[2048,1024]{1,0:T(8,128)(2,1)} %weight_ref.1) | copy-start | bytes 12582916
  175.8 1.6 collective-permute-start.31
  (4 other events, 2.9 us)
